TPU v7x, 128 devices: a whole 4x4x4 slice. The times are simulated.
128 devices in a mesh: loop: 8 (over x, core), tower: 16 (over z, y).
Axes of the slice: x: 4, y: 4, z: 4, core: 2. Of those that a mesh axis runs over, the one named last changes fastest.
Arguments:
- image_emb: float32 [2048, 1152], P('loop', 'tower'), may hold values from -304 to 304, as said below
- text_emb: float32 [2048, 1152], P('loop', 'tower'), may hold values from -304 to 304, as said below
- image_owner: int32 [2048], P('loop'), may hold values from 0 to 1023, as said below
- text_owner: int32 [2048], P('loop'), may hold values from 0 to 1023, as said below
- log_scale: float32 [1], replicated, may hold values from 3.9 to 4.7
- bias: float32 [1], replicated, may hold values from -6 to -3.5
Outputs:
- image_grad: float32 [2048, 1152], P('loop', 'tower')
- text_grad: float32 [2048, 1152], P('loop', 'tower')
Inputs may be any that keep to these rules, and one draw needn't show every extreme that they name: Image row i and text row j form a positive pair exactly when image_owner[i] equals text_owner[j]; a row may have several positives or none. `text_owner`: owner ids of text rows, compared with image_owner. `image_emb`: entries of any sign; rows are not normalized. `text_emb`: entries of any sign; rows are not normalized.
All inputs are finite; a program needn't handle non-finite values.
Results may differ from a plain program's by a relative error of at most 0.0003.
Values sent between devices are 32-bit elements; how exact they have to be, the bound alone decides.
No kernel may reach another device: no remote copies, remote signals or barrier semaphores. Data moves between devices by JAX's collectives and lax.ppermute only.
A program may use at most 128 MiB of HBM per device.

v0:
```python
import jax
import jax.numpy as jnp
from jax import lax
from jax.sharding import PartitionSpec as P

EPSILON = 1e-06


def from_behind(x, axis, by):
    size = lax.axis_size(axis)
    return lax.ppermute(x, axis, [(i, (i + by) % size) for i in range(size)])


def product_nt(first_mat, second_mat):
    return lax.dot_general(
        first_mat,
        second_mat,
        (((1,), (1,)), ((), ())),
        precision=lax.Precision.HIGHEST,
        preferred_element_type=jnp.float32,
    )


def product_tn(first_mat, second_mat):
    return lax.dot_general(
        first_mat,
        second_mat,
        (((0,), (0,)), ((), ())),
        precision=lax.Precision.HIGHEST,
        preferred_element_type=jnp.float32,
    )


def product_nn(first_mat, second_mat):
    return jnp.dot(
        first_mat, second_mat, precision=lax.Precision.HIGHEST, preferred_element_type=jnp.float32
    )


def pair_grad(cosines, row_owner, col_owner, logit_scale, logit_bias):
    labels = jnp.where(row_owner[:, None] == col_owner[None, :], 1.0, -1.0)
    logits = logit_scale * cosines + logit_bias
    return -labels * jax.nn.sigmoid(-labels * logits)


def pair_terms(image_unit, row_owner, text_block, col_owner, logit_scale, logit_bias):
    slab_rows = image_unit.shape[0] // lax.axis_size("tower")
    first_own = lax.axis_index("tower") * slab_rows
    own_logits = lax.psum_scatter(
        product_nt(image_unit, text_block), "tower", scatter_dimension=0, tiled=True
    )
    own_owners = lax.dynamic_slice_in_dim(row_owner, first_own, slab_rows)
    grad_rows = pair_grad(own_logits, own_owners, col_owner, logit_scale, logit_bias)
    grad_piece = lax.all_gather(grad_rows, "tower", axis=0, tiled=True)
    image_part = product_nn(grad_piece, text_block)
    return (image_part, product_tn(grad_piece, image_unit))


def local(image_emb, text_emb, image_owner, text_owner, log_scale, bias):
    row_count = image_emb.shape[0]
    loop_size = lax.axis_size("loop")
    loop_pos = lax.axis_index("loop")
    logit_scale = jnp.exp(log_scale[0])
    logit_bias = bias[0]
    all_owner = lax.all_gather(text_owner, "loop", axis=0, tiled=True)
    squares = lax.psum(
        (jnp.sum(image_emb * image_emb, axis=1), jnp.sum(text_emb * text_emb, axis=1)), "tower"
    )
    image_inv = lax.rsqrt(squares[0] + EPSILON)[:, None]
    text_inv = lax.rsqrt(squares[1] + EPSILON)[:, None]
    image_unit = image_emb * image_inv
    text_unit = text_emb * text_inv

    def anchor_of(step_index):
        anchor = (loop_pos - step_index) % loop_size
        return (lax.dynamic_slice_in_dim(all_owner, anchor * row_count, row_count), anchor)

    image_start = jnp.zeros_like(image_unit)

    def cycle_step(step_index, state):
        text_block, text_acc, image_acc = state
        col_owner, anchor = anchor_of(step_index)
        image_term, text_term = pair_terms(
            image_unit, image_owner, text_block, col_owner, logit_scale, logit_bias
        )
        moved = from_behind((text_block, text_acc + text_term), "loop", 1)
        return (moved[0], moved[1], image_acc + image_term)

    text_block, text_acc, image_acc = lax.fori_loop(
        0, loop_size - 1, cycle_step, (text_unit, jnp.zeros_like(text_unit), image_start)
    )
    col_owner, anchor = anchor_of(loop_size - 1)
    image_term, text_term = pair_terms(
        image_unit, image_owner, text_block, col_owner, logit_scale, logit_bias
    )
    image_acc = image_acc + image_term
    text_sum = from_behind(text_acc + text_term, "loop", 1)
    image_unit_grad = logit_scale * image_acc
    text_unit_grad = logit_scale * text_sum
    projections = lax.psum(
        (
            jnp.sum(image_unit * image_unit_grad, axis=1),
            jnp.sum(text_unit * text_unit_grad, axis=1),
        ),
        "tower",
    )
    image_result = (image_unit_grad - image_unit * projections[0][:, None]) * image_inv
    text_result = (text_unit_grad - text_unit * projections[1][:, None]) * text_inv
    return (image_result, text_result)


def solution(mesh):
    placed = (P("loop", "tower"), P("loop", "tower"), P("loop"), P("loop"), P(), P())
    return jax.shard_map(
        local,
        mesh=mesh,
        in_specs=placed,
        out_specs=(P("loop", "tower"), P("loop", "tower")),
        check_vma=False,
    )
```

profile of v0, /device:TPU:1, one launch (start us, length us, event | category | flops | bytes accessed | tf_op | source)
XLA Modules:
  0.0 926.7 jit_solution(10372695101666470187)
XLA Ops:
  8.0 12.1 %all-gather = s32[8,1,256]{2,1,0:T(1,128)S(1)} all-gather(s32[1,1,256]{2,1,0:T(1,128)} %bitcast.30), channel_id=1, replica_groups=mesh['loop'=8,'tower'=16] {'loop'}, dimensions={0}, use_global_device_ids=true | all-gather | bytes 9216 | tf_op jit(solution)/shard_map/all_gather | solution.py:65
  21.2 34.7 %all-reduce.1 = (f32[256]{0:T(256)S(1)}, f32[256]{0:T(256)S(1)}) all-reduce(f32[256]{0:T(256)S(1)} %multiply_reduce_fusion.3, f32[256]{0:T(256)S(1)} %multiply_reduce_fusion.2), channel_id=1, replica_groups=mesh['loop'=8,'tower'=16] {'tower'}, use_global_device_ids=true, to_apply=%region_1.0 | all-reduce | flops 512 | bytes 4096 | tf_op jit(solution)/shard_map/psum | solution.py:66
  57.5 727.1 %while.20 = (s32[]{:T(128)}, f32[256,72]{1,0:T(8,128)S(1)}, f32[256,72]{0,1:T(8,128)S(1)}, f32[256,72]{0,1:T(8,128)S(1)}, s32[256]{0:T(256)S(1)}, /*index=5*/s32...) while((s32[]{:T(128)}, f32[256,72]{1,0:T(8,128)S(1)}, ...), condition=%wide.region_6.7_spmd.clone, body=%wide.region_4.6_spmd.clone.sunk | while | flops 169965568 | bytes 3264224 | solution.py:89
  65.4 67.8 %reduce-scatter.5.cloned.1.call-done = f32[16,256]{1,0:T(8,128)} async-done(((f32[256,256]{1,0:T(8,128)}), f32[16,256]{1,0:T(8,128)}) %reduce-scatter.5.cloned.1.call-update) | async-done | bytes 16400 | tf_op jit(solution)/shard_map/while/body/eval_jaxpr/reduce_scatter | solution.py:49
  134.6 17.0 %all_gather.20 = f32[256,256]{1,0:T(8,128)S(1)} all-gather(f32[16,256]{1,0:T(8,128)S(1)} %divide_multiply_fusion.3), channel_id=1, replica_groups=mesh['loop'=8,'tower'=16] {'tower'}, dimensions={0}, use_global_device_ids=true | all-gather | bytes 278528 | tf_op jit(solution)/shard_map/while/body/eval_jaxpr/all_gather | solution.py:54
  152.0 9.5 %collective-permute-start.1 = (f32[256,72]{0,1:T(8,128)S(1)}, f32[256,72]{0,1:T(8,128)S(1)}, u32[]{:S(2)}, u32[]{:S(2)}) collective-permute-start(f32[256,72]{0,1:T(8,128)S(1)} %convolution_add_fusion.6), channel_id=1, source_target_pairs={{0,16},{16,32},{32,48},{48,64},{64,80},{80,96},{96,112},{112,0},{1... | collective-permute-start | bytes 221192 | tf_op jit(solution)/shard_map/while/body/eval_jaxpr/ppermute | solution.py:11
  166.6 70.2 %reduce-scatter.5.cloned.1.call-done = f32[16,256]{1,0:T(8,128)} async-done(((f32[256,256]{1,0:T(8,128)}), f32[16,256]{1,0:T(8,128)}) %reduce-scatter.5.cloned.1.call-update) | async-done | bytes 16400 | tf_op jit(solution)/shard_map/while/body/eval_jaxpr/reduce_scatter | solution.py:49
  238.2 17.3 %all_gather.20 = f32[256,256]{1,0:T(8,128)S(1)} all-gather(f32[16,256]{1,0:T(8,128)S(1)} %divide_multiply_fusion.3), channel_id=1, replica_groups=mesh['loop'=8,'tower'=16] {'tower'}, dimensions={0}, use_global_device_ids=true | all-gather | bytes 278528 | tf_op jit(solution)/shard_map/while/body/eval_jaxpr/all_gather | solution.py:54
  255.9 9.5 %collective-permute-start.1 = (f32[256,72]{0,1:T(8,128)S(1)}, f32[256,72]{0,1:T(8,128)S(1)}, u32[]{:S(2)}, u32[]{:S(2)}) collective-permute-start(f32[256,72]{0,1:T(8,128)S(1)} %convolution_add_fusion.6), channel_id=1, source_target_pairs={{0,16},{16,32},{32,48},{48,64},{64,80},{80,96},{96,112},{112,0},{1... | collective-permute-start | bytes 221192 | tf_op jit(solution)/shard_map/while/body/eval_jaxpr/ppermute | solution.py:11
  270.4 70.3 %reduce-scatter.5.cloned.1.call-done = f32[16,256]{1,0:T(8,128)} async-done(((f32[256,256]{1,0:T(8,128)}), f32[16,256]{1,0:T(8,128)}) %reduce-scatter.5.cloned.1.call-update) | async-done | bytes 16400 | tf_op jit(solution)/shard_map/while/body/eval_jaxpr/reduce_scatter | solution.py:49
  342.2 17.0 %all_gather.20 = f32[256,256]{1,0:T(8,128)S(1)} all-gather(f32[16,256]{1,0:T(8,128)S(1)} %divide_multiply_fusion.3), channel_id=1, replica_groups=mesh['loop'=8,'tower'=16] {'tower'}, dimensions={0}, use_global_device_ids=true | all-gather | bytes 278528 | tf_op jit(solution)/shard_map/while/body/eval_jaxpr/all_gather | solution.py:54
  374.1 70.0 %reduce-scatter.5.cloned.1.call-done = f32[16,256]{1,0:T(8,128)} async-done(((f32[256,256]{1,0:T(8,128)}), f32[16,256]{1,0:T(8,128)}) %reduce-scatter.5.cloned.1.call-update) | async-done | bytes 16400 | tf_op jit(solution)/shard_map/while/body/eval_jaxpr/reduce_scatter | solution.py:49
  445.6 17.0 %all_gather.20 = f32[256,256]{1,0:T(8,128)S(1)} all-gather(f32[16,256]{1,0:T(8,128)S(1)} %divide_multiply_fusion.3), channel_id=1, replica_groups=mesh['loop'=8,'tower'=16] {'tower'}, dimensions={0}, use_global_device_ids=true | all-gather | bytes 278528 | tf_op jit(solution)/shard_map/while/body/eval_jaxpr/all_gather | solution.py:54
  477.5 70.1 %reduce-scatter.5.cloned.1.call-done = f32[16,256]{1,0:T(8,128)} async-done(((f32[256,256]{1,0:T(8,128)}), f32[16,256]{1,0:T(8,128)}) %reduce-scatter.5.cloned.1.call-update) | async-done | bytes 16400 | tf_op jit(solution)/shard_map/while/body/eval_jaxpr/reduce_scatter | solution.py:49
  549.0 17.0 %all_gather.20 = f32[256,256]{1,0:T(8,128)S(1)} all-gather(f32[16,256]{1,0:T(8,128)S(1)} %divide_multiply_fusion.3), channel_id=1, replica_groups=mesh['loop'=8,'tower'=16] {'tower'}, dimensions={0}, use_global_device_ids=true | all-gather | bytes 278528 | tf_op jit(solution)/shard_map/while/body/eval_jaxpr/all_gather | solution.py:54
  580.9 70.2 %reduce-scatter.5.cloned.1.call-done = f32[16,256]{1,0:T(8,128)} async-done(((f32[256,256]{1,0:T(8,128)}), f32[16,256]{1,0:T(8,128)}) %reduce-scatter.5.cloned.1.call-update) | async-done | bytes 16400 | tf_op jit(solution)/shard_map/while/body/eval_jaxpr/reduce_scatter | solution.py:49
  652.6 17.0 %all_gather.20 = f32[256,256]{1,0:T(8,128)S(1)} all-gather(f32[16,256]{1,0:T(8,128)S(1)} %divide_multiply_fusion.3), channel_id=1, replica_groups=mesh['loop'=8,'tower'=16] {'tower'}, dimensions={0}, use_global_device_ids=true | all-gather | bytes 278528 | tf_op jit(solution)/shard_map/while/body/eval_jaxpr/all_gather | solution.py:54
  669.9 9.5 %collective-permute-start.1 = (f32[256,72]{0,1:T(8,128)S(1)}, f32[256,72]{0,1:T(8,128)S(1)}, u32[]{:S(2)}, u32[]{:S(2)}) collective-permute-start(f32[256,72]{0,1:T(8,128)S(1)} %convolution_add_fusion.6), channel_id=1, source_target_pairs={{0,16},{16,32},{32,48},{48,64},{64,80},{80,96},{96,112},{112,0},{1... | collective-permute-start | bytes 221192 | tf_op jit(solution)/shard_map/while/body/eval_jaxpr/ppermute | solution.py:11
  684.5 70.5 %reduce-scatter.5.cloned.1.call-done = f32[16,256]{1,0:T(8,128)} async-done(((f32[256,256]{1,0:T(8,128)}), f32[16,256]{1,0:T(8,128)}) %reduce-scatter.5.cloned.1.call-update) | async-done | bytes 16400 | tf_op jit(solution)/shard_map/while/body/eval_jaxpr/reduce_scatter | solution.py:49
  756.4 17.0 %all_gather.20 = f32[256,256]{1,0:T(8,128)S(1)} all-gather(f32[16,256]{1,0:T(8,128)S(1)} %divide_multiply_fusion.3), channel_id=1, replica_groups=mesh['loop'=8,'tower'=16] {'tower'}, dimensions={0}, use_global_device_ids=true | all-gather | bytes 278528 | tf_op jit(solution)/shard_map/while/body/eval_jaxpr/all_gather | solution.py:54
  786.6 71.2 %reduce-scatter.3.cloned.1.call-done = f32[16,256]{1,0:T(8,128)} async-done(((f32[256,256]{1,0:T(8,128)}), f32[16,256]{1,0:T(8,128)}) %reduce-scatter.3.cloned.1.call-update) | async-done | bytes 16400 | tf_op jit(solution)/shard_map/reduce_scatter | solution.py:49
  858.6 17.2 %all_gather.17 = f32[256,256]{1,0:T(8,128)S(1)} all-gather(f32[16,256]{1,0:T(8,128)S(1)} %divide_multiply_fusion.1), channel_id=1, replica_groups=mesh['loop'=8,'tower'=16] {'tower'}, dimensions={0}, use_global_device_ids=true | all-gather | bytes 278528 | tf_op jit(solution)/shard_map/all_gather | solution.py:54
  876.1 9.6 %collective-permute-start.2 = (f32[256,72]{0,1:T(8,128)S(1)}, f32[256,72]{0,1:T(8,128)S(1)}, u32[]{:S(2)}, u32[]{:S(2)}) collective-permute-start(f32[256,72]{0,1:T(8,128)S(1)} %convolution_add_fusion.2), channel_id=1, source_target_pairs={{0,16},{16,32},{32,48},{48,64},{64,80},{80,96},{96,112},{112,0},{1... | collective-permute-start | bytes 221192 | tf_op jit(solution)/shard_map/ppermute | solution.py:11
  887.1 30.9 %all-reduce = (f32[256]{0:T(256)S(1)}, f32[256]{0:T(256)S(1)}) all-reduce(f32[256]{0:T(256)S(1)} %get-tuple-element.327, f32[256]{0:T(256)S(1)} %multiply_reduce_fusion), channel_id=1, replica_groups=mesh['loop'=8,'tower'=16] {'tower'}, use_global_device_ids=true, to_apply=%region_9.10 | all-reduce | flops 512 | bytes 4096 | tf_op jit(solution)/shard_map/psum | solution.py:100
  (115 shorter events, 97.0 us)
Async XLA Ops:
  20.1 35.7 %copy-start.1 = (f32[256,72]{0,1:T(8,128)S(1)}, f32[256,72]{0,1:T(8,128)}, u32[]{:S(2)}) copy-start(f32[256,72]{0,1:T(8,128)} %param.8) | copy-start | bytes 221188
  57.5 75.7 %reduce-scatter.5.cloned.1.call-start = ((), (), s32[]{:S(2)}) async-start(), calls=%async_computation.3 | async-start | bytes 278528 | tf_op jit(solution)/shard_map/while/body/eval_jaxpr/reduce_scatter | solution.py:49
  58.6 103.4 %collective-permute-start = (f32[256,72]{1,0:T(8,128)S(1)}, f32[256,72]{1,0:T(8,128)S(1)}, u32[]{:S(2)}, u32[]{:S(2)}) collective-permute-start(f32[256,72]{1,0:T(8,128)S(1)} %copy.17), channel_id=1, source_target_pairs={{0,16},{16,32},{32,48},{48,64},{64,80},{80,96},{96,112},{112,0},{1... | collective-permute-start | bytes 221192 | tf_op jit(solution)/shard_map/while/body/eval_jaxpr/ppermute | solution.py:11
  152.0 10.9 %collective-permute-start.1 = (f32[256,72]{0,1:T(8,128)S(1)}, f32[256,72]{0,1:T(8,128)S(1)}, u32[]{:S(2)}, u32[]{:S(2)}) collective-permute-start(f32[256,72]{0,1:T(8,128)S(1)} %convolution_add_fusion.6), channel_id=1, source_target_pairs={{0,16},{16,32},{32,48},{48,64},{64,80},{80,96},{96,112},{112,0},{1... | collective-permute-start | bytes 221192 | tf_op jit(solution)/shard_map/while/body/eval_jaxpr/ppermute | solution.py:11
  162.9 73.8 %reduce-scatter.5.cloned.1.call-start = ((), (), s32[]{:S(2)}) async-start(), calls=%async_computation.3 | async-start | bytes 278528 | tf_op jit(solution)/shard_map/while/body/eval_jaxpr/reduce_scatter | solution.py:49
  164.1 101.7 %collective-permute-start = (f32[256,72]{1,0:T(8,128)S(1)}, f32[256,72]{1,0:T(8,128)S(1)}, u32[]{:S(2)}, u32[]{:S(2)}) collective-permute-start(f32[256,72]{1,0:T(8,128)S(1)} %copy.17), channel_id=1, source_target_pairs={{0,16},{16,32},{32,48},{48,64},{64,80},{80,96},{96,112},{112,0},{1... | collective-permute-start | bytes 221192 | tf_op jit(solution)/shard_map/while/body/eval_jaxpr/ppermute | solution.py:11
  255.9 10.9 %collective-permute-start.1 = (f32[256,72]{0,1:T(8,128)S(1)}, f32[256,72]{0,1:T(8,128)S(1)}, u32[]{:S(2)}, u32[]{:S(2)}) collective-permute-start(f32[256,72]{0,1:T(8,128)S(1)} %convolution_add_fusion.6), channel_id=1, source_target_pairs={{0,16},{16,32},{32,48},{48,64},{64,80},{80,96},{96,112},{112,0},{1... | collective-permute-start | bytes 221192 | tf_op jit(solution)/shard_map/while/body/eval_jaxpr/ppermute | solution.py:11
  266.8 74.0 %reduce-scatter.5.cloned.1.call-start = ((), (), s32[]{:S(2)}) async-start(), calls=%async_computation.3 | async-start | bytes 278528 | tf_op jit(solution)/shard_map/while/body/eval_jaxpr/reduce_scatter | solution.py:49
  267.9 101.6 %collective-permute-start = (f32[256,72]{1,0:T(8,128)S(1)}, f32[256,72]{1,0:T(8,128)S(1)}, u32[]{:S(2)}, u32[]{:S(2)}) collective-permute-start(f32[256,72]{1,0:T(8,128)S(1)} %copy.17), channel_id=1, source_target_pairs={{0,16},{16,32},{32,48},{48,64},{64,80},{80,96},{96,112},{112,0},{1... | collective-permute-start | bytes 221192 | tf_op jit(solution)/shard_map/while/body/eval_jaxpr/ppermute | solution.py:11
  359.6 10.9 %collective-permute-start.1 = (f32[256,72]{0,1:T(8,128)S(1)}, f32[256,72]{0,1:T(8,128)S(1)}, u32[]{:S(2)}, u32[]{:S(2)}) collective-permute-start(f32[256,72]{0,1:T(8,128)S(1)} %convolution_add_fusion.6), channel_id=1, source_target_pairs={{0,16},{16,32},{32,48},{48,64},{64,80},{80,96},{96,112},{112,0},{1... | collective-permute-start | bytes 221192 | tf_op jit(solution)/shard_map/while/body/eval_jaxpr/ppermute | solution.py:11
  370.5 73.6 %reduce-scatter.5.cloned.1.call-start = ((), (), s32[]{:S(2)}) async-start(), calls=%async_computation.3 | async-start | bytes 278528 | tf_op jit(solution)/shard_map/while/body/eval_jaxpr/reduce_scatter | solution.py:49
  371.6 101.3 %collective-permute-start = (f32[256,72]{1,0:T(8,128)S(1)}, f32[256,72]{1,0:T(8,128)S(1)}, u32[]{:S(2)}, u32[]{:S(2)}) collective-permute-start(f32[256,72]{1,0:T(8,128)S(1)} %copy.17), channel_id=1, source_target_pairs={{0,16},{16,32},{32,48},{48,64},{64,80},{80,96},{96,112},{112,0},{1... | collective-permute-start | bytes 221192 | tf_op jit(solution)/shard_map/while/body/eval_jaxpr/ppermute | solution.py:11
  463.0 10.9 %collective-permute-start.1 = (f32[256,72]{0,1:T(8,128)S(1)}, f32[256,72]{0,1:T(8,128)S(1)}, u32[]{:S(2)}, u32[]{:S(2)}) collective-permute-start(f32[256,72]{0,1:T(8,128)S(1)} %convolution_add_fusion.6), channel_id=1, source_target_pairs={{0,16},{16,32},{32,48},{48,64},{64,80},{80,96},{96,112},{112,0},{1... | collective-permute-start | bytes 221192 | tf_op jit(solution)/shard_map/while/body/eval_jaxpr/ppermute | solution.py:11
  473.8 73.7 %reduce-scatter.5.cloned.1.call-start = ((), (), s32[]{:S(2)}) async-start(), calls=%async_computation.3 | async-start | bytes 278528 | tf_op jit(solution)/shard_map/while/body/eval_jaxpr/reduce_scatter | solution.py:49
  475.0 101.4 %collective-permute-start = (f32[256,72]{1,0:T(8,128)S(1)}, f32[256,72]{1,0:T(8,128)S(1)}, u32[]{:S(2)}, u32[]{:S(2)}) collective-permute-start(f32[256,72]{1,0:T(8,128)S(1)} %copy.17), channel_id=1, source_target_pairs={{0,16},{16,32},{32,48},{48,64},{64,80},{80,96},{96,112},{112,0},{1... | collective-permute-start | bytes 221192 | tf_op jit(solution)/shard_map/while/body/eval_jaxpr/ppermute | solution.py:11
  566.4 10.9 %collective-permute-start.1 = (f32[256,72]{0,1:T(8,128)S(1)}, f32[256,72]{0,1:T(8,128)S(1)}, u32[]{:S(2)}, u32[]{:S(2)}) collective-permute-start(f32[256,72]{0,1:T(8,128)S(1)} %convolution_add_fusion.6), channel_id=1, source_target_pairs={{0,16},{16,32},{32,48},{48,64},{64,80},{80,96},{96,112},{112,0},{1... | collective-permute-start | bytes 221192 | tf_op jit(solution)/shard_map/while/body/eval_jaxpr/ppermute | solution.py:11
  577.3 73.8 %reduce-scatter.5.cloned.1.call-start = ((), (), s32[]{:S(2)}) async-start(), calls=%async_computation.3 | async-start | bytes 278528 | tf_op jit(solution)/shard_map/while/body/eval_jaxpr/reduce_scatter | solution.py:49
  578.4 101.4 %collective-permute-start = (f32[256,72]{1,0:T(8,128)S(1)}, f32[256,72]{1,0:T(8,128)S(1)}, u32[]{:S(2)}, u32[]{:S(2)}) collective-permute-start(f32[256,72]{1,0:T(8,128)S(1)} %copy.17), channel_id=1, source_target_pairs={{0,16},{16,32},{32,48},{48,64},{64,80},{80,96},{96,112},{112,0},{1... | collective-permute-start | bytes 221192 | tf_op jit(solution)/shard_map/while/body/eval_jaxpr/ppermute | solution.py:11
  669.9 10.9 %collective-permute-start.1 = (f32[256,72]{0,1:T(8,128)S(1)}, f32[256,72]{0,1:T(8,128)S(1)}, u32[]{:S(2)}, u32[]{:S(2)}) collective-permute-start(f32[256,72]{0,1:T(8,128)S(1)} %convolution_add_fusion.6), channel_id=1, source_target_pairs={{0,16},{16,32},{32,48},{48,64},{64,80},{80,96},{96,112},{112,0},{1... | collective-permute-start | bytes 221192 | tf_op jit(solution)/shard_map/while/body/eval_jaxpr/ppermute | solution.py:11
  680.8 74.1 %reduce-scatter.5.cloned.1.call-start = ((), (), s32[]{:S(2)}) async-start(), calls=%async_computation.3 | async-start | bytes 278528 | tf_op jit(solution)/shard_map/while/body/eval_jaxpr/reduce_scatter | solution.py:49
  681.9 101.7 %collective-permute-start = (f32[256,72]{1,0:T(8,128)S(1)}, f32[256,72]{1,0:T(8,128)S(1)}, u32[]{:S(2)}, u32[]{:S(2)}) collective-permute-start(f32[256,72]{1,0:T(8,128)S(1)} %copy.17), channel_id=1, source_target_pairs={{0,16},{16,32},{32,48},{48,64},{64,80},{80,96},{96,112},{112,0},{1... | collective-permute-start | bytes 221192 | tf_op jit(solution)/shard_map/while/body/eval_jaxpr/ppermute | solution.py:11
  773.8 10.9 %collective-permute-start.1 = (f32[256,72]{0,1:T(8,128)S(1)}, f32[256,72]{0,1:T(8,128)S(1)}, u32[]{:S(2)}, u32[]{:S(2)}) collective-permute-start(f32[256,72]{0,1:T(8,128)S(1)} %convolution_add_fusion.6), channel_id=1, source_target_pairs={{0,16},{16,32},{32,48},{48,64},{64,80},{80,96},{96,112},{112,0},{1... | collective-permute-start | bytes 221192 | tf_op jit(solution)/shard_map/while/body/eval_jaxpr/ppermute | solution.py:11
  784.6 73.2 %reduce-scatter.3.cloned.1.call-start = ((), (), s32[]{:S(2)}) async-start(), calls=%async_computation.2 | async-start | bytes 278528 | tf_op jit(solution)/shard_map/reduce_scatter | solution.py:49
  876.1 11.0 %collective-permute-start.2 = (f32[256,72]{0,1:T(8,128)S(1)}, f32[256,72]{0,1:T(8,128)S(1)}, u32[]{:S(2)}, u32[]{:S(2)}) collective-permute-start(f32[256,72]{0,1:T(8,128)S(1)} %convolution_add_fusion.2), channel_id=1, source_target_pairs={{0,16},{16,32},{32,48},{48,64},{64,80},{80,96},{96,112},{112,0},{1... | collective-permute-start | bytes 221192 | tf_op jit(solution)/shard_map/ppermute | solution.py:11
  (2 other events, 13.8 us)
Sparse Core Ops, SparseCore 0:
  61.8 71.3 reduce-scatter.4
  167.3 69.4 reduce-scatter.4
  271.1 69.6 reduce-scatter.4
  374.5 69.5 reduce-scatter.4
  477.8 69.6 reduce-scatter.4
  581.3 69.7 reduce-scatter.4
  685.1 69.7 reduce-scatter.4
Sparse Core Ops, SparseCore 1:
  788.2 69.5 reduce-scatter.2
where the time goes:
time: 936 us; the launch traced here: 927 us
  waiting for transfers between devices  568 us (61%)
  blocking collectives  214 us (23%)
  starting transfers between devices  96.7 us (10%)
  between operations  16.9 us (2%)
  matrix products  14.9 us (2%)
  other arithmetic  13.3 us (1%)
    reduce_scatter x8, waiting for transfers between devices, pair_terms(): lax.psum_scatter(product_nt(image_unit, text_block), 'tower', scatter_dim...  560 us
    all_gather x8, blocking collectives, pair_terms(): grad_piece = lax.all_gather(grad_rows, 'tower', axis=0, tiled=True)  137 us
    ppermute x15, starting transfers between devices, from_behind(): return lax.ppermute(x, axis, [(i, (i + by) % size) for i in range(size)])  96.7 us
    psum x1, blocking collectives, local(): lax.psum((jnp.sum(image_emb * image_emb, axis=1), jnp.sum(text_emb * text...  34.7 us
    psum x1, blocking collectives, local(): lax.psum((jnp.sum(image_unit * image_unit_grad, axis=1), jnp.sum(text_uni...  30.9 us
  transfers between devices with their start and end apart: 23, of which 16 were waited for; matrix products, arithmetic and copies ran while one was open for 2% of the time, Pallas kernels for 0%

commit v1 on v0

v1 whole, which is shorter than its diff:
```python
import jax
import jax.numpy as jnp
from jax import lax
from jax.experimental import pallas as pl
from jax.experimental.pallas import tpu as pltpu
from jax.sharding import Mesh
from jax.sharding import PartitionSpec as P

EPSILON = 1e-06
F32 = jnp.float32
BF16 = jnp.bfloat16

FEATS = 72
HALF = 40
ROWS = 256
PART = 64
PEERS = 64


def other_core(x):
    return lax.ppermute(x, "c", [(0, 1), (1, 0)])


def spare_rows(core, count):
    row = lax.broadcasted_iota(jnp.int32, (count, 1), 0) % HALF
    low = jnp.where(core == 0, HALF - 4, 0)
    return (row >= low) & (row < low + 4)


def halves(x):
    high = x.astype(BF16)
    return high, (x - high.astype(F32)).astype(BF16)


def product(first, second):
    a, b = halves(first)
    c, d = halves(second)

    def dot(p, q):
        return jnp.dot(p, q, preferred_element_type=F32)

    return dot(a, c) + (dot(a, d) + dot(b, c))


def pack_kernel(image, image_far, text, text_far, image_owner, text_owner, out):
    core = lax.axis_index("c")
    spare = spare_rows(core, HALF)

    def both(near, far, owner):
        def half(ref):
            turned = ref[...].T
            return jnp.where(core == 0, turned[:HALF], turned[FEATS - HALF :])

        own = jnp.where(spare, owner[...].astype(F32), half(near))
        other = jnp.where(spare, 0.0, half(far))
        return jnp.concatenate(
            [jnp.where(core == 0, own, other), jnp.where(core == 0, other, own)], axis=1
        )

    images = both(image, image_far, image_owner)
    texts = both(text, text_far, text_owner)
    for i in range(8):
        for j in range(8):
            out[i * 8 + j] = jnp.concatenate(
                [images[:, i * PART : (i + 1) * PART], texts[:, j * PART : (j + 1) * PART]], axis=1
            )


def unpacked(pieces, spare):
    blocks = [pieces[x * 16 : (x + 1) * 16].reshape(16 * HALF, 2 * PART) for x in range(4)]
    image = jnp.concatenate([b[:, :PART] for b in blocks], axis=1)
    text = jnp.concatenate([b[:, PART:] for b in blocks], axis=1)
    return jnp.where(spare, 0.0, image), jnp.where(spare, 0.0, text)


def gram_kernel(pieces, out):
    core = lax.axis_index("c")
    image, text = unpacked(pieces, spare_rows(core, 16 * HALF))
    out[:ROWS] = product(image.T, text)
    owners = [
        jnp.where(core == 0, pieces[x * 16, HALF - 4 : HALF - 3], pieces[x * 16, 0:1])
        for x in range(4)
    ]
    out[ROWS : ROWS + 8] = jnp.concatenate(
        [
            jnp.sum(image * image, axis=0, keepdims=True),
            jnp.sum(text * text, axis=0, keepdims=True),
            jnp.concatenate([o[:, :PART] for o in owners], axis=1),
            jnp.concatenate([o[:, PART:] for o in owners], axis=1),
            jnp.zeros((4, ROWS), F32),
        ],
        axis=0,
    )


def grad_kernel(log_scale, bias, pieces, near, far, out):
    core = lax.axis_index("c")
    image, text = unpacked(pieces, spare_rows(core, 16 * HALF))
    scale = jnp.exp(jnp.full((1, 1), log_scale[0], F32))
    extra = near[ROWS:] + far[ROWS:]
    extra_turned = extra.T
    image_inv = lax.rsqrt(extra[0:1] + EPSILON)
    text_inv = lax.rsqrt(extra[1:2] + EPSILON)
    image_inv_col = lax.rsqrt(extra_turned[:, 0:1] + EPSILON)
    inv = image_inv_col * text_inv
    cosines = (near[:ROWS] + far[:ROWS]) * inv
    labels = jnp.where(extra_turned[:, 2:3] == extra[3:4], 1.0, -1.0)
    logits = scale * cosines + bias[0]
    grads = scale * (-labels * jax.nn.sigmoid(-labels * logits))
    weighted = grads * cosines
    text_dot = jnp.sum(weighted, axis=0, keepdims=True)
    image_dot = jnp.broadcast_to(jnp.sum(weighted, axis=1, keepdims=True), (ROWS, 128)).T[0:1]
    mixed = grads * inv
    image_grad = product(text, mixed.T) - image * (image_inv * image_inv * image_dot)
    text_grad = product(image, mixed) - text * (text_inv * text_inv * text_dot)
    for x in range(4):
        own = slice(x * PART, (x + 1) * PART)
        out[x * 16 : (x + 1) * 16] = jnp.concatenate(
            [image_grad[:, own], text_grad[:, own]], axis=1
        ).reshape(16, HALF, 2 * PART)


def sum_kernel(pieces, own, send):
    core = lax.axis_index("c")
    image_sums = [sum(pieces[i * 8 + j] for j in range(8)) for i in range(8)]
    text_sums = [sum(pieces[i * 8 + j] for i in range(8)) for j in range(8)]
    for k, sums, part in ((0, image_sums, slice(0, PART)), (1, text_sums, slice(PART, 2 * PART))):
        low = jnp.concatenate([s[:, part] for s in sums[:4]], axis=1)
        high = jnp.concatenate([s[:, part] for s in sums[4:]], axis=1)
        own[k] = jnp.where(core == 0, low, high)
        send[k] = jnp.where(core == 0, high, low)


def finish_kernel(own, received, image_grad, text_grad):
    core = lax.axis_index("c")
    for k, out in ((0, image_grad), (1, text_grad)):
        low = jnp.where(core == 0, own[k], received[k])
        high = jnp.where(core == 0, received[k], own[k])
        full = jnp.concatenate([low[:32], low[32:] + high[:8], high[8:]], axis=0)
        out[...] = full.T


def call(kernel, outs, args, scalars=0):
    smem = [pl.BlockSpec(memory_space=pltpu.SMEM)] * scalars
    vmem = [pl.BlockSpec(memory_space=pltpu.VMEM)] * (len(args) - scalars)
    return pl.pallas_call(
        kernel,
        out_shape=[jax.ShapeDtypeStruct(s, F32) for s in outs],
        in_specs=smem + vmem,
        out_specs=[pl.BlockSpec(memory_space=pltpu.VMEM)] * len(outs),
        compiler_params=pltpu.CompilerParams(vmem_limit_bytes=40 * 1024 * 1024),
    )(*args)


def local(image_emb, text_emb, image_owner, text_owner, log_scale, bias):
    image_far = other_core(image_emb)
    text_far = other_core(text_emb)
    pieces = (PEERS, HALF, 2 * PART)
    (packed,) = call(
        pack_kernel,
        [pieces],
        (
            image_emb,
            image_far,
            text_emb,
            text_far,
            image_owner.reshape(1, ROWS),
            text_owner.reshape(1, ROWS),
        ),
    )
    held = lax.all_to_all(packed, ("x", "tower"), 0, 0, tiled=True)
    (partial,) = call(gram_kernel, [(ROWS + 8, ROWS)], (held,))
    (grads,) = call(
        grad_kernel, [pieces], (log_scale, bias, held, partial, other_core(partial)), scalars=2
    )
    back = lax.all_to_all(grads, ("x", "tower"), 0, 0, tiled=True)
    own, send = call(sum_kernel, [(2, HALF, ROWS)] * 2, (back,))
    return tuple(call(finish_kernel, [(ROWS, FEATS)] * 2, (own, other_core(send))))


def solution(mesh):
    fine = Mesh(mesh.devices.reshape(4, 2, 16), ("x", "c", "tower"))
    rows = P(("x", "c"))
    block = P(("x", "c"), "tower")
    return jax.shard_map(
        local,
        mesh=fine,
        in_specs=(block, block, rows, rows, P(), P()),
        out_specs=(block, block),
        check_vma=False,
    )
```

time: 936 us -> 74.2 us (0.08)
  waiting for transfers between devices: 568 us -> 2.25 us
  blocking collectives: 214 us -> 55.1 us
  starting transfers between devices: 96.7 us -> 6.72 us
  matrix products: 14.9 us -> 0 us
  between operations: 16.9 us -> 2 us
  other arithmetic: 13.3 us -> 0 us
    reduce_scatter x8 -> x0, waiting for transfers between devices: 560 us -> none  [pair_terms(): lax.psum_scatter(product_nt(image_unit, text_block), 'tower', scatter_dim...]
    all_gather x9 -> x0, blocking collectives: 149 us -> none  [the longest x8 137 us: pair_terms(): grad_piece = lax.all_gather(grad_rows, 'tower', axis=0, tiled=True)]
    ppermute x15 -> x4, starting transfers between devices: 96.7 us -> 6.72 us  [other_core(): return lax.ppermute(x, 'c', [(0, 1), (1, 0)])]
    psum x2 -> x0, blocking collectives: 65.6 us -> none  [the longest x1 34.7 us: local(): lax.psum((jnp.sum(image_emb * image_emb, axis=1), jnp.sum(text_emb * text...]
    all_to_all x0 -> x2, blocking collectives: none -> 55.1 us  [the longest x1 31 us: local(): held = lax.all_to_all(packed, ('x', 'tower'), 0, 0, tiled=True)]
    dot_general x24 -> x0, matrix products: 14.9 us -> none  [the longest x8 8.64 us: product_nt(): lax.dot_general(first_mat, second_mat, (((1,), (1,)), ((), ())), precisio...]
    mul x12 -> x0, other arithmetic: 12.3 us -> none  [the longest x8 10.9 us: pair_grad(): return -labels * jax.nn.sigmoid(-labels * logits)]
  transfers between devices with their start and end apart: 23 -> 4, of which waited for: 16 -> 2; matrix products, arithmetic and copies ran while one was open for 2% -> 1% of each run, Pallas kernels for 0% -> 0%
where the time goes in v1:
time: 74.2 us; the launch traced here: 73.9 us
  blocking collectives  55.1 us (74%)
  starting transfers between devices  6.72 us (9%)
  local copies, waits for them, and re-layouts  4.75 us (6%)
  Pallas kernels  3.07 us (4%)
  waiting for transfers between devices  2.25 us (3%)
  between operations  2 us (3%)
    all_to_all x1, blocking collectives, local(): held = lax.all_to_all(packed, ('x', 'tower'), 0, 0, tiled=True)  31 us
    all_to_all x1, blocking collectives, local(): back = lax.all_to_all(grads, ('x', 'tower'), 0, 0, tiled=True)  24.2 us
    ppermute x4, starting transfers between devices, other_core(): return lax.ppermute(x, 'c', [(0, 1), (1, 0)])  6.72 us
    unnamed x6, local copies, waits for them, and re-layouts  3.31 us
    pallas_call x5, Pallas kernels, call(): pl.pallas_call(kernel, out_shape=[jax.ShapeDtypeStruct(s, F32) for s in o...  3.07 us
    ppermute x4, waiting for transfers between devices, other_core(): return lax.ppermute(x, 'c', [(0, 1), (1, 0)])  2.25 us
  transfers between devices with their start and end apart: 4, of which 2 were waited for; matrix products, arithmetic and copies ran while one was open for 1% of the time, Pallas kernels for 0%

profile of v1, /device:TPU:1, one launch (start us, length us, event | category | flops | bytes accessed | tf_op | source)
XLA Modules:
  0.0 73.9 jit_solution(10991961049465907377)
XLA Ops:
  0.6 1.0 %copy.11.text = f32[256,72]{1,0:T(8,128)S(1)} copy(f32[256,72]{0,1:T(8,128)} %param.7) | data formatting | bytes 147456 | tf_op args[1]
  1.6 1.5 %collective-permute-start.1 = (f32[256,72]{1,0:T(8,128)S(1)}, f32[256,72]{1,0:T(8,128)S(1)}, u32[]{:S(2)}, u32[]{:S(2)}) collective-permute-start(f32[256,72]{1,0:T(8,128)S(1)} %copy.11.text), channel_id=1, source_target_pairs={{0,16},{16,0},{1,17},{17,1},{2,18},{18,2},{3,19},{19,3},{4,20},{20... | collective-permute-start | bytes 221192 | tf_op jit(solution)/shard_map/ppermute | solution.py:21
  3.1 1.0 %copy.10.image = f32[256,72]{1,0:T(8,128)S(1)} copy(f32[256,72]{0,1:T(8,128)} %param.6) | data formatting | bytes 147456 | tf_op args[0]
  4.1 0.1 collective-permute-start
  4.2 0.0 collective-permute-done.1.text_far
  4.2 1.3 %collective-permute-done.image_far = f32[256,72]{1,0:T(8,128)S(1)} collective-permute-done((f32[256,72]{1,0:T(8,128)S(1)}, f32[256,72]{1,0:T(8,128)S(1)}, u32[]{:S(2)}, u32[]{:S(2)}) %collective-permute-start) | collective-permute-done | bytes 73760 | tf_op jit(solution)/shard_map/ppermute | solution.py:21
  5.5 0.0 copy-start
  5.5 0.7 copy-done
  6.2 0.0 copy-start.1
  6.2 0.7 copy-done.1
  6.9 0.3 shard_map.77
  7.2 31.0 %all_to_all.10.pieces = f32[64,40,128]{2,1,0:T(8,128)S(1)} all-to-all(f32[64,40,128]{2,1,0:T(8,128)S(1)} %shard_map.77), channel_id=1, replica_groups=mesh['x'=4,'c'=2,'tower'=16] {'x','tower'}, dimensions={0} | all-to-all | bytes 2621440 | tf_op jit(solution)/shard_map/all_to_all | solution.py:171
  38.2 0.9 %shard_map.78.near = f32[264,256]{1,0:T(8,128)S(1)} custom-call(f32[64,40,128]{2,1,0:T(8,128)S(1)} %all_to_all.10.pieces), custom_call_target="tpu_custom_call" | custom-call | tf_op jit(solution)/shard_map/pallas_call | solution.py:146
  39.1 2.5 %collective-permute-start.2 = (f32[264,256]{1,0:T(8,128)S(1)}, f32[264,256]{1,0:T(8,128)S(1)}, u32[]{:S(2)}, u32[]{:S(2)}) collective-permute-start(f32[264,256]{1,0:T(8,128)S(1)} %shard_map.78.near), channel_id=1, source_target_pairs={{0,16},{16,0},{1,17},{17,1},{2,18},{18,2},{3,19},{19,3},{4,20},{20... | collective-permute-start | bytes 811016 | tf_op jit(solution)/shard_map/ppermute | solution.py:21
  42.9 0.0 collective-permute-done.2.far
  42.9 1.6 %shard_map.79 = f32[64,40,128]{2,1,0:T(8,128)S(1)} custom-call(f32[1]{0:T(128)S(6)} %copy.14.log_scale, f32[1]{0:T(128)S(6)} %copy.15.bias, f32[64,40,128]{2,1,0:T(8,128)S(1)} %all_to_all.10.pieces, f32[264,256]{1,0:T(8,128)S(1)} %shard_map.78.near, f32[264,256]{1,0:T(8,128)S(1)} %collective-permute-done.2.far), custom_call_target="tpu_custom_call" | custom-call | tf_op jit(solution)/shard_map/pallas_call | solution.py:146
  44.5 24.2 %all_to_all.11.pieces = f32[64,40,128]{2,1,0:T(8,128)S(1)} all-to-all(f32[64,40,128]{2,1,0:T(8,128)S(1)} %shard_map.79), channel_id=1, replica_groups=mesh['x'=4,'c'=2,'tower'=16] {'x','tower'}, dimensions={0} | all-to-all | bytes 2621440 | tf_op jit(solution)/shard_map/all_to_all | solution.py:176
  68.7 0.1 shard_map.80
  68.8 2.6 %collective-permute-start.3 = (f32[2,40,256]{2,1,0:T(8,128)S(1)}, f32[2,40,256]{2,1,0:T(8,128)S(1)}, u32[]{:S(2)}, u32[]{:S(2)}) collective-permute-start(f32[2,40,256]{2,1,0:T(8,128)S(1)} %get-tuple-element.5), channel_id=1, source_target_pairs={{0,16},{16,0},{1,17},{17,1},{2,18},{18,2},{3,19},{19,3},{4,20},{20... | collective-permute-start | bytes 245768 | tf_op jit(solution)/shard_map/ppermute | solution.py:21
  71.4 0.9 %collective-permute-done.3.received = f32[2,40,256]{2,1,0:T(8,128)S(1)} collective-permute-done((f32[2,40,256]{2,1,0:T(8,128)S(1)}, f32[2,40,256]{2,1,0:T(8,128)S(1)}, u32[]{:S(2)}, u32[]{:S(2)}) %collective-permute-start.3) | collective-permute-done | bytes 81952 | tf_op jit(solution)/shard_map/ppermute | solution.py:21
  72.3 0.1 shard_map.81
  72.5 0.7 copy.12
  73.2 0.7 copy.13
Async XLA Ops:
  1.6 2.6 %collective-permute-start.1 = (f32[256,72]{1,0:T(8,128)S(1)}, f32[256,72]{1,0:T(8,128)S(1)}, u32[]{:S(2)}, u32[]{:S(2)}) collective-permute-start(f32[256,72]{1,0:T(8,128)S(1)} %copy.11.text), channel_id=1, source_target_pairs={{0,16},{16,0},{1,17},{17,1},{2,18},{18,2},{3,19},{19,3},{4,20},{20... | collective-permute-start | bytes 221192 | tf_op jit(solution)/shard_map/ppermute | solution.py:21
  4.1 1.4 %collective-permute-start = (f32[256,72]{1,0:T(8,128)S(1)}, f32[256,72]{1,0:T(8,128)S(1)}, u32[]{:S(2)}, u32[]{:S(2)}) collective-permute-start(f32[256,72]{1,0:T(8,128)S(1)} %copy.10.image), channel_id=1, source_target_pairs={{0,16},{16,0},{1,17},{17,1},{2,18},{18,2},{3,19},{19,3},{4,20},{20... | collective-permute-start | bytes 221192 | tf_op jit(solution)/shard_map/ppermute | solution.py:21
  5.5 0.7 copy-start
  6.2 0.7 copy-start.1
  39.1 3.8 %collective-permute-start.2 = (f32[264,256]{1,0:T(8,128)S(1)}, f32[264,256]{1,0:T(8,128)S(1)}, u32[]{:S(2)}, u32[]{:S(2)}) collective-permute-start(f32[264,256]{1,0:T(8,128)S(1)} %shard_map.78.near), channel_id=1, source_target_pairs={{0,16},{16,0},{1,17},{17,1},{2,18},{18,2},{3,19},{19,3},{4,20},{20... | collective-permute-start | bytes 811016 | tf_op jit(solution)/shard_map/ppermute | solution.py:21
  68.8 3.5 %collective-permute-start.3 = (f32[2,40,256]{2,1,0:T(8,128)S(1)}, f32[2,40,256]{2,1,0:T(8,128)S(1)}, u32[]{:S(2)}, u32[]{:S(2)}) collective-permute-start(f32[2,40,256]{2,1,0:T(8,128)S(1)} %get-tuple-element.5), channel_id=1, source_target_pairs={{0,16},{16,0},{1,17},{17,1},{2,18},{18,2},{3,19},{19,3},{4,20},{20... | collective-permute-start | bytes 245768 | tf_op jit(solution)/shard_map/ppermute | solution.py:21

commit v2 on v1

v2 whole, which is shorter than its diff:
```python
import jax
import jax.numpy as jnp
from jax import lax
from jax.experimental import pallas as pl
from jax.experimental.pallas import tpu as pltpu
from jax.sharding import Mesh
from jax.sharding import PartitionSpec as P

EPSILON = 1e-06
F32 = jnp.float32
BF16 = jnp.bfloat16

HALF = 36
HELD = 40
ROWS = 256
PART = 64
PEERS = 64
PEER_AXES = ("x", "y", "z")


def peers_at(x):
    place = PEER_AXES.index("x")
    return [s for s in range(PEERS) if s // (16, 4, 1)[place] % 4 == x]


def other_core(x):
    return lax.ppermute(x, "c", [(0, 1), (1, 0)])


def halves(x):
    high = x.astype(BF16)
    return high, (x - high.astype(F32)).astype(BF16)


def product(first, second):
    a, b = halves(first)
    c, d = halves(second)

    def dot(p, q):
        return jnp.dot(p, q, preferred_element_type=F32)

    return dot(a, c) + (dot(a, d) + dot(b, c))


def near_kernel(image, text, image_owner, text_owner, out, held, owners, sems):
    core = lax.axis_index("c")
    copies = [
        pltpu.make_async_copy(src, dst, sems.at[i])
        for i, (src, dst) in enumerate(
            (
                (image, held.at[0]),
                (text, held.at[1]),
                (image_owner, owners.at[0]),
                (text_owner, owners.at[1]),
            )
        )
    ]
    for copy in copies:
        copy.start()
    for copy in copies:
        copy.wait()
    for k in range(2):
        out[k, :HALF] = jnp.where(core == 0, held[k, :HALF], held[k, HALF:])
        out[k, HALF:] = jnp.concatenate(
            [owners[k].astype(F32), jnp.zeros((HELD - HALF - 1, ROWS), F32)], axis=0
        )


def pack_kernel(near, image_far, text_far, out):
    core = lax.axis_index("c")

    def both(k, far):
        own = near[k]
        other = jnp.concatenate(
            [
                jnp.where(core == 0, far[:HALF], far[HALF:]),
                jnp.zeros((HELD - HALF, ROWS), F32),
            ],
            axis=0,
        )
        return jnp.concatenate(
            [jnp.where(core == 0, own, other), jnp.where(core == 0, other, own)], axis=1
        )

    images = both(0, image_far)
    texts = both(1, text_far)
    for i in range(8):
        for j in range(8):
            out[i * 8 + j] = jnp.concatenate(
                [images[:, i * PART : (i + 1) * PART], texts[:, j * PART : (j + 1) * PART]], axis=1
            )


def unpacked(pieces):
    row = lax.broadcasted_iota(jnp.int32, (HELD, 1), 0)
    blocks = [
        jnp.concatenate([jnp.where(row < HALF, pieces[s], 0.0) for s in peers_at(x)], axis=0)
        for x in range(4)
    ]
    image = jnp.concatenate([b[:, :PART] for b in blocks], axis=1)
    text = jnp.concatenate([b[:, PART:] for b in blocks], axis=1)
    return image, text


def gram_kernel(pieces, out):
    image, text = unpacked(pieces)
    out[:ROWS] = product(image.T, text)
    owners = [pieces[peers_at(x)[0], HALF : HALF + 1] for x in range(4)]
    out[ROWS : ROWS + 8] = jnp.concatenate(
        [
            jnp.sum(image * image, axis=0, keepdims=True),
            jnp.sum(text * text, axis=0, keepdims=True),
            jnp.concatenate([o[:, :PART] for o in owners], axis=1),
            jnp.concatenate([o[:, PART:] for o in owners], axis=1),
            jnp.zeros((4, ROWS), F32),
        ],
        axis=0,
    )


def grad_kernel(log_scale, bias, pieces, near, far, out):
    image, text = unpacked(pieces)
    scale = jnp.exp(jnp.full((1, 1), log_scale[0], F32))
    extra = near[ROWS:] + far[ROWS:]
    extra_turned = extra.T
    image_inv = lax.rsqrt(extra[0:1] + EPSILON)
    text_inv = lax.rsqrt(extra[1:2] + EPSILON)
    image_inv_col = lax.rsqrt(extra_turned[:, 0:1] + EPSILON)
    inv = image_inv_col * text_inv
    cosines = (near[:ROWS] + far[:ROWS]) * inv
    labels = jnp.where(extra_turned[:, 2:3] == extra[3:4], 1.0, -1.0)
    logits = scale * cosines + bias[0]
    grads = scale * (-labels * jax.nn.sigmoid(-labels * logits))
    weighted = grads * cosines
    text_dot = jnp.sum(weighted, axis=0, keepdims=True)
    image_dot = jnp.broadcast_to(jnp.sum(weighted, axis=1, keepdims=True), (ROWS, 128)).T[0:1]
    mixed = grads * inv
    image_grad = product(text, mixed.T) - image * (image_inv * image_inv * image_dot)
    text_grad = product(image, mixed) - text * (text_inv * text_inv * text_dot)
    for x in range(4):
        own = slice(x * PART, (x + 1) * PART)
        block = jnp.concatenate([image_grad[:, own], text_grad[:, own]], axis=1)
        for t, s in enumerate(peers_at(x)):
            for k in range(HALF // 4):
                out[s, k] = block[t * HELD + 4 * k : t * HELD + 4 * k + 4]


def sum_kernel(pieces, own, send):
    core = lax.axis_index("c")
    image_sums = [sum(pieces[i * 8 + j] for j in range(8)) for i in range(8)]
    text_sums = [sum(pieces[i * 8 + j] for i in range(8)) for j in range(8)]
    for k, sums, part in ((0, image_sums, slice(0, PART)), (1, text_sums, slice(PART, 2 * PART))):
        flat = [jnp.concatenate([s[q, :, part] for q in range(HALF // 4)], axis=0) for s in sums]
        low = jnp.concatenate(flat[:4], axis=1)
        high = jnp.concatenate(flat[4:], axis=1)
        own[k] = jnp.where(core == 0, low, high)
        send[k] = jnp.where(core == 0, high, low)


def finish_kernel(own, received, image_grad, text_grad):
    core = lax.axis_index("c")
    for k, out in ((0, image_grad), (1, text_grad)):
        low = jnp.where(core == 0, own[k], received[k])
        high = jnp.where(core == 0, received[k], own[k])
        out[...] = jnp.concatenate([low, high], axis=0)


def call(kernel, outs, args, scalars=0, **more):
    smem = [pl.BlockSpec(memory_space=pltpu.SMEM)] * scalars
    vmem = [pl.BlockSpec(memory_space=pltpu.VMEM)] * (len(args) - scalars)
    return pl.pallas_call(
        kernel,
        out_shape=[jax.ShapeDtypeStruct(s, F32) for s in outs],
        in_specs=more.pop("in_specs", smem + vmem),
        out_specs=[pl.BlockSpec(memory_space=pltpu.VMEM)] * len(outs),
        compiler_params=pltpu.CompilerParams(vmem_limit_bytes=40 * 1024 * 1024),
        **more,
    )(*args)


def local(image_emb, text_emb, image_owner, text_owner, log_scale, bias):
    image = image_emb.T
    text = text_emb.T
    image_far = other_core(image)
    text_far = other_core(text)
    (near,) = call(
        near_kernel,
        [(2, HELD, ROWS)],
        tuple(
            pltpu.with_memory_space_constraint(x, pltpu.HBM)
            for x in (image, text, image_owner.reshape(1, ROWS), text_owner.reshape(1, ROWS))
        ),
        in_specs=[pl.BlockSpec(memory_space=pltpu.HBM)] * 4,
        scratch_shapes=[
            pltpu.VMEM((2, 2 * HALF, ROWS), F32),
            pltpu.VMEM((2, 1, ROWS), jnp.int32),
            pltpu.SemaphoreType.DMA((4,)),
        ],
        cost_estimate=pl.CostEstimate(flops=0, bytes_accessed=230000, transcendentals=0),
    )
    (packed,) = call(pack_kernel, [(PEERS, HELD, 2 * PART)], (near, image_far, text_far))
    held = lax.all_to_all(packed, PEER_AXES, 0, 0, tiled=True)
    (partial,) = call(gram_kernel, [(ROWS + 8, ROWS)], (held,))
    (grads,) = call(
        grad_kernel,
        [(PEERS, HALF // 4, 4, 2 * PART)],
        (log_scale, bias, held, partial, other_core(partial)),
        scalars=2,
    )
    back = lax.all_to_all(grads, PEER_AXES, 0, 0, tiled=True)
    own, send = call(sum_kernel, [(2, HALF, ROWS)] * 2, (back,))
    image_grad, text_grad = call(finish_kernel, [(2 * HALF, ROWS)] * 2, (own, other_core(send)))
    return image_grad.T, text_grad.T


def solution(mesh):
    fine = Mesh(mesh.devices.reshape(4, 2, 4, 4), ("x", "c", "z", "y"))
    rows = P(("x", "c"))
    block = P(("x", "c"), ("z", "y"))
    return jax.shard_map(
        local,
        mesh=fine,
        in_specs=(block, block, rows, rows, P(), P()),
        out_specs=(block, block),
        check_vma=False,
    )
```

time: 74.2 us -> 68.2 us (0.919)
  local copies, waits for them, and re-layouts: 4.75 us -> 0 us
  blocking collectives: 55.1 us -> 53.2 us
  Pallas kernels: 3.07 us -> 4.42 us
  waiting for transfers between devices: 2.25 us -> 1.33 us
    unnamed x6 -> x0, local copies, waits for them, and re-layouts: 3.31 us -> none
    all_to_all x2, blocking collectives: 55.1 us -> 53.2 us  [the longest x1 30.8 us: local(): held = lax.all_to_all(packed, PEER_AXES, 0, 0, tiled=True)]
    pallas_call x2 -> x0, local copies, waits for them, and re-layouts: 1.44 us -> none  [call(): pl.pallas_call(kernel, out_shape=[jax.ShapeDtypeStruct(s, F32) for s in o...]
    pallas_call x5 -> x6, Pallas kernels: 3.07 us -> 4.42 us  [call(): pl.pallas_call(kernel, out_shape=[jax.ShapeDtypeStruct(s, F32) for s in o...]
    ppermute x4, waiting for transfers between devices: 2.25 us -> 1.33 us  [other_core(): return lax.ppermute(x, 'c', [(0, 1), (1, 0)])]
  transfers between devices with their start and end apart: 4 -> 4, of which waited for: 2 -> 3; matrix products, arithmetic and copies ran while one was open for 1% -> 0% of each run, Pallas kernels for 0% -> 1%
where the time goes in v2:
time: 68.2 us; the launch traced here: 68 us
  blocking collectives  53.2 us (78%)
  starting transfers between devices  7.04 us (10%)
  Pallas kernels  4.42 us (6%)
  between operations  1.97 us (3%)
  waiting for transfers between devices  1.33 us (2%)
    all_to_all x1, blocking collectives, local(): held = lax.all_to_all(packed, PEER_AXES, 0, 0, tiled=True)  30.8 us
    all_to_all x1, blocking collectives, local(): back = lax.all_to_all(grads, PEER_AXES, 0, 0, tiled=True)  22.4 us
    ppermute x4, starting transfers between devices, other_core(): return lax.ppermute(x, 'c', [(0, 1), (1, 0)])  7.04 us
    pallas_call x6, Pallas kernels, call(): pl.pallas_call(kernel, out_shape=[jax.ShapeDtypeStruct(s, F32) for s in o...  4.42 us
  transfers between devices with their start and end apart: 4, of which 3 were waited for; matrix products, arithmetic and copies ran while one was open for 0% of the time, Pallas kernels for 1%

profile of v2, /device:TPU:1, one launch (start us, length us, event | category | flops | bytes accessed | tf_op | source)
XLA Modules:
  0.0 68.0 jit_solution(6986173181962863022)
XLA Ops:
  0.6 1.5 %collective-permute-start = (f32[72,256]{1,0:T(8,128)}, f32[72,256]{1,0:T(8,128)S(1)}, u32[]{:S(2)}, u32[]{:S(2)}) collective-permute-start(f32[72,256]{1,0:T(8,128)} %bitcast.6), channel_id=1, source_target_pairs={{0,16},{16,0},{1,17},{17,1},{2,18},{18,2},{3,19},{19,3},{4,20},{20... | collective-permute-start | bytes 221192 | tf_op jit(solution)/shard_map/ppermute | solution.py:27
  2.1 0.1 collective-permute-start.1
  2.2 1.0 %shard_map.77.near = f32[2,40,256]{2,1,0:T(8,128)S(1)} custom-call(f32[72,256]{1,0:T(8,128)} %bitcast.7, f32[72,256]{1,0:T(8,128)} %bitcast.9, s32[1,256]{1,0:T(1,128)} %bitcast.10, s32[1,256]{1,0:T(1,128)} %bitcast.11), custom_call_target="tpu_custom_call" | custom-call | bytes 230000 | tf_op jit(solution)/shard_map/pallas_call | solution.py:171
  3.2 0.1 collective-permute-done.image_far
  3.3 0.4 collective-permute-done.1.text_far
  3.6 0.1 shard_map.78
  3.8 30.8 %all_to_all.10.pieces = f32[64,40,128]{2,1,0:T(8,128)S(1)} all-to-all(f32[64,40,128]{2,1,0:T(8,128)S(1)} %shard_map.78), channel_id=1, replica_groups=mesh['x'=4,'c'=2,'z'=4,'y'=4] {'x','y','z'}, dimensions={0} | all-to-all | bytes 2621440 | tf_op jit(solution)/shard_map/all_to_all | solution.py:202
  34.6 0.9 %shard_map.79.near = f32[264,256]{1,0:T(8,128)S(1)} custom-call(f32[64,40,128]{2,1,0:T(8,128)S(1)} %all_to_all.10.pieces), custom_call_target="tpu_custom_call" | custom-call | tf_op jit(solution)/shard_map/pallas_call | solution.py:171
  35.5 2.7 %collective-permute-start.2 = (f32[264,256]{1,0:T(8,128)S(1)}, f32[264,256]{1,0:T(8,128)S(1)}, u32[]{:S(2)}, u32[]{:S(2)}) collective-permute-start(f32[264,256]{1,0:T(8,128)S(1)} %shard_map.79.near), channel_id=1, source_target_pairs={{0,16},{16,0},{1,17},{17,1},{2,18},{18,2},{3,19},{19,3},{4,20},{20... | collective-permute-start | bytes 811016 | tf_op jit(solution)/shard_map/ppermute | solution.py:27
  39.5 0.0 collective-permute-done.2.far
  39.5 1.5 %shard_map.80 = f32[64,9,4,128]{3,2,1,0:T(4,128)S(1)} custom-call(f32[1]{0:T(128)S(6)} %copy.8.log_scale, f32[1]{0:T(128)S(6)} %copy.9.bias, f32[64,40,128]{2,1,0:T(8,128)S(1)} %all_to_all.10.pieces, f32[264,256]{1,0:T(8,128)S(1)} %shard_map.79.near, f32[264,256]{1,0:T(8,128)S(1)} %collective-permute-done.2.far), custom_call_target="tpu_custom_call" | custom-call | tf_op jit(solution)/shard_map/pallas_call | solution.py:171
  41.0 22.4 %all_to_all.11.pieces = f32[64,9,4,128]{3,2,1,0:T(4,128)S(1)} all-to-all(f32[64,9,4,128]{3,2,1,0:T(4,128)S(1)} %shard_map.80), channel_id=1, replica_groups=mesh['x'=4,'c'=2,'z'=4,'y'=4] {'x','y','z'}, dimensions={0} | all-to-all | bytes 2359296 | tf_op jit(solution)/shard_map/all_to_all | solution.py:210
  63.4 0.2 shard_map.81
  63.7 2.7 %collective-permute-start.3 = (f32[2,36,256]{2,1,0:T(8,128)S(1)}, f32[2,36,256]{2,1,0:T(8,128)S(1)}, u32[]{:S(2)}, u32[]{:S(2)}) collective-permute-start(f32[2,36,256]{2,1,0:T(8,128)S(1)} %get-tuple-element.7), channel_id=1, source_target_pairs={{0,16},{16,0},{1,17},{17,1},{2,18},{18,2},{3,19},{19,3},{4,20},{20... | collective-permute-start | bytes 221192 | tf_op jit(solution)/shard_map/ppermute | solution.py:27
  66.4 0.9 %collective-permute-done.3.received = f32[2,36,256]{2,1,0:T(8,128)S(1)} collective-permute-done((f32[2,36,256]{2,1,0:T(8,128)S(1)}, f32[2,36,256]{2,1,0:T(8,128)S(1)}, u32[]{:S(2)}, u32[]{:S(2)}) %collective-permute-start.3) | collective-permute-done | bytes 73760 | tf_op jit(solution)/shard_map/ppermute | solution.py:27
  67.3 0.7 shard_map.82
Async XLA Ops:
  0.6 2.6 %collective-permute-start = (f32[72,256]{1,0:T(8,128)}, f32[72,256]{1,0:T(8,128)S(1)}, u32[]{:S(2)}, u32[]{:S(2)}) collective-permute-start(f32[72,256]{1,0:T(8,128)} %bitcast.6), channel_id=1, source_target_pairs={{0,16},{16,0},{1,17},{17,1},{2,18},{18,2},{3,19},{19,3},{4,20},{20... | collective-permute-start | bytes 221192 | tf_op jit(solution)/shard_map/ppermute | solution.py:27
  2.1 1.5 %collective-permute-start.1 = (f32[72,256]{1,0:T(8,128)}, f32[72,256]{1,0:T(8,128)S(1)}, u32[]{:S(2)}, u32[]{:S(2)}) collective-permute-start(f32[72,256]{1,0:T(8,128)} %bitcast.8), channel_id=1, source_target_pairs={{0,16},{16,0},{1,17},{17,1},{2,18},{18,2},{3,19},{19,3},{4,20},{20... | collective-permute-start | bytes 221192 | tf_op jit(solution)/shard_map/ppermute | solution.py:27
  35.5 4.0 %collective-permute-start.2 = (f32[264,256]{1,0:T(8,128)S(1)}, f32[264,256]{1,0:T(8,128)S(1)}, u32[]{:S(2)}, u32[]{:S(2)}) collective-permute-start(f32[264,256]{1,0:T(8,128)S(1)} %shard_map.79.near), channel_id=1, source_target_pairs={{0,16},{16,0},{1,17},{17,1},{2,18},{18,2},{3,19},{19,3},{4,20},{20... | collective-permute-start | bytes 811016 | tf_op jit(solution)/shard_map/ppermute | solution.py:27
  63.7 3.7 %collective-permute-start.3 = (f32[2,36,256]{2,1,0:T(8,128)S(1)}, f32[2,36,256]{2,1,0:T(8,128)S(1)}, u32[]{:S(2)}, u32[]{:S(2)}) collective-permute-start(f32[2,36,256]{2,1,0:T(8,128)S(1)} %get-tuple-element.7), channel_id=1, source_target_pairs={{0,16},{16,0},{1,17},{17,1},{2,18},{18,2},{3,19},{19,3},{4,20},{20... | collective-permute-start | bytes 221192 | tf_op jit(solution)/shard_map/ppermute | solution.py:27

commit v3 on v2

--- a/solution.py
+++ b/solution.py
@@ -15,12 +15,38 @@
 ROWS = 256
 PART = 64
 PEERS = 64
-PEER_AXES = ("x", "y", "z")
-
-
-def peers_at(x):
-    place = PEER_AXES.index("x")
-    return [s for s in range(PEERS) if s // (16, 4, 1)[place] % 4 == x]
+
+def spread(x, z, y):
+    high = (x // 2) * 4 + (y // 2) * 2 + z // 2
+    low = (x % 2) * 4 + (y % 2) * 2 + z % 2
+    return high * 8 + low
+
+
+CHIPS = [(x, z, y) for x in range(4) for z in range(4) for y in range(4)]
+SPOTS = [spread(*chip) for chip in CHIPS]
+OPPOSITE = spread(2, 2, 2)
+AXES = ("x", "c", "z", "y")
+
+
+def peer_groups():
+    at_spot = [CHIPS[SPOTS.index(s)] for s in range(PEERS)]
+    return [
+        [
+            ((x * 2 + core) * 4 + z) * 4 + y
+            for x, z, y in (at_spot[s ^ (core * OPPOSITE)] for s in range(PEERS))
+        ]
+        for core in range(2)
+    ]
+
+
+def exchange(pieces):
+    return lax.all_to_all(
+        pieces, AXES, 0, 0, axis_index_groups=peer_groups(), tiled=True
+    )
+
+
+def spot_of(chip, core):
+    return SPOTS[chip] ^ (core * OPPOSITE)
 
 
 def other_core(x):
@@ -86,15 +112,19 @@
     texts = both(1, text_far)
     for i in range(8):
         for j in range(8):
-            out[i * 8 + j] = jnp.concatenate(
+            out[spot_of(i * 8 + j, core)] = jnp.concatenate(
                 [images[:, i * PART : (i + 1) * PART], texts[:, j * PART : (j + 1) * PART]], axis=1
             )
 
 
 def unpacked(pieces):
+    core = lax.axis_index("c")
     row = lax.broadcasted_iota(jnp.int32, (HELD, 1), 0)
     blocks = [
-        jnp.concatenate([jnp.where(row < HALF, pieces[s], 0.0) for s in peers_at(x)], axis=0)
+        jnp.concatenate(
+            [jnp.where(row < HALF, pieces[spot_of(x * 16 + t, core)], 0.0) for t in range(16)],
+            axis=0,
+        )
         for x in range(4)
     ]
     image = jnp.concatenate([b[:, :PART] for b in blocks], axis=1)
@@ -103,9 +133,10 @@
 
 
 def gram_kernel(pieces, out):
+    core = lax.axis_index("c")
     image, text = unpacked(pieces)
     out[:ROWS] = product(image.T, text)
-    owners = [pieces[peers_at(x)[0], HALF : HALF + 1] for x in range(4)]
+    owners = [pieces[spot_of(x * 16, core)][HALF : HALF + 1] for x in range(4)]
     out[ROWS : ROWS + 8] = jnp.concatenate(
         [
             jnp.sum(image * image, axis=0, keepdims=True),
@@ -119,6 +150,7 @@
 
 
 def grad_kernel(log_scale, bias, pieces, near, far, out):
+    core = lax.axis_index("c")
     image, text = unpacked(pieces)
     scale = jnp.exp(jnp.full((1, 1), log_scale[0], F32))
     extra = near[ROWS:] + far[ROWS:]
@@ -140,15 +172,17 @@
     for x in range(4):
         own = slice(x * PART, (x + 1) * PART)
         block = jnp.concatenate([image_grad[:, own], text_grad[:, own]], axis=1)
-        for t, s in enumerate(peers_at(x)):
+        for t in range(16):
+            spot = spot_of(x * 16 + t, core)
             for k in range(HALF // 4):
-                out[s, k] = block[t * HELD + 4 * k : t * HELD + 4 * k + 4]
+                out[spot, k] = block[t * HELD + 4 * k : t * HELD + 4 * k + 4]
 
 
 def sum_kernel(pieces, own, send):
     core = lax.axis_index("c")
-    image_sums = [sum(pieces[i * 8 + j] for j in range(8)) for i in range(8)]
-    text_sums = [sum(pieces[i * 8 + j] for i in range(8)) for j in range(8)]
+    held = [[pieces[spot_of(i * 8 + j, core)] for j in range(8)] for i in range(8)]
+    image_sums = [sum(held[i][j] for j in range(8)) for i in range(8)]
+    text_sums = [sum(held[i][j] for i in range(8)) for j in range(8)]
     for k, sums, part in ((0, image_sums, slice(0, PART)), (1, text_sums, slice(PART, 2 * PART))):
         flat = [jnp.concatenate([s[q, :, part] for q in range(HALF // 4)], axis=0) for s in sums]
         low = jnp.concatenate(flat[:4], axis=1)
@@ -199,7 +233,7 @@
         cost_estimate=pl.CostEstimate(flops=0, bytes_accessed=230000, transcendentals=0),
     )
     (packed,) = call(pack_kernel, [(PEERS, HELD, 2 * PART)], (near, image_far, text_far))
-    held = lax.all_to_all(packed, PEER_AXES, 0, 0, tiled=True)
+    held = exchange(packed)
     (partial,) = call(gram_kernel, [(ROWS + 8, ROWS)], (held,))
     (grads,) = call(
         grad_kernel,
@@ -207,7 +241,7 @@
         (log_scale, bias, held, partial, other_core(partial)),
         scalars=2,
     )
-    back = lax.all_to_all(grads, PEER_AXES, 0, 0, tiled=True)
+    back = exchange(grads)
     own, send = call(sum_kernel, [(2, HALF, ROWS)] * 2, (back,))
     image_grad, text_grad = call(finish_kernel, [(2 * HALF, ROWS)] * 2, (own, other_core(send)))
     return image_grad.T, text_grad.T

time: 68.2 us -> 63.7 us (0.934)
  starting transfers between devices: 7.04 us -> 4.15 us
  blocking collectives: 53.2 us -> 51.4 us
    ppermute x4, starting transfers between devices: 7.04 us -> 4.15 us  [other_core(): return lax.ppermute(x, 'c', [(0, 1), (1, 0)])]
    all_to_all x2, blocking collectives: 53.2 us -> 51.4 us  [exchange(): lax.all_to_all(pieces, AXES, 0, 0, axis_index_groups=peer_groups(), tiled...]
  transfers between devices with their start and end apart: 4 -> 4, of which waited for: 3 -> 3; matrix products, arithmetic and copies ran while one was open for 0% -> 0% of each run, Pallas kernels for 1% -> 2%
where the time goes in v3:
time: 63.7 us; the launch traced here: 63.4 us
  blocking collectives  51.4 us (81%)
  Pallas kernels  4.58 us (7%)
  starting transfers between devices  4.15 us (7%)
  between operations  1.98 us (3%)
  waiting for transfers between devices  1.33 us (2%)
    all_to_all x2, blocking collectives, exchange(): lax.all_to_all(pieces, AXES, 0, 0, axis_index_groups=peer_groups(), tiled...  51.4 us
    pallas_call x6, Pallas kernels, call(): pl.pallas_call(kernel, out_shape=[jax.ShapeDtypeStruct(s, F32) for s in o...  4.58 us
    ppermute x4, starting transfers between devices, other_core(): return lax.ppermute(x, 'c', [(0, 1), (1, 0)])  4.15 us
    ppermute x4, waiting for transfers between devices, other_core(): return lax.ppermute(x, 'c', [(0, 1), (1, 0)])  1.33 us
  transfers between devices with their start and end apart: 4, of which 3 were waited for; matrix products, arithmetic and copies ran while one was open for 0% of the time, Pallas kernels for 2%

profile of v3, /device:TPU:1, one launch (start us, length us, event | category | flops | bytes accessed | tf_op | source)
XLA Modules:
  0.0 63.4 jit_solution(11937805658582688585)
XLA Ops:
  0.6 1.5 %collective-permute-start = (f32[72,256]{1,0:T(8,128)}, f32[72,256]{1,0:T(8,128)S(1)}, u32[]{:S(2)}, u32[]{:S(2)}) collective-permute-start(f32[72,256]{1,0:T(8,128)} %bitcast.6), channel_id=1, source_target_pairs={{0,16},{16,0},{1,17},{17,1},{2,18},{18,2},{3,19},{19,3},{4,20},{20... | collective-permute-start | bytes 221192 | tf_op jit(solution)/shard_map/ppermute | solution.py:53
  2.1 0.1 collective-permute-start.1
  2.2 1.0 %shard_map.77.near = f32[2,40,256]{2,1,0:T(8,128)S(1)} custom-call(f32[72,256]{1,0:T(8,128)} %bitcast.7, f32[72,256]{1,0:T(8,128)} %bitcast.9, s32[1,256]{1,0:T(1,128)} %bitcast.10, s32[1,256]{1,0:T(1,128)} %bitcast.11), custom_call_target="tpu_custom_call" | custom-call | bytes 230000 | tf_op jit(solution)/shard_map/pallas_call | solution.py:205
  3.2 0.1 collective-permute-done.image_far
  3.3 0.4 collective-permute-done.1.text_far
  3.6 0.2 shard_map.78
  3.8 27.7 %all_to_all.10.pieces = f32[64,40,128]{2,1,0:T(8,128)S(1)} all-to-all(f32[64,40,128]{2,1,0:T(8,128)S(1)} %shard_map.78), channel_id=1, replica_groups={{0,4,1,5,32,36,33,37,8,12,9,13,40,44,41,45,2,6,3,7,34,38,35,39,10,14,11..., dimensions={0} | all-to-all | bytes 2621440 | tf_op jit(solution)/shard_map/all_to_all | solution.py:43
  31.5 0.9 %shard_map.79.near = f32[264,256]{1,0:T(8,128)S(1)} custom-call(f32[64,40,128]{2,1,0:T(8,128)S(1)} %all_to_all.10.pieces), custom_call_target="tpu_custom_call" | custom-call | tf_op jit(solution)/shard_map/pallas_call | solution.py:205
  32.4 1.3 %collective-permute-start.2 = (f32[264,256]{1,0:T(8,128)S(1)}, f32[264,256]{1,0:T(8,128)S(1)}, u32[]{:S(2)}, u32[]{:S(2)}) collective-permute-start(f32[264,256]{1,0:T(8,128)S(1)} %shard_map.79.near), channel_id=1, source_target_pairs={{0,16},{16,0},{1,17},{17,1},{2,18},{18,2},{3,19},{19,3},{4,20},{20... | collective-permute-start | bytes 811016 | tf_op jit(solution)/shard_map/ppermute | solution.py:53
  35.1 0.0 collective-permute-done.2.far
  35.1 1.5 %shard_map.80 = f32[64,9,4,128]{3,2,1,0:T(4,128)S(1)} custom-call(f32[1]{0:T(128)S(6)} %copy.8.log_scale, f32[1]{0:T(128)S(6)} %copy.9.bias, f32[64,40,128]{2,1,0:T(8,128)S(1)} %all_to_all.10.pieces, f32[264,256]{1,0:T(8,128)S(1)} %shard_map.79.near, f32[264,256]{1,0:T(8,128)S(1)} %collective-permute-done.2.far), custom_call_target="tpu_custom_call" | custom-call | tf_op jit(solution)/shard_map/pallas_call | solution.py:205
  36.6 23.7 %all_to_all.11.pieces = f32[64,9,4,128]{3,2,1,0:T(4,128)S(1)} all-to-all(f32[64,9,4,128]{3,2,1,0:T(4,128)S(1)} %shard_map.80), channel_id=1, replica_groups={{0,4,1,5,32,36,33,37,8,12,9,13,40,44,41,45,2,6,3,7,34,38,35,39,10,14,11..., dimensions={0} | all-to-all | bytes 2359296 | tf_op jit(solution)/shard_map/all_to_all | solution.py:43
  60.3 0.3 shard_map.81
  60.6 1.2 %collective-permute-start.3 = (f32[2,36,256]{2,1,0:T(8,128)S(1)}, f32[2,36,256]{2,1,0:T(8,128)S(1)}, u32[]{:S(2)}, u32[]{:S(2)}) collective-permute-start(f32[2,36,256]{2,1,0:T(8,128)S(1)} %get-tuple-element.7), channel_id=1, source_target_pairs={{0,16},{16,0},{1,17},{17,1},{2,18},{18,2},{3,19},{19,3},{4,20},{20... | collective-permute-start | bytes 221192 | tf_op jit(solution)/shard_map/ppermute | solution.py:53
  61.8 0.9 %collective-permute-done.3.received = f32[2,36,256]{2,1,0:T(8,128)S(1)} collective-permute-done((f32[2,36,256]{2,1,0:T(8,128)S(1)}, f32[2,36,256]{2,1,0:T(8,128)S(1)}, u32[]{:S(2)}, u32[]{:S(2)}) %collective-permute-start.3) | collective-permute-done | bytes 73760 | tf_op jit(solution)/shard_map/ppermute | solution.py:53
  62.7 0.7 %shard_map.82 = (f32[72,256]{1,0:T(8,128)}, f32[72,256]{1,0:T(8,128)}) custom-call(f32[2,36,256]{2,1,0:T(8,128)S(1)} %get-tuple-element.6.own, f32[2,36,256]{2,1,0:T(8,128)S(1)} %collective-permute-done.3.received), custom_call_target="tpu_custom_call" | custom-call | tf_op jit(solution)/shard_map/pallas_call | solution.py:205
Async XLA Ops:
  0.6 2.6 %collective-permute-start = (f32[72,256]{1,0:T(8,128)}, f32[72,256]{1,0:T(8,128)S(1)}, u32[]{:S(2)}, u32[]{:S(2)}) collective-permute-start(f32[72,256]{1,0:T(8,128)} %bitcast.6), channel_id=1, source_target_pairs={{0,16},{16,0},{1,17},{17,1},{2,18},{18,2},{3,19},{19,3},{4,20},{20... | collective-permute-start | bytes 221192 | tf_op jit(solution)/shard_map/ppermute | solution.py:53
  2.1 1.5 %collective-permute-start.1 = (f32[72,256]{1,0:T(8,128)}, f32[72,256]{1,0:T(8,128)S(1)}, u32[]{:S(2)}, u32[]{:S(2)}) collective-permute-start(f32[72,256]{1,0:T(8,128)} %bitcast.8), channel_id=1, source_target_pairs={{0,16},{16,0},{1,17},{17,1},{2,18},{18,2},{3,19},{19,3},{4,20},{20... | collective-permute-start | bytes 221192 | tf_op jit(solution)/shard_map/ppermute | solution.py:53
  32.4 2.6 %collective-permute-start.2 = (f32[264,256]{1,0:T(8,128)S(1)}, f32[264,256]{1,0:T(8,128)S(1)}, u32[]{:S(2)}, u32[]{:S(2)}) collective-permute-start(f32[264,256]{1,0:T(8,128)S(1)} %shard_map.79.near), channel_id=1, source_target_pairs={{0,16},{16,0},{1,17},{17,1},{2,18},{18,2},{3,19},{19,3},{4,20},{20... | collective-permute-start | bytes 811016 | tf_op jit(solution)/shard_map/ppermute | solution.py:53
  60.6 2.1 %collective-permute-start.3 = (f32[2,36,256]{2,1,0:T(8,128)S(1)}, f32[2,36,256]{2,1,0:T(8,128)S(1)}, u32[]{:S(2)}, u32[]{:S(2)}) collective-permute-start(f32[2,36,256]{2,1,0:T(8,128)S(1)} %get-tuple-element.7), channel_id=1, source_target_pairs={{0,16},{16,0},{1,17},{17,1},{2,18},{18,2},{3,19},{19,3},{4,20},{20... | collective-permute-start | bytes 221192 | tf_op jit(solution)/shard_map/ppermute | solution.py:53

commit v4 on v2

v4 whole, which is shorter than its diff:
```python
import jax
import jax.numpy as jnp
from jax import lax
from jax.experimental import pallas as pl
from jax.experimental.pallas import tpu as pltpu
from jax.sharding import Mesh
from jax.sharding import PartitionSpec as P

EPSILON = 1e-06
F32 = jnp.float32
BF16 = jnp.bfloat16

HALF = 36
PIECE = 37
ROWS = 256
PART = 64
PEERS = 64
BLOCK = 16 * PIECE
BACK = 16 * HALF

AXES = ("x", "c", "z", "y")
OPPOSITE = 42


def peer_groups():
    groups = []
    for core in range(2):
        chips = [p ^ (core * OPPOSITE) for p in range(PEERS)]
        groups.append([(q // 16 * 2 + core) * 16 + q % 16 for q in chips])
    return groups


def exchange(pieces):
    rows = pieces.shape[0] // PEERS
    held = lax.all_to_all(
        pieces.reshape(PEERS, rows, 1, 2 * PART),
        AXES,
        0,
        0,
        axis_index_groups=peer_groups(),
        tiled=True,
    )
    return held.reshape(pieces.shape)


def sets(x, order):
    return jnp.concatenate([x[:, k * PART : (k + 1) * PART] for k in order], axis=1)


def other_core(x):
    return lax.ppermute(x, "c", [(0, 1), (1, 0)])


def halves(x):
    high = x.astype(BF16)
    return high, (x - high.astype(F32)).astype(BF16)


def joined(x, axis, left):
    high, low = halves(x)
    return jnp.concatenate([high, high, low] if left else [high, low, high], axis=axis)


def product(first, second, axis):
    dims = (((axis,), (0,)), ((), ()))
    return lax.dot_general(
        joined(first, axis, True), joined(second, 0, False), dims, preferred_element_type=F32
    )


def near_kernel(image, text, image_owner, text_owner, out, held, owners, sems):
    core = lax.axis_index("c")
    copies = [
        pltpu.make_async_copy(src, dst, sems.at[i])
        for i, (src, dst) in enumerate(
            (
                (image, held.at[0]),
                (text, held.at[1]),
                (image_owner, owners.at[0]),
                (text_owner, owners.at[1]),
            )
        )
    ]
    for copy in copies:
        copy.start()
    for copy in copies:
        copy.wait()
    for k in range(2):
        out[k, :HALF] = jnp.where(core == 0, held[k, :HALF], held[k, HALF:])
        out[k, HALF:] = owners[k].astype(F32)


def pack_kernel(near, image_far, text_far, out):
    core = lax.axis_index("c")

    def other(far):
        half = jnp.where(core == 0, far[:HALF], far[HALF:])
        return jnp.concatenate([half, jnp.zeros((1, ROWS), F32)], axis=0)

    images = jnp.concatenate([near[0], other(image_far)], axis=1)
    images = jnp.where(core == 0, images, sets(images, (1, 0, 3, 2, 5, 4, 7, 6)))
    texts = jnp.concatenate([near[1], other(text_far)], axis=1)
    texts = jnp.where(core == 0, texts, sets(texts, (6, 7, 4, 5, 2, 3, 0, 1)))
    for p in range(PEERS):
        a, b = p // 8, p % 8
        out[p * PIECE : (p + 1) * PIECE] = jnp.concatenate(
            [images[:, a * PART : (a + 1) * PART], texts[:, b * PART : (b + 1) * PART]], axis=1
        )


def block_of(x, core, size):
    return pl.ds(pl.multiple_of((x ^ (2 * core)) * size, 8), size)


def unpacked(pieces):
    core = lax.axis_index("c")
    row = lax.broadcasted_iota(jnp.int32, (BLOCK, 2 * PART), 0)
    owner = row - PIECE * ((row * 1772) >> 16) == HALF
    blocks = [jnp.where(owner, 0.0, pieces[block_of(x, core, BLOCK)]) for x in range(4)]
    image = jnp.concatenate([b[:, :PART] for b in blocks], axis=1)
    text = jnp.concatenate([b[:, PART:] for b in blocks], axis=1)
    return image, text


def gram_kernel(pieces, out):
    core = lax.axis_index("c")
    image, text = unpacked(pieces)
    out[:ROWS] = product(image, text, 0)
    owners = [pieces[block_of(x, core, BLOCK)][HALF : HALF + 1] for x in range(4)]
    out[ROWS : ROWS + 8] = jnp.concatenate(
        [
            jnp.sum(image * image, axis=0, keepdims=True),
            jnp.sum(text * text, axis=0, keepdims=True),
            jnp.concatenate([o[:, :PART] for o in owners], axis=1),
            jnp.concatenate([o[:, PART:] for o in owners], axis=1),
            jnp.zeros((4, ROWS), F32),
        ],
        axis=0,
    )


def grad_kernel(log_scale, bias, pieces, near, far, out):
    core = lax.axis_index("c")
    image, text = unpacked(pieces)
    scale = jnp.exp(jnp.full((1, 1), log_scale[0], F32))
    extra = near[ROWS:] + far[ROWS:]
    extra_turned = extra.T
    image_inv = lax.rsqrt(extra[0:1] + EPSILON)
    text_inv = lax.rsqrt(extra[1:2] + EPSILON)
    image_inv_col = lax.rsqrt(extra_turned[:, 0:1] + EPSILON)
    inv = image_inv_col * text_inv
    cosines = (near[:ROWS] + far[:ROWS]) * inv
    labels = jnp.where(extra_turned[:, 2:3] == extra[3:4], 1.0, -1.0)
    logits = scale * cosines + bias[0]
    grads = scale * (-labels * jax.nn.sigmoid(-labels * logits))
    weighted = grads * cosines
    text_dot = jnp.sum(weighted, axis=0, keepdims=True)
    image_dot = jnp.broadcast_to(jnp.sum(weighted, axis=1, keepdims=True), (ROWS, 128)).T[0:1]
    mixed = grads * inv
    image_grad = product(text, mixed.T, 1) - image * (image_inv * image_inv * image_dot)
    text_grad = product(image, mixed, 1) - text * (text_inv * text_inv * text_dot)
    for x in range(4):
        own = slice(x * PART, (x + 1) * PART)
        block = jnp.concatenate([image_grad[:, own], text_grad[:, own]], axis=1)
        out[block_of(x, core, BACK)] = jnp.concatenate(
            [block[t * PIECE : t * PIECE + HALF] for t in range(16)], axis=0
        )


def sum_kernel(pieces, own, send):
    core = lax.axis_index("c")
    pair = 2 * HALF

    def at(a, k):
        first = (a * 4 + k) * pair
        return pieces[first : first + pair]

    images = []
    for a in range(8):
        total = sum(at(a, k) for k in range(4))
        images.append((total[:HALF] + total[HALF:])[:, :PART])
    texts = []
    for k in range(4):
        total = sum(at(a, k) for a in range(8))
        texts += [total[:HALF, PART:], total[HALF:, PART:]]

    def order(parts, first, second):
        return jnp.where(
            core == 0,
            jnp.concatenate([parts[k] for k in first], axis=1),
            jnp.concatenate([parts[k] for k in second], axis=1),
        )

    own[0] = order(images, (0, 1, 2, 3), (1, 0, 3, 2))
    send[0] = order(images, (4, 5, 6, 7), (5, 4, 7, 6))
    own[1] = order(texts, (0, 1, 2, 3), (6, 7, 4, 5))
    send[1] = order(texts, (4, 5, 6, 7), (2, 3, 0, 1))


def finish_kernel(own, received, image_grad, text_grad):
    core = lax.axis_index("c")
    for k, out in ((0, image_grad), (1, text_grad)):
        low = jnp.where(core == 0, own[k], received[k])
        high = jnp.where(core == 0, received[k], own[k])
        out[...] = jnp.concatenate([low, high], axis=0)


def call(kernel, outs, args, scalars=0, **more):
    smem = [pl.BlockSpec(memory_space=pltpu.SMEM)] * scalars
    vmem = [pl.BlockSpec(memory_space=pltpu.VMEM)] * (len(args) - scalars)
    return pl.pallas_call(
        kernel,
        out_shape=[jax.ShapeDtypeStruct(s, F32) for s in outs],
        in_specs=more.pop("in_specs", smem + vmem),
        out_specs=[pl.BlockSpec(memory_space=pltpu.VMEM)] * len(outs),
        compiler_params=pltpu.CompilerParams(vmem_limit_bytes=40 * 1024 * 1024),
        **more,
    )(*args)


def local(image_emb, text_emb, image_owner, text_owner, log_scale, bias):
    image = image_emb.T
    text = text_emb.T
    image_far = other_core(image)
    text_far = other_core(text)
    (near,) = call(
        near_kernel,
        [(2, PIECE, ROWS)],
        tuple(
            pltpu.with_memory_space_constraint(x, pltpu.HBM)
            for x in (image, text, image_owner.reshape(1, ROWS), text_owner.reshape(1, ROWS))
        ),
        in_specs=[pl.BlockSpec(memory_space=pltpu.HBM)] * 4,
        scratch_shapes=[
            pltpu.VMEM((2, 2 * HALF, ROWS), F32),
            pltpu.VMEM((2, 1, ROWS), jnp.int32),
            pltpu.SemaphoreType.DMA((4,)),
        ],
        cost_estimate=pl.CostEstimate(flops=0, bytes_accessed=230000, transcendentals=0),
    )
    (packed,) = call(pack_kernel, [(PEERS * PIECE, 2 * PART)], (near, image_far, text_far))
    held = exchange(packed)
    (partial,) = call(gram_kernel, [(ROWS + 8, ROWS)], (held,))
    (grads,) = call(
        grad_kernel,
        [(PEERS * HALF, 2 * PART)],
        (log_scale, bias, held, partial, other_core(partial)),
        scalars=2,
    )
    back = exchange(grads)
    own, send = call(sum_kernel, [(2, HALF, ROWS)] * 2, (back,))
    image_grad, text_grad = call(finish_kernel, [(2 * HALF, ROWS)] * 2, (own, other_core(send)))
    return image_grad.T, text_grad.T


def solution(mesh):
    fine = Mesh(mesh.devices.reshape(4, 2, 4, 4), ("x", "c", "z", "y"))
    rows = P(("x", "c"))
    block = P(("x", "c"), ("z", "y"))
    return jax.shard_map(
        local,
        mesh=fine,
        in_specs=(block, block, rows, rows, P(), P()),
        out_specs=(block, block),
        check_vma=False,
    )
```

time: 68.2 us -> 62.7 us (0.919)
  blocking collectives: 53.2 us -> 50.3 us
  starting transfers between devices: 7.04 us -> 4.54 us
    all_to_all x2, blocking collectives: 53.2 us -> 50.3 us  [exchange(): lax.all_to_all(pieces.reshape(PEERS, rows, 1, 2 * PART), AXES, 0, 0, axis...]
    ppermute x4, starting transfers between devices: 7.04 us -> 4.54 us  [other_core(): return lax.ppermute(x, 'c', [(0, 1), (1, 0)])]
  transfers between devices with their start and end apart: 4 -> 4, of which waited for: 3 -> 3; matrix products, arithmetic and copies ran while one was open for 0% -> 0% of each run, Pallas kernels for 1% -> 2%
where the time goes in v4:
time: 62.7 us; the launch traced here: 62.4 us
  blocking collectives  50.3 us (80%)
  starting transfers between devices  4.54 us (7%)
  Pallas kernels  4.26 us (7%)
  between operations  1.98 us (3%)
  waiting for transfers between devices  1.33 us (2%)
    all_to_all x2, blocking collectives, exchange(): lax.all_to_all(pieces.reshape(PEERS, rows, 1, 2 * PART), AXES, 0, 0, axis...  50.3 us
    ppermute x4, starting transfers between devices, other_core(): return lax.ppermute(x, 'c', [(0, 1), (1, 0)])  4.54 us
    pallas_call x6, Pallas kernels, call(): pl.pallas_call(kernel, out_shape=[jax.ShapeDtypeStruct(s, F32) for s in o...  4.26 us
    ppermute x4, waiting for transfers between devices, other_core(): return lax.ppermute(x, 'c', [(0, 1), (1, 0)])  1.33 us
  transfers between devices with their start and end apart: 4, of which 3 were waited for; matrix products, arithmetic and copies ran while one was open for 0% of the time, Pallas kernels for 2%

profile of v4, /device:TPU:1, one launch (start us, length us, event | category | flops | bytes accessed | tf_op | source)
XLA Modules:
  0.0 62.4 jit_solution(5949365555715482592)
XLA Ops:
  0.6 1.5 %collective-permute-start = (f32[72,256]{1,0:T(8,128)}, f32[72,256]{1,0:T(8,128)S(1)}, u32[]{:S(2)}, u32[]{:S(2)}) collective-permute-start(f32[72,256]{1,0:T(8,128)} %bitcast.15), channel_id=1, source_target_pairs={{0,16},{16,0},{1,17},{17,1},{2,18},{18,2},{3,19},{19,3},{4,20},{20... | collective-permute-start | bytes 221192 | tf_op jit(solution)/shard_map/ppermute | solution.py:51
  2.1 0.1 collective-permute-start.1
  2.2 1.0 %shard_map.77.near = f32[2,37,256]{2,1,0:T(8,128)S(1)} custom-call(f32[72,256]{1,0:T(8,128)} %bitcast.16, f32[72,256]{1,0:T(8,128)} %bitcast.18, s32[1,256]{1,0:T(1,128)} %bitcast.19, s32[1,256]{1,0:T(1,128)} %bitcast.20), custom_call_target="tpu_custom_call" | custom-call | bytes 230000 | tf_op jit(solution)/shard_map/pallas_call | solution.py:211
  3.2 0.1 collective-permute-done.image_far
  3.3 0.4 collective-permute-done.1.text_far
  3.6 0.2 shard_map.78
  3.8 26.3 %all_to_all.10 = f32[64,37,1,128]{3,2,1,0:T(1,128)S(1)} all-to-all(f32[64,37,1,128]{3,2,1,0:T(1,128)S(1)} %bitcast.12), channel_id=1, replica_groups={{0,1,2,3,4,5,6,7,8,9,10,11,12,13,14,15,32,33,34,35,36,37,38,39,40,41,42..., dimensions={0} | all-to-all | bytes 2424832 | tf_op jit(solution)/shard_map/all_to_all | solution.py:35
  30.1 0.9 %shard_map.79.near = f32[264,256]{1,0:T(8,128)S(1)} custom-call(f32[2368,128]{1,0:T(8,128)S(1)} %bitcast.10), custom_call_target="tpu_custom_call" | custom-call | tf_op jit(solution)/shard_map/pallas_call | solution.py:211
  31.0 1.8 %collective-permute-start.2 = (f32[264,256]{1,0:T(8,128)S(1)}, f32[264,256]{1,0:T(8,128)S(1)}, u32[]{:S(2)}, u32[]{:S(2)}) collective-permute-start(f32[264,256]{1,0:T(8,128)S(1)} %shard_map.79.near), channel_id=1, source_target_pairs={{0,16},{16,0},{1,17},{17,1},{2,18},{18,2},{3,19},{19,3},{4,20},{20... | collective-permute-start | bytes 811016 | tf_op jit(solution)/shard_map/ppermute | solution.py:51
  34.1 0.0 collective-permute-done.2.far
  34.1 1.4 %shard_map.80 = f32[2304,128]{1,0:T(8,128)S(1)} custom-call(f32[1]{0:T(128)S(6)} %copy.10.log_scale, f32[1]{0:T(128)S(6)} %copy.11.bias, f32[2368,128]{1,0:T(8,128)S(1)} %bitcast.11, f32[264,256]{1,0:T(8,128)S(1)} %shard_map.79.near, f32[264,256]{1,0:T(8,128)S(1)} %collective-permute-done.2.far), custom_call_target="tpu_custom_call" | custom-call | tf_op jit(solution)/shard_map/pallas_call | solution.py:211
  35.5 24.0 %all_to_all.11 = f32[64,36,1,128]{3,2,1,0:T(1,128)S(1)} all-to-all(f32[64,36,1,128]{3,2,1,0:T(1,128)S(1)} %bitcast.13), channel_id=1, replica_groups={{0,1,2,3,4,5,6,7,8,9,10,11,12,13,14,15,32,33,34,35,36,37,38,39,40,41,42..., dimensions={0} | all-to-all | bytes 2359296 | tf_op jit(solution)/shard_map/all_to_all | solution.py:35
  59.5 0.2 shard_map.81
  59.7 1.1 %collective-permute-start.3 = (f32[2,36,256]{2,1,0:T(8,128)S(1)}, f32[2,36,256]{2,1,0:T(8,128)S(1)}, u32[]{:S(2)}, u32[]{:S(2)}) collective-permute-start(f32[2,36,256]{2,1,0:T(8,128)S(1)} %get-tuple-element.7), channel_id=1, source_target_pairs={{0,16},{16,0},{1,17},{17,1},{2,18},{18,2},{3,19},{19,3},{4,20},{20... | collective-permute-start | bytes 221192 | tf_op jit(solution)/shard_map/ppermute | solution.py:51
  60.8 0.9 %collective-permute-done.3.received = f32[2,36,256]{2,1,0:T(8,128)S(1)} collective-permute-done((f32[2,36,256]{2,1,0:T(8,128)S(1)}, f32[2,36,256]{2,1,0:T(8,128)S(1)}, u32[]{:S(2)}, u32[]{:S(2)}) %collective-permute-start.3) | collective-permute-done | bytes 73760 | tf_op jit(solution)/shard_map/ppermute | solution.py:51
  61.8 0.7 %shard_map.82 = (f32[72,256]{1,0:T(8,128)}, f32[72,256]{1,0:T(8,128)}) custom-call(f32[2,36,256]{2,1,0:T(8,128)S(1)} %get-tuple-element.6.own, f32[2,36,256]{2,1,0:T(8,128)S(1)} %collective-permute-done.3.received), custom_call_target="tpu_custom_call" | custom-call | tf_op jit(solution)/shard_map/pallas_call | solution.py:211
Async XLA Ops:
  0.6 2.6 %collective-permute-start = (f32[72,256]{1,0:T(8,128)}, f32[72,256]{1,0:T(8,128)S(1)}, u32[]{:S(2)}, u32[]{:S(2)}) collective-permute-start(f32[72,256]{1,0:T(8,128)} %bitcast.15), channel_id=1, source_target_pairs={{0,16},{16,0},{1,17},{17,1},{2,18},{18,2},{3,19},{19,3},{4,20},{20... | collective-permute-start | bytes 221192 | tf_op jit(solution)/shard_map/ppermute | solution.py:51
  2.1 1.5 %collective-permute-start.1 = (f32[72,256]{1,0:T(8,128)}, f32[72,256]{1,0:T(8,128)S(1)}, u32[]{:S(2)}, u32[]{:S(2)}) collective-permute-start(f32[72,256]{1,0:T(8,128)} %bitcast.17), channel_id=1, source_target_pairs={{0,16},{16,0},{1,17},{17,1},{2,18},{18,2},{3,19},{19,3},{4,20},{20... | collective-permute-start | bytes 221192 | tf_op jit(solution)/shard_map/ppermute | solution.py:51
  31.0 3.1 %collective-permute-start.2 = (f32[264,256]{1,0:T(8,128)S(1)}, f32[264,256]{1,0:T(8,128)S(1)}, u32[]{:S(2)}, u32[]{:S(2)}) collective-permute-start(f32[264,256]{1,0:T(8,128)S(1)} %shard_map.79.near), channel_id=1, source_target_pairs={{0,16},{16,0},{1,17},{17,1},{2,18},{18,2},{3,19},{19,3},{4,20},{20... | collective-permute-start | bytes 811016 | tf_op jit(solution)/shard_map/ppermute | solution.py:51
  59.7 2.1 %collective-permute-start.3 = (f32[2,36,256]{2,1,0:T(8,128)S(1)}, f32[2,36,256]{2,1,0:T(8,128)S(1)}, u32[]{:S(2)}, u32[]{:S(2)}) collective-permute-start(f32[2,36,256]{2,1,0:T(8,128)S(1)} %get-tuple-element.7), channel_id=1, source_target_pairs={{0,16},{16,0},{1,17},{17,1},{2,18},{18,2},{3,19},{19,3},{4,20},{20... | collective-permute-start | bytes 221192 | tf_op jit(solution)/shard_map/ppermute | solution.py:51

commit v5 on v4

v5 whole, which is shorter than its diff:
```python
import jax
import jax.numpy as jnp
from jax import lax
from jax.experimental import pallas as pl
from jax.experimental.pallas import tpu as pltpu
from jax.sharding import Mesh
from jax.sharding import PartitionSpec as P

EPSILON = 1e-06
F32 = jnp.float32
BF16 = jnp.bfloat16

FEATS = 72
ROWS = 256
PEERS = 32
WIDE = 64
THIN = 32
TRIO = 18
IN_ROWS = 55
BACK_ROWS = 54
OPPOSITE = 22
STRIP = 8 * TRIO
DEPTH = 4 * STRIP
AXES = ("x", "c", "z", "y")


def peer_groups():
    groups = []
    for core in range(2):
        for half in range(2):
            peers = [p ^ (core * OPPOSITE) for p in range(PEERS)]
            groups.append(
                [((q // 8 * 2 + core) * 4 + half * 2 + q // 4 % 2) * 4 + q % 4 for q in peers]
            )
    return groups


def exchange(pieces):
    rows = pieces.shape[0] // PEERS
    held = lax.all_to_all(
        pieces.reshape(PEERS, rows, 1, 128),
        AXES,
        0,
        0,
        axis_index_groups=peer_groups(),
        tiled=True,
    )
    return held.reshape(pieces.shape)


def other_core(x):
    return lax.ppermute(x, "c", [(0, 1), (1, 0)])


def other_half(x):
    return lax.ppermute(x, "z", [(0, 2), (2, 0), (1, 3), (3, 1)])


def joined(x, axis, left):
    high = x.astype(BF16)
    low = (x - high.astype(F32)).astype(BF16)
    return jnp.concatenate([high, high, low] if left else [high, low, high], axis=axis)


def product(first, second, axis):
    dims = (((axis,), (0,)), ((), ()))
    return lax.dot_general(
        joined(first, axis, True), joined(second, 0, False), dims, preferred_element_type=F32
    )


def squares(x):
    return jnp.sum(x * x, axis=0, keepdims=True)


def other_order(x):
    pair = 2 * TRIO
    return jnp.concatenate(
        [
            x[g * STRIP + k * pair : g * STRIP + (k + 1) * pair]
            for g in range(4)
            for k in (3, 2, 1, 0)
        ],
        axis=0,
    )


def block_of(x, core, rows):
    size = 8 * rows
    return pl.ds(pl.multiple_of((x ^ (2 * core)) * size, 8), size)


def strip(block, rows, first):
    return jnp.concatenate(
        [block[t * rows + first : t * rows + first + TRIO] for t in range(8)], axis=0
    )


def pack_kernel(image, text, image_owner, text_owner, out, held, owners, sems):
    core = lax.axis_index("c")
    copies = [
        pltpu.make_async_copy(src, dst, sems.at[i])
        for i, (src, dst) in enumerate(
            (
                (image, held.at[0]),
                (text, held.at[1]),
                (image_owner, owners.at[0]),
                (text_owner, owners.at[1]),
            )
        )
    ]
    for copy in copies:
        copy.start()
    for copy in copies:
        copy.wait()

    def wide(a):
        own = slice(a * WIDE, (a + 1) * WIDE)
        return jnp.concatenate([held[0, :36, own], held[0, 36:, own]], axis=1)

    def thin(b):
        own = slice(b * THIN, (b + 1) * THIN)
        return jnp.concatenate(
            [held[1, g * TRIO : (g + 1) * TRIO, own] for g in range(4)], axis=1
        )

    def owner(k, i, size):
        return owners[k, :, i * size : (i + 1) * size].astype(F32)

    wides = [wide(a) for a in range(4)]
    thins = [thin(b) for b in range(8)]
    wide_owners = [owner(0, a, WIDE) for a in range(4)]
    thin_owners = [owner(1, b, THIN) for b in range(8)]

    def mine(parts, flip):
        return [jnp.where(core == 0, parts[i], parts[i ^ flip]) for i in range(len(parts))]

    wides, wide_owners = mine(wides, 2), mine(wide_owners, 2)
    thins, thin_owners = mine(thins, 6), mine(thin_owners, 6)
    none = jnp.zeros((1, THIN), F32)
    for p in range(PEERS):
        a, b = p // 8, p % 8
        last = jnp.concatenate([wide_owners[a], thin_owners[b], none], axis=1)
        out[p * IN_ROWS : (p + 1) * IN_ROWS] = jnp.concatenate(
            [wides[a], thins[b], last], axis=0
        )


def text_kernel(pieces, out):
    core = lax.axis_index("c")
    blocks = [pieces[block_of(x, core, IN_ROWS)] for x in range(4)]
    strips = [strip(b, IN_ROWS, 36) for b in blocks]
    text = jnp.concatenate(
        [
            jnp.concatenate([s[:, g * THIN : (g + 1) * THIN] for s in strips], axis=1)
            for g in range(4)
        ],
        axis=0,
    )
    owner = jnp.concatenate([b[54:55, WIDE : WIDE + THIN] for b in blocks], axis=1)
    out[:DEPTH] = text
    out[DEPTH:] = jnp.concatenate([squares(text), owner, jnp.zeros((6, 128), F32)], axis=0)


def image_kernel(pieces, text, image_out, extra, part):
    core = lax.axis_index("c")
    blocks = [pieces[block_of(x, core, IN_ROWS)] for x in range(4)]
    strips = [[strip(b, IN_ROWS, e * TRIO) for b in blocks] for e in range(2)]
    image = jnp.concatenate(
        [
            jnp.concatenate(
                [s[:, g // 2 * WIDE : (g // 2 + 1) * WIDE] for s in strips[g % 2]], axis=1
            )
            for g in range(4)
        ],
        axis=0,
    )
    image_out[...] = image
    image_squares = squares(image)
    owner = jnp.concatenate([b[54:55, :WIDE] for b in blocks], axis=1)
    extra[...] = jnp.concatenate([owner, jnp.zeros((7, ROWS), F32)], axis=0)
    part[:ROWS] = product(image, text[:DEPTH], 0)
    part[ROWS:] = jnp.concatenate(
        [
            text[DEPTH : DEPTH + 1],
            image_squares[:, :128],
            image_squares[:, 128:],
            jnp.zeros((5, 128), F32),
        ],
        axis=0,
    )


def far_kernel(image, text_far, text_out, part):
    text = other_order(text_far[:DEPTH])
    text_out[:DEPTH] = text
    text_out[DEPTH:] = text_far[DEPTH:]
    part[:ROWS] = product(image[...], text, 0)
    part[ROWS:] = text_far[DEPTH:]


def pair_kernel(
    log_scale, bias, image, extra, text, text_far, own, own_more, far, far_more, sent, mixed, factors
):
    scale = jnp.exp(jnp.full((1, 1), log_scale[0], F32))
    raw = jnp.concatenate(
        [own[:ROWS] + own_more[:ROWS], far[:ROWS] + far_more[:ROWS]], axis=1
    )
    own_sums = own[ROWS:] + own_more[ROWS:]
    far_sums = far[ROWS:] + far_more[ROWS:]
    image_sums = jnp.concatenate([own_sums[1:2], own_sums[2:3]], axis=1)
    image_inv = lax.rsqrt(image_sums + EPSILON)
    text_inv = lax.rsqrt(jnp.concatenate([own_sums[0:1], far_sums[0:1]], axis=1) + EPSILON)
    text_owner = jnp.concatenate(
        [text[DEPTH + 1 : DEPTH + 2], text_far[DEPTH + 1 : DEPTH + 2]], axis=1
    )
    turned = jnp.concatenate([image_inv, extra[0:1], jnp.zeros((6, ROWS), F32)], axis=0).T
    inv = turned[:, 0:1] * text_inv
    cosines = raw * inv
    labels = jnp.where(turned[:, 1:2] == text_owner, 1.0, -1.0)
    logits = scale * cosines + bias[0]
    grads = scale * (-labels * jax.nn.sigmoid(-labels * logits))
    weighted = grads * cosines
    text_dot = jnp.sum(weighted, axis=0, keepdims=True)
    image_dot = jnp.broadcast_to(jnp.sum(weighted, axis=1, keepdims=True), (ROWS, 128)).T[0:1]
    both = grads * inv
    text_factor = text_inv * text_inv * text_dot
    mixed[...] = both
    factors[...] = jnp.concatenate(
        [image_inv * image_inv * image_dot, text_factor, jnp.zeros((6, ROWS), F32)], axis=0
    )
    far_grad = product(image[...], both[:, 128:], 1) - text_far[:DEPTH] * text_factor[:, 128:]
    sent[...] = other_order(far_grad)


def own_kernel(image, text, text_far, mixed, factors, image_out, text_out):
    texts = jnp.concatenate([text[:DEPTH], text_far[:DEPTH]], axis=1)
    image_grad = product(texts, mixed[...].T, 1) - image[...] * factors[0:1]
    text_out[...] = product(image[...], mixed[:, :128], 1) - text[:DEPTH] * factors[1:2, :128]
    for x in range(4):
        own = slice(x * WIDE, (x + 1) * WIDE)
        for e in range(2):
            image_out[x, e] = jnp.concatenate(
                [
                    image_grad[e * STRIP : (e + 1) * STRIP, own],
                    image_grad[(e + 2) * STRIP : (e + 3) * STRIP, own],
                ],
                axis=1,
            )


def join_kernel(image_grad, text_grad, received, out):
    core = lax.axis_index("c")
    text = text_grad[...] + received[...]
    for x in range(4):
        own = slice(x * THIN, (x + 1) * THIN)
        thin = jnp.concatenate(
            [text[g * STRIP : (g + 1) * STRIP, own] for g in range(4)], axis=1
        )
        parts = (image_grad[x, 0], image_grad[x, 1], thin)
        out[block_of(x, core, BACK_ROWS)] = jnp.concatenate(
            [part[t * TRIO : (t + 1) * TRIO] for t in range(8) for part in parts], axis=0
        )


def sum_kernel(pieces, image_grad, text_grad):
    core = lax.axis_index("c")
    size = 8 * BACK_ROWS
    blocks = [pieces[x * size : (x + 1) * size] for x in range(4)]
    wides = [
        sum(b[t * BACK_ROWS : t * BACK_ROWS + 36] for t in range(8)) for b in blocks
    ]
    total = sum(blocks)
    thins = [total[t * BACK_ROWS + 36 : (t + 1) * BACK_ROWS] for t in range(8)]

    def order(parts, flip):
        return jnp.where(
            core == 0,
            jnp.concatenate(parts, axis=1),
            jnp.concatenate([parts[i ^ flip] for i in range(len(parts))], axis=1),
        )

    for h in range(2):
        image_grad[h * 36 : (h + 1) * 36] = order(
            [w[:, h * WIDE : (h + 1) * WIDE] for w in wides], 2
        )
    for g in range(4):
        text_grad[g * TRIO : (g + 1) * TRIO] = order(
            [s[:, g * THIN : (g + 1) * THIN] for s in thins], 6
        )


def call(kernel, outs, args, scalars=0, flops=0, **more):
    smem = [pl.BlockSpec(memory_space=pltpu.SMEM)] * scalars
    vmem = [pl.BlockSpec(memory_space=pltpu.VMEM)] * (len(args) - scalars)
    return pl.pallas_call(
        kernel,
        out_shape=[jax.ShapeDtypeStruct(s, F32) for s in outs],
        in_specs=more.pop("in_specs", smem + vmem),
        out_specs=[pl.BlockSpec(memory_space=pltpu.VMEM)] * len(outs),
        compiler_params=pltpu.CompilerParams(vmem_limit_bytes=40 * 1024 * 1024),
        cost_estimate=pl.CostEstimate(
            flops=flops, bytes_accessed=3000000, transcendentals=0
        ),
        **more,
    )(*args)


def local(image_emb, text_emb, image_owner, text_owner, log_scale, bias):
    inputs = (
        image_emb.T,
        text_emb.T,
        image_owner.reshape(1, ROWS),
        text_owner.reshape(1, ROWS),
    )
    (packed,) = call(
        pack_kernel,
        [(PEERS * IN_ROWS, 128)],
        tuple(pltpu.with_memory_space_constraint(x, pltpu.HBM) for x in inputs),
        in_specs=[pl.BlockSpec(memory_space=pltpu.HBM)] * 4,
        scratch_shapes=[
            pltpu.VMEM((2, FEATS, ROWS), F32),
            pltpu.VMEM((2, 1, ROWS), jnp.int32),
            pltpu.SemaphoreType.DMA((4,)),
        ],
    )
    held = exchange(packed)
    (text,) = call(text_kernel, [(DEPTH + 8, 128)], (held,))
    text_received = other_core(text)
    image, extra, own = call(
        image_kernel, [(DEPTH, ROWS), (8, ROWS), (ROWS + 8, 128)], (held, text)
    )
    own_more = other_half(own)
    text_far, far = call(
        far_kernel, [(DEPTH + 8, 128), (ROWS + 8, 128)], (image, text_received)
    )
    far_more = other_half(far)
    sent, mixed, factors = call(
        pair_kernel,
        [(DEPTH, 128), (ROWS, ROWS), (8, ROWS)],
        (log_scale, bias, image, extra, text, text_far, own, own_more, far, far_more),
        scalars=2,
    )
    received = other_core(sent)
    image_grad, text_grad = call(
        own_kernel,
        [(4, 2, STRIP, 128), (DEPTH, 128)],
        (image, text, text_far, mixed, factors),
    )
    (grads,) = call(
        join_kernel, [(PEERS * BACK_ROWS, 128)], (image_grad, text_grad, received)
    )
    back = exchange(grads)
    image_result, text_result = call(sum_kernel, [(FEATS, ROWS)] * 2, (back,))
    return image_result.T, text_result.T


def solution(mesh):
    fine = Mesh(mesh.devices.reshape(4, 2, 4, 4), ("x", "c", "z", "y"))
    rows = P(("x", "c"))
    block = P(("x", "c"), ("z", "y"))
    return jax.shard_map(
        local,
        mesh=fine,
        in_specs=(block, block, rows, rows, P(), P()),
        out_specs=(block, block),
        check_vma=False,
    )
```

time: 62.7 us -> 58.6 us (0.935)
  blocking collectives: 50.3 us -> 39 us
  waiting for transfers between devices: 1.33 us -> 5.03 us
  starting transfers between devices: 4.54 us -> 6.98 us
  Pallas kernels: 4.26 us -> 5.29 us
    all_to_all x2, blocking collectives: 50.3 us -> 39 us  [exchange(): lax.all_to_all(pieces.reshape(PEERS, rows, 1, 128), AXES, 0, 0, axis_inde...]
    ppermute x0 -> x2, waiting for transfers between devices: none -> 4.61 us  [other_half(): return lax.ppermute(x, 'z', [(0, 2), (2, 0), (1, 3), (3, 1)])]
    ppermute x0 -> x2, starting transfers between devices: none -> 3.93 us  [other_half(): return lax.ppermute(x, 'z', [(0, 2), (2, 0), (1, 3), (3, 1)])]
    ppermute x4 -> x2, starting transfers between devices: 4.54 us -> 3.05 us  [other_core(): return lax.ppermute(x, 'c', [(0, 1), (1, 0)])]
    pallas_call x6 -> x8, Pallas kernels: 4.26 us -> 5.29 us  [call(): pl.pallas_call(kernel, out_shape=[jax.ShapeDtypeStruct(s, F32) for s in o...]
    ppermute x4 -> x2, waiting for transfers between devices: 1.33 us -> 0.42 us  [other_core(): return lax.ppermute(x, 'c', [(0, 1), (1, 0)])]
  transfers between devices with their start and end apart: 4 -> 4, of which waited for: 3 -> 3; matrix products, arithmetic and copies ran while one was open for 0% -> 0% of each run, Pallas kernels for 2% -> 3%
where the time goes in v5:
time: 58.6 us; the launch traced here: 58.3 us
  blocking collectives  39 us (67%)
  starting transfers between devices  6.98 us (12%)
  Pallas kernels  5.29 us (9%)
  waiting for transfers between devices  5.03 us (9%)
  between operations  1.97 us (3%)
    all_to_all x2, blocking collectives, exchange(): lax.all_to_all(pieces.reshape(PEERS, rows, 1, 128), AXES, 0, 0, axis_inde...  39 us
    pallas_call x8, Pallas kernels, call(): pl.pallas_call(kernel, out_shape=[jax.ShapeDtypeStruct(s, F32) for s in o...  5.29 us
    ppermute x2, waiting for transfers between devices, other_half(): return lax.ppermute(x, 'z', [(0, 2), (2, 0), (1, 3), (3, 1)])  4.61 us
    ppermute x2, starting transfers between devices, other_half(): return lax.ppermute(x, 'z', [(0, 2), (2, 0), (1, 3), (3, 1)])  3.93 us
    ppermute x2, starting transfers between devices, other_core(): return lax.ppermute(x, 'c', [(0, 1), (1, 0)])  3.05 us
  transfers between devices with their start and end apart: 4, of which 3 were waited for; matrix products, arithmetic and copies ran while one was open for 0% of the time, Pallas kernels for 3%

profile of v5, /device:TPU:1, one launch (start us, length us, event | category | flops | bytes accessed | tf_op | source)
XLA Modules:
  0.0 58.3 jit_solution(15760694213500285355)
XLA Ops:
  0.6 1.2 %shard_map.77 = f32[1760,128]{1,0:T(8,128)S(1)} custom-call(f32[72,256]{1,0:T(8,128)} %bitcast.15, f32[72,256]{1,0:T(8,128)} %bitcast.16, s32[1,256]{1,0:T(1,128)} %bitcast.17, s32[1,256]{1,0:T(1,128)} %bitcast.18), custom_call_target="tpu_custom_call" | custom-call | bytes 3000000 | tf_op jit(solution)/shard_map/pallas_call | solution.py:296
  1.8 20.4 %all_to_all.10 = f32[32,55,1,128]{3,2,1,0:T(1,128)S(1)} all-to-all(f32[32,55,1,128]{3,2,1,0:T(1,128)S(1)} %bitcast.12), channel_id=1, replica_groups={{0,1,2,3,4,5,6,7,32,33,34,35,36,37,38,39,64,65,66,67,68,69,70,71,96,97,..., dimensions={0} | all-to-all | bytes 1802240 | tf_op jit(solution)/shard_map/all_to_all | solution.py:40
  22.2 0.3 shard_map.78.text
  22.6 1.8 %collective-permute-start = (f32[584,128]{1,0:T(8,128)S(1)}, f32[584,128]{1,0:T(8,128)S(1)}, u32[]{:S(2)}, u32[]{:S(2)}) collective-permute-start(f32[584,128]{1,0:T(8,128)S(1)} %shard_map.78.text), channel_id=1, source_target_pairs={{0,16},{16,0},{1,17},{17,1},{2,18},{18,2},{3,19},{19,3},{4,20},{20... | collective-permute-start | bytes 897032 | tf_op jit(solution)/shard_map/ppermute | solution.py:52
  24.4 0.7 %shard_map.79 = (f32[576,256]{1,0:T(8,128)S(1)}, f32[8,256]{1,0:T(8,128)S(1)}, f32[264,128]{1,0:T(8,128)S(1)}) custom-call(f32[1760,128]{1,0:T(8,128)S(1)} %bitcast.11, f32[584,128]{1,0:T(8,128)S(1)} %shard_map.78.text), custom_call_target="tpu_custom_call" | custom-call | bytes 3000000 | tf_op jit(solution)/shard_map/pallas_call | solution.py:296
  25.1 3.4 %collective-permute-start.1 = (f32[264,128]{1,0:T(8,128)S(1)}, f32[264,128]{1,0:T(8,128)S(1)}, u32[]{:S(2)}, u32[]{:S(2)}) collective-permute-start(f32[264,128]{1,0:T(8,128)S(1)} %get-tuple-element.17.own), channel_id=1, source_target_pairs={{0,8},{8,0},{4,12},{12,4},{1,9},{9,1},{5,13},{13,5},{2,10},{10,2},... | collective-permute-start | bytes 405512 | tf_op jit(solution)/shard_map/ppermute | solution.py:56
  28.4 0.0 collective-permute-done.text_far
  28.4 0.4 shard_map.80
  28.9 0.5 collective-permute-start.2
  30.7 1.6 %collective-permute-done.1.own_more = f32[264,128]{1,0:T(8,128)S(1)} collective-permute-done((f32[264,128]{1,0:T(8,128)S(1)}, f32[264,128]{1,0:T(8,128)S(1)}, u32[]{:S(2)}, u32[]{:S(2)}) %collective-permute-start.1) | collective-permute-done | bytes 135200 | tf_op jit(solution)/shard_map/ppermute | solution.py:56
  32.4 3.0 %collective-permute-done.2.far_more = f32[264,128]{1,0:T(8,128)S(1)} collective-permute-done((f32[264,128]{1,0:T(8,128)S(1)}, f32[264,128]{1,0:T(8,128)S(1)}, u32[]{:S(2)}, u32[]{:S(2)}) %collective-permute-start.2) | collective-permute-done | bytes 135200 | tf_op jit(solution)/shard_map/ppermute | solution.py:56
  35.3 0.7 %shard_map.81 = (f32[576,128]{1,0:T(8,128)S(1)}, f32[256,256]{1,0:T(8,128)S(1)}, f32[8,256]{1,0:T(8,128)S(1)}) custom-call(f32[1]{0:T(128)S(6)} %copy.10.log_scale, f32[1]{0:T(128)S(6)} %copy.11.bias, f32[576,256]{1,0:T(8,128)S(1)} %get-tuple-element.14.image, f32[8,256]{1,0:T(8,128)S(1)} %get-tuple-element.16.extra, f32[584,128]{1,0:T(8,128)S(1)} %shard_map.78.text, ...), custom_call_target="tpu_custom_call" | custom-call | bytes 3000000 | tf_op jit(solution)/shard_map/pallas_call | solution.py:296
  36.1 1.2 %collective-permute-start.3 = (f32[576,128]{1,0:T(8,128)S(1)}, f32[576,128]{1,0:T(8,128)S(1)}, u32[]{:S(2)}, u32[]{:S(2)}) collective-permute-start(f32[576,128]{1,0:T(8,128)S(1)} %get-tuple-element.23), channel_id=1, source_target_pairs={{0,16},{16,0},{1,17},{17,1},{2,18},{18,2},{3,19},{19,3},{4,20},{20... | collective-permute-start | bytes 884744 | tf_op jit(solution)/shard_map/ppermute | solution.py:52
  37.3 0.8 %shard_map.82 = (f32[4,2,144,128]{3,2,1,0:T(8,128)S(1)}, f32[576,128]{1,0:T(8,128)S(1)}) custom-call(f32[576,256]{1,0:T(8,128)S(1)} %get-tuple-element.14.image, f32[584,128]{1,0:T(8,128)S(1)} %shard_map.78.text, f32[584,128]{1,0:T(8,128)S(1)} %get-tuple-element.15.text_far, f32[256,256]{1,0:T(8,128)S(1)} %get-tuple-element.19.mixed, ...), custom_call_target="tpu_custom_call" | custom-call | bytes 3000000 | tf_op jit(solution)/shard_map/pallas_call | solution.py:296
  38.1 0.4 collective-permute-done.3.received
  38.5 0.3 shard_map.83
  38.8 18.6 %all_to_all.11 = f32[32,54,1,128]{3,2,1,0:T(1,128)S(1)} all-to-all(f32[32,54,1,128]{3,2,1,0:T(1,128)S(1)} %bitcast.14), channel_id=1, replica_groups={{0,1,2,3,4,5,6,7,32,33,34,35,36,37,38,39,64,65,66,67,68,69,70,71,96,97,..., dimensions={0} | all-to-all | bytes 1769472 | tf_op jit(solution)/shard_map/all_to_all | solution.py:40
  57.4 0.9 %shard_map.84 = (f32[72,256]{1,0:T(8,128)}, f32[72,256]{1,0:T(8,128)}) custom-call(f32[1728,128]{1,0:T(8,128)S(1)} %bitcast.13), custom_call_target="tpu_custom_call" | custom-call | bytes 3000000 | tf_op jit(solution)/shard_map/pallas_call | solution.py:296
Async XLA Ops:
  22.6 5.9 %collective-permute-start = (f32[584,128]{1,0:T(8,128)S(1)}, f32[584,128]{1,0:T(8,128)S(1)}, u32[]{:S(2)}, u32[]{:S(2)}) collective-permute-start(f32[584,128]{1,0:T(8,128)S(1)} %shard_map.78.text), channel_id=1, source_target_pairs={{0,16},{16,0},{1,17},{17,1},{2,18},{18,2},{3,19},{19,3},{4,20},{20... | collective-permute-start | bytes 897032 | tf_op jit(solution)/shard_map/ppermute | solution.py:52
  25.1 7.3 %collective-permute-start.1 = (f32[264,128]{1,0:T(8,128)S(1)}, f32[264,128]{1,0:T(8,128)S(1)}, u32[]{:S(2)}, u32[]{:S(2)}) collective-permute-start(f32[264,128]{1,0:T(8,128)S(1)} %get-tuple-element.17.own), channel_id=1, source_target_pairs={{0,8},{8,0},{4,12},{12,4},{1,9},{9,1},{5,13},{13,5},{2,10},{10,2},... | collective-permute-start | bytes 405512 | tf_op jit(solution)/shard_map/ppermute | solution.py:56
  28.9 6.5 %collective-permute-start.2 = (f32[264,128]{1,0:T(8,128)S(1)}, f32[264,128]{1,0:T(8,128)S(1)}, u32[]{:S(2)}, u32[]{:S(2)}) collective-permute-start(f32[264,128]{1,0:T(8,128)S(1)} %get-tuple-element.18.far), channel_id=1, source_target_pairs={{0,8},{8,0},{4,12},{12,4},{1,9},{9,1},{5,13},{13,5},{2,10},{10,2},... | collective-permute-start | bytes 405512 | tf_op jit(solution)/shard_map/ppermute | solution.py:56
  36.1 2.4 %collective-permute-start.3 = (f32[576,128]{1,0:T(8,128)S(1)}, f32[576,128]{1,0:T(8,128)S(1)}, u32[]{:S(2)}, u32[]{:S(2)}) collective-permute-start(f32[576,128]{1,0:T(8,128)S(1)} %get-tuple-element.23), channel_id=1, source_target_pairs={{0,16},{16,0},{1,17},{17,1},{2,18},{18,2},{3,19},{19,3},{4,20},{20... | collective-permute-start | bytes 884744 | tf_op jit(solution)/shard_map/ppermute | solution.py:52

commit v6 on v5

--- a/solution.py
+++ b/solution.py
@@ -30,7 +30,10 @@
         for half in range(2):
             peers = [p ^ (core * OPPOSITE) for p in range(PEERS)]
             groups.append(
-                [((q // 8 * 2 + core) * 4 + half * 2 + q // 4 % 2) * 4 + q % 4 for q in peers]
+                [
+                    ((q // 8 * 2 + core) * 4 + (3 - q // 4 % 2 if half else q // 4 % 2)) * 4 + q % 4
+                    for q in peers
+                ]
             )
     return groups
 
@@ -53,7 +56,7 @@
 
 
 def other_half(x):
-    return lax.ppermute(x, "z", [(0, 2), (2, 0), (1, 3), (3, 1)])
+    return lax.ppermute(x, "z", [(0, 3), (3, 0), (1, 2), (2, 1)])
 
 
 def joined(x, axis, left):
@@ -146,7 +149,7 @@
         )
 
 
-def text_kernel(pieces, out):
+def near_kernel(pieces, text_out, image_out, extra, part):
     core = lax.axis_index("c")
     blocks = [pieces[block_of(x, core, IN_ROWS)] for x in range(4)]
     strips = [strip(b, IN_ROWS, 36) for b in blocks]
@@ -158,13 +161,9 @@
         axis=0,
     )
     owner = jnp.concatenate([b[54:55, WIDE : WIDE + THIN] for b in blocks], axis=1)
-    out[:DEPTH] = text
-    out[DEPTH:] = jnp.concatenate([squares(text), owner, jnp.zeros((6, 128), F32)], axis=0)
-
-
-def image_kernel(pieces, text, image_out, extra, part):
-    core = lax.axis_index("c")
-    blocks = [pieces[block_of(x, core, IN_ROWS)] for x in range(4)]
+    text_squares = squares(text)
+    text_out[:DEPTH] = text
+    text_out[DEPTH:] = jnp.concatenate([text_squares, owner, jnp.zeros((6, 128), F32)], axis=0)
     strips = [[strip(b, IN_ROWS, e * TRIO) for b in blocks] for e in range(2)]
     image = jnp.concatenate(
         [
@@ -179,10 +178,10 @@
     image_squares = squares(image)
     owner = jnp.concatenate([b[54:55, :WIDE] for b in blocks], axis=1)
     extra[...] = jnp.concatenate([owner, jnp.zeros((7, ROWS), F32)], axis=0)
-    part[:ROWS] = product(image, text[:DEPTH], 0)
+    part[:ROWS] = product(image, text, 0)
     part[ROWS:] = jnp.concatenate(
         [
-            text[DEPTH : DEPTH + 1],
+            text_squares,
             image_squares[:, :128],
             image_squares[:, 128:],
             jnp.zeros((5, 128), F32),
@@ -325,11 +324,12 @@
         ],
     )
     held = exchange(packed)
-    (text,) = call(text_kernel, [(DEPTH + 8, 128)], (held,))
+    text, image, extra, own = call(
+        near_kernel,
+        [(DEPTH + 8, 128), (DEPTH, ROWS), (8, ROWS), (ROWS + 8, 128)],
+        (held,),
+    )
     text_received = other_core(text)
-    image, extra, own = call(
-        image_kernel, [(DEPTH, ROWS), (8, ROWS), (ROWS + 8, 128)], (held, text)
-    )
     own_more = other_half(own)
     text_far, far = call(
         far_kernel, [(DEPTH + 8, 128), (ROWS + 8, 128)], (image, text_received)

time: 58.6 us -> 58.1 us (level)
  waiting for transfers between devices: 5.03 us -> 3.95 us
  starting transfers between devices: 6.98 us -> 7.77 us
    ppermute x2, waiting for transfers between devices: 4.61 us -> 3.53 us  [other_half(): return lax.ppermute(x, 'z', [(0, 3), (3, 0), (1, 2), (2, 1)])]
    ppermute x2, starting transfers between devices: 3.93 us -> 4.66 us  [other_half(): return lax.ppermute(x, 'z', [(0, 3), (3, 0), (1, 2), (2, 1)])]
    pallas_call x8 -> x7, Pallas kernels: 5.29 us -> 5.23 us  [call(): pl.pallas_call(kernel, out_shape=[jax.ShapeDtypeStruct(s, F32) for s in o...]
  transfers between devices with their start and end apart: 4 -> 4, of which waited for: 3 -> 3; matrix products, arithmetic and copies ran while one was open for 0% -> 0% of each run, Pallas kernels for 3% -> 2%
where the time goes in v6:
time: 58.1 us; the launch traced here: 57.9 us
  blocking collectives  39 us (67%)
  starting transfers between devices  7.77 us (13%)
  Pallas kernels  5.23 us (9%)
  waiting for transfers between devices  3.95 us (7%)
  between operations  1.97 us (3%)
    all_to_all x2, blocking collectives, exchange(): lax.all_to_all(pieces.reshape(PEERS, rows, 1, 128), AXES, 0, 0, axis_inde...  39 us
    pallas_call x7, Pallas kernels, call(): pl.pallas_call(kernel, out_shape=[jax.ShapeDtypeStruct(s, F32) for s in o...  5.23 us
    ppermute x2, starting transfers between devices, other_half(): return lax.ppermute(x, 'z', [(0, 3), (3, 0), (1, 2), (2, 1)])  4.66 us
    ppermute x2, waiting for transfers between devices, other_half(): return lax.ppermute(x, 'z', [(0, 3), (3, 0), (1, 2), (2, 1)])  3.53 us
    ppermute x2, starting transfers between devices, other_core(): return lax.ppermute(x, 'c', [(0, 1), (1, 0)])  3.11 us
  transfers between devices with their start and end apart: 4, of which 3 were waited for; matrix products, arithmetic and copies ran while one was open for 0% of the time, Pallas kernels for 2%

profile of v6, /device:TPU:1, one launch (start us, length us, event | category | flops | bytes accessed | tf_op | source)
XLA Modules:
  0.0 57.9 jit_solution(2991259354432696704)
XLA Ops:
  0.6 1.2 %shard_map.77 = f32[1760,128]{1,0:T(8,128)S(1)} custom-call(f32[72,256]{1,0:T(8,128)} %bitcast.14, f32[72,256]{1,0:T(8,128)} %bitcast.15, s32[1,256]{1,0:T(1,128)} %bitcast.16, s32[1,256]{1,0:T(1,128)} %bitcast.17), custom_call_target="tpu_custom_call" | custom-call | bytes 3000000 | tf_op jit(solution)/shard_map/pallas_call | solution.py:295
  1.8 20.4 %all_to_all.10 = f32[32,55,1,128]{3,2,1,0:T(1,128)S(1)} all-to-all(f32[32,55,1,128]{3,2,1,0:T(1,128)S(1)} %bitcast.11), channel_id=1, replica_groups={{0,1,2,3,4,5,6,7,32,33,34,35,36,37,38,39,64,65,66,67,68,69,70,71,96,97,..., dimensions={0} | all-to-all | bytes 1802240 | tf_op jit(solution)/shard_map/all_to_all | solution.py:43
  22.2 0.9 %shard_map.78 = (f32[584,128]{1,0:T(8,128)S(1)}, f32[576,256]{1,0:T(8,128)S(1)}, f32[8,256]{1,0:T(8,128)S(1)}, f32[264,128]{1,0:T(8,128)S(1)}) custom-call(f32[1760,128]{1,0:T(8,128)S(1)} %bitcast.10), custom_call_target="tpu_custom_call" | custom-call | bytes 3000000 | tf_op jit(solution)/shard_map/pallas_call | solution.py:295
  23.1 1.8 %collective-permute-start = (f32[584,128]{1,0:T(8,128)S(1)}, f32[584,128]{1,0:T(8,128)S(1)}, u32[]{:S(2)}, u32[]{:S(2)}) collective-permute-start(f32[584,128]{1,0:T(8,128)S(1)} %get-tuple-element.16.text), channel_id=1, source_target_pairs={{0,16},{16,0},{1,17},{17,1},{2,18},{18,2},{3,19},{19,3},{4,20},{20... | collective-permute-start | bytes 897032 | tf_op jit(solution)/shard_map/ppermute | solution.py:55
  25.0 3.4 %collective-permute-start.1 = (f32[264,128]{1,0:T(8,128)S(1)}, f32[264,128]{1,0:T(8,128)S(1)}, u32[]{:S(2)}, u32[]{:S(2)}) collective-permute-start(f32[264,128]{1,0:T(8,128)S(1)} %get-tuple-element.19.own), channel_id=1, source_target_pairs={{0,12},{12,0},{4,8},{8,4},{1,13},{13,1},{5,9},{9,5},{2,14},{14,2},... | collective-permute-start | bytes 405512 | tf_op jit(solution)/shard_map/ppermute | solution.py:59
  28.4 0.0 collective-permute-done.text_far
  28.4 0.4 shard_map.79
  28.8 1.3 %collective-permute-start.2 = (f32[264,128]{1,0:T(8,128)S(1)}, f32[264,128]{1,0:T(8,128)S(1)}, u32[]{:S(2)}, u32[]{:S(2)}) collective-permute-start(f32[264,128]{1,0:T(8,128)S(1)} %get-tuple-element.20.far), channel_id=1, source_target_pairs={{0,12},{12,0},{4,8},{8,4},{1,13},{13,1},{5,9},{9,5},{2,14},{14,2},... | collective-permute-start | bytes 405512 | tf_op jit(solution)/shard_map/ppermute | solution.py:59
  31.4 0.8 %collective-permute-done.1.own_more = f32[264,128]{1,0:T(8,128)S(1)} collective-permute-done((f32[264,128]{1,0:T(8,128)S(1)}, f32[264,128]{1,0:T(8,128)S(1)}, u32[]{:S(2)}, u32[]{:S(2)}) %collective-permute-start.1) | collective-permute-done | bytes 135200 | tf_op jit(solution)/shard_map/ppermute | solution.py:59
  32.2 2.7 %collective-permute-done.2.far_more = f32[264,128]{1,0:T(8,128)S(1)} collective-permute-done((f32[264,128]{1,0:T(8,128)S(1)}, f32[264,128]{1,0:T(8,128)S(1)}, u32[]{:S(2)}, u32[]{:S(2)}) %collective-permute-start.2) | collective-permute-done | bytes 135200 | tf_op jit(solution)/shard_map/ppermute | solution.py:59
  34.9 0.7 %shard_map.80 = (f32[576,128]{1,0:T(8,128)S(1)}, f32[256,256]{1,0:T(8,128)S(1)}, f32[8,256]{1,0:T(8,128)S(1)}) custom-call(f32[1]{0:T(128)S(6)} %copy.10.log_scale, f32[1]{0:T(128)S(6)} %copy.11.bias, f32[576,256]{1,0:T(8,128)S(1)} %get-tuple-element.15.image, f32[8,256]{1,0:T(8,128)S(1)} %get-tuple-element.18.extra, f32[584,128]{1,0:T(8,128)S(1)} %get-tuple-element.16.text, ...), custom_call_target="tpu_custom_call" | custom-call | bytes 3000000 | tf_op jit(solution)/shard_map/pallas_call | solution.py:295
  35.6 1.3 %collective-permute-start.3 = (f32[576,128]{1,0:T(8,128)S(1)}, f32[576,128]{1,0:T(8,128)S(1)}, u32[]{:S(2)}, u32[]{:S(2)}) collective-permute-start(f32[576,128]{1,0:T(8,128)S(1)} %get-tuple-element.25), channel_id=1, source_target_pairs={{0,16},{16,0},{1,17},{17,1},{2,18},{18,2},{3,19},{19,3},{4,20},{20... | collective-permute-start | bytes 884744 | tf_op jit(solution)/shard_map/ppermute | solution.py:55
  36.9 0.8 %shard_map.81 = (f32[4,2,144,128]{3,2,1,0:T(8,128)S(1)}, f32[576,128]{1,0:T(8,128)S(1)}) custom-call(f32[576,256]{1,0:T(8,128)S(1)} %get-tuple-element.15.image, f32[584,128]{1,0:T(8,128)S(1)} %get-tuple-element.16.text, f32[584,128]{1,0:T(8,128)S(1)} %get-tuple-element.17.text_far, f32[256,256]{1,0:T(8,128)S(1)} %get-tuple-element.21.mixed, ...), custom_call_target="tpu_custom_call" | custom-call | bytes 3000000 | tf_op jit(solution)/shard_map/pallas_call | solution.py:295
  37.7 0.4 collective-permute-done.3.received
  38.1 0.3 shard_map.82
  38.4 18.6 %all_to_all.11 = f32[32,54,1,128]{3,2,1,0:T(1,128)S(1)} all-to-all(f32[32,54,1,128]{3,2,1,0:T(1,128)S(1)} %bitcast.13), channel_id=1, replica_groups={{0,1,2,3,4,5,6,7,32,33,34,35,36,37,38,39,64,65,66,67,68,69,70,71,96,97,..., dimensions={0} | all-to-all | bytes 1769472 | tf_op jit(solution)/shard_map/all_to_all | solution.py:43
  57.0 0.9 %shard_map.83 = (f32[72,256]{1,0:T(8,128)}, f32[72,256]{1,0:T(8,128)}) custom-call(f32[1728,128]{1,0:T(8,128)S(1)} %bitcast.12), custom_call_target="tpu_custom_call" | custom-call | bytes 3000000 | tf_op jit(solution)/shard_map/pallas_call | solution.py:295
Async XLA Ops:
  23.1 5.2 %collective-permute-start = (f32[584,128]{1,0:T(8,128)S(1)}, f32[584,128]{1,0:T(8,128)S(1)}, u32[]{:S(2)}, u32[]{:S(2)}) collective-permute-start(f32[584,128]{1,0:T(8,128)S(1)} %get-tuple-element.16.text), channel_id=1, source_target_pairs={{0,16},{16,0},{1,17},{17,1},{2,18},{18,2},{3,19},{19,3},{4,20},{20... | collective-permute-start | bytes 897032 | tf_op jit(solution)/shard_map/ppermute | solution.py:55
  25.0 7.2 %collective-permute-start.1 = (f32[264,128]{1,0:T(8,128)S(1)}, f32[264,128]{1,0:T(8,128)S(1)}, u32[]{:S(2)}, u32[]{:S(2)}) collective-permute-start(f32[264,128]{1,0:T(8,128)S(1)} %get-tuple-element.19.own), channel_id=1, source_target_pairs={{0,12},{12,0},{4,8},{8,4},{1,13},{13,1},{5,9},{9,5},{2,14},{14,2},... | collective-permute-start | bytes 405512 | tf_op jit(solution)/shard_map/ppermute | solution.py:59
  28.8 6.1 %collective-permute-start.2 = (f32[264,128]{1,0:T(8,128)S(1)}, f32[264,128]{1,0:T(8,128)S(1)}, u32[]{:S(2)}, u32[]{:S(2)}) collective-permute-start(f32[264,128]{1,0:T(8,128)S(1)} %get-tuple-element.20.far), channel_id=1, source_target_pairs={{0,12},{12,0},{4,8},{8,4},{1,13},{13,1},{5,9},{9,5},{2,14},{14,2},... | collective-permute-start | bytes 405512 | tf_op jit(solution)/shard_map/ppermute | solution.py:59
  35.6 2.5 %collective-permute-start.3 = (f32[576,128]{1,0:T(8,128)S(1)}, f32[576,128]{1,0:T(8,128)S(1)}, u32[]{:S(2)}, u32[]{:S(2)}) collective-permute-start(f32[576,128]{1,0:T(8,128)S(1)} %get-tuple-element.25), channel_id=1, source_target_pairs={{0,16},{16,0},{1,17},{17,1},{2,18},{18,2},{3,19},{19,3},{4,20},{20... | collective-permute-start | bytes 884744 | tf_op jit(solution)/shard_map/ppermute | solution.py:55

commit v7 on v5

--- a/solution.py
+++ b/solution.py
@@ -21,6 +21,7 @@
 OPPOSITE = 22
 STRIP = 8 * TRIO
 DEPTH = 4 * STRIP
+SENT = DEPTH // 3
 AXES = ("x", "c", "z", "y")
 
 
@@ -30,7 +31,10 @@
         for half in range(2):
             peers = [p ^ (core * OPPOSITE) for p in range(PEERS)]
             groups.append(
-                [((q // 8 * 2 + core) * 4 + half * 2 + q // 4 % 2) * 4 + q % 4 for q in peers]
+                [
+                    ((q // 8 * 2 + core) * 4 + (3 - q // 4 % 2 if half else q // 4 % 2)) * 4 + q % 4
+                    for q in peers
+                ]
             )
     return groups
 
@@ -53,7 +57,7 @@
 
 
 def other_half(x):
-    return lax.ppermute(x, "z", [(0, 2), (2, 0), (1, 3), (3, 1)])
+    return lax.ppermute(x, "z", [(0, 3), (3, 0), (1, 2), (2, 1)])
 
 
 def joined(x, axis, left):
@@ -63,10 +67,12 @@
 
 
 def product(first, second, axis):
+    return joined_product(joined(first, axis, True), second, axis)
+
+
+def joined_product(left, second, axis):
     dims = (((axis,), (0,)), ((), ()))
-    return lax.dot_general(
-        joined(first, axis, True), joined(second, 0, False), dims, preferred_element_type=F32
-    )
+    return lax.dot_general(left, joined(second, 0, False), dims, preferred_element_type=F32)
 
 
 def squares(x):
@@ -176,67 +182,88 @@
         axis=0,
     )
     image_out[...] = image
-    image_squares = squares(image)
     owner = jnp.concatenate([b[54:55, :WIDE] for b in blocks], axis=1)
-    extra[...] = jnp.concatenate([owner, jnp.zeros((7, ROWS), F32)], axis=0)
+    extra[...] = jnp.concatenate([owner, squares(image), jnp.zeros((6, ROWS), F32)], axis=0)
     part[:ROWS] = product(image, text[:DEPTH], 0)
-    part[ROWS:] = jnp.concatenate(
-        [
-            text[DEPTH : DEPTH + 1],
-            image_squares[:, :128],
-            image_squares[:, 128:],
-            jnp.zeros((5, 128), F32),
-        ],
-        axis=0,
-    )
-
-
-def far_kernel(image, text_far, text_out, part):
+    part[ROWS:] = text[DEPTH:]
+
+
+def far_kernel(image, extra, text_far, text_out, part):
     text = other_order(text_far[:DEPTH])
     text_out[:DEPTH] = text
     text_out[DEPTH:] = text_far[DEPTH:]
     part[:ROWS] = product(image[...], text, 0)
-    part[ROWS:] = text_far[DEPTH:]
-
-
-def pair_kernel(
-    log_scale, bias, image, extra, text, text_far, own, own_more, far, far_more, sent, mixed, factors
-):
-    scale = jnp.exp(jnp.full((1, 1), log_scale[0], F32))
-    raw = jnp.concatenate(
-        [own[:ROWS] + own_more[:ROWS], far[:ROWS] + far_more[:ROWS]], axis=1
-    )
-    own_sums = own[ROWS:] + own_more[ROWS:]
-    far_sums = far[ROWS:] + far_more[ROWS:]
-    image_sums = jnp.concatenate([own_sums[1:2], own_sums[2:3]], axis=1)
-    image_inv = lax.rsqrt(image_sums + EPSILON)
-    text_inv = lax.rsqrt(jnp.concatenate([own_sums[0:1], far_sums[0:1]], axis=1) + EPSILON)
-    text_owner = jnp.concatenate(
-        [text[DEPTH + 1 : DEPTH + 2], text_far[DEPTH + 1 : DEPTH + 2]], axis=1
-    )
-    turned = jnp.concatenate([image_inv, extra[0:1], jnp.zeros((6, ROWS), F32)], axis=0).T
+    part[ROWS:] = jnp.concatenate(
+        [
+            text_far[DEPTH : DEPTH + 1],
+            extra[1:2, :128],
+            extra[1:2, 128:],
+            jnp.zeros((5, 128), F32),
+        ],
+        axis=0,
+    )
+
+
+def left_kernel(image, text, text_far, image_left, text_left, far_left):
+    image_left[...] = joined(image[...], 1, True)
+    text_left[...] = joined(text[:DEPTH], 1, True)
+    far_left[...] = joined(text_far[:DEPTH], 1, True)
+
+
+def pair_grads(scale, bias, part, more, image_inv, image_owner, text_owner):
+    text_inv = lax.rsqrt(part[ROWS : ROWS + 1] + more[ROWS : ROWS + 1] + EPSILON)
+    turned = jnp.concatenate([image_inv, image_owner, jnp.zeros((6, ROWS), F32)], axis=0).T
     inv = turned[:, 0:1] * text_inv
-    cosines = raw * inv
+    cosines = (part[:ROWS] + more[:ROWS]) * inv
     labels = jnp.where(turned[:, 1:2] == text_owner, 1.0, -1.0)
-    logits = scale * cosines + bias[0]
+    logits = scale * cosines + bias
     grads = scale * (-labels * jax.nn.sigmoid(-labels * logits))
     weighted = grads * cosines
     text_dot = jnp.sum(weighted, axis=0, keepdims=True)
     image_dot = jnp.broadcast_to(jnp.sum(weighted, axis=1, keepdims=True), (ROWS, 128)).T[0:1]
-    both = grads * inv
-    text_factor = text_inv * text_inv * text_dot
+    return grads * inv, text_inv * text_inv * text_dot, image_dot
+
+
+def far_grad_kernel(
+    log_scale, bias, extra, image_left, text_far, part, more, near, sent0, sent1, sent2, mixed, factors
+):
+    scale = jnp.exp(jnp.full((1, 1), log_scale[0], F32))
+    sums = part[ROWS + 1 : ROWS + 3] + more[ROWS + 1 : ROWS + 3]
+    image_inv = lax.rsqrt(jnp.concatenate([sums[0:1], sums[1:2]], axis=1) + EPSILON)
+    text_owner = text_far[DEPTH + 1 : DEPTH + 2]
+    both, text_factor, image_dot = pair_grads(
+        scale, bias[0], part, more, image_inv, extra[0:1], text_owner
+    )
+    grad = joined_product(image_left[...], both, 1) - text_far[:DEPTH] * text_factor
+    grad = other_order(grad)
+    for g, sent in enumerate((sent0, sent1, sent2)):
+        sent[...] = grad[g * SENT : (g + 1) * SENT]
     mixed[...] = both
     factors[...] = jnp.concatenate(
-        [image_inv * image_inv * image_dot, text_factor, jnp.zeros((6, ROWS), F32)], axis=0
-    )
-    far_grad = product(image[...], both[:, 128:], 1) - text_far[:DEPTH] * text_factor[:, 128:]
-    sent[...] = other_order(far_grad)
-
-
-def own_kernel(image, text, text_far, mixed, factors, image_out, text_out):
-    texts = jnp.concatenate([text[:DEPTH], text_far[:DEPTH]], axis=1)
-    image_grad = product(texts, mixed[...].T, 1) - image[...] * factors[0:1]
-    text_out[...] = product(image[...], mixed[:, :128], 1) - text[:DEPTH] * factors[1:2, :128]
+        [image_inv, image_dot, jnp.broadcast_to(scale, (1, ROWS)), jnp.zeros((5, ROWS), F32)],
+        axis=0,
+    )
+
+
+def near_grad_kernel(
+    bias, image, extra, image_left, text_left, text, part, more, far_left, far_mixed, factors, image_out, text_out
+):
+    image_inv = factors[0:1]
+    both, text_factor, image_dot = pair_grads(
+        factors[2:3, :128],
+        bias[0],
+        part,
+        more,
+        image_inv,
+        extra[0:1],
+        text[DEPTH + 1 : DEPTH + 2],
+    )
+    image_dot = image_dot + factors[1:2]
+    image_grad = joined_product(text_left[...], both.T, 1) + joined_product(
+        far_left[...], far_mixed[...].T, 1
+    )
+    image_grad = image_grad - image[...] * (image_inv * image_inv * image_dot)
+    text_out[...] = joined_product(image_left[...], both, 1) - text[:DEPTH] * text_factor
     for x in range(4):
         own = slice(x * WIDE, (x + 1) * WIDE)
         for e in range(2):
@@ -249,9 +276,10 @@
             )
 
 
-def join_kernel(image_grad, text_grad, received, out):
+def join_kernel(image_grad, text_grad, first, second, third, out):
     core = lax.axis_index("c")
-    text = text_grad[...] + received[...]
+    received = jnp.concatenate([first[...], second[...], third[...]], axis=0)
+    text = text_grad[...] + received
     for x in range(4):
         own = slice(x * THIN, (x + 1) * THIN)
         thin = jnp.concatenate(
@@ -267,8 +295,9 @@
     core = lax.axis_index("c")
     size = 8 * BACK_ROWS
     blocks = [pieces[x * size : (x + 1) * size] for x in range(4)]
+    folded = [b[: size // 2] + b[size // 2 :] for b in blocks]
     wides = [
-        sum(b[t * BACK_ROWS : t * BACK_ROWS + 36] for t in range(8)) for b in blocks
+        sum(b[t * BACK_ROWS : t * BACK_ROWS + 36] for t in range(4)) for b in folded
     ]
     total = sum(blocks)
     thins = [total[t * BACK_ROWS + 36 : (t + 1) * BACK_ROWS] for t in range(8)]
@@ -290,18 +319,17 @@
         )
 
 
-def call(kernel, outs, args, scalars=0, flops=0, **more):
+def call(kernel, outs, args, scalars=0, types=None, **more):
     smem = [pl.BlockSpec(memory_space=pltpu.SMEM)] * scalars
     vmem = [pl.BlockSpec(memory_space=pltpu.VMEM)] * (len(args) - scalars)
+    types = types or [F32] * len(outs)
     return pl.pallas_call(
         kernel,
-        out_shape=[jax.ShapeDtypeStruct(s, F32) for s in outs],
+        out_shape=[jax.ShapeDtypeStruct(s, t) for s, t in zip(outs, types)],
         in_specs=more.pop("in_specs", smem + vmem),
         out_specs=[pl.BlockSpec(memory_space=pltpu.VMEM)] * len(outs),
         compiler_params=pltpu.CompilerParams(vmem_limit_bytes=40 * 1024 * 1024),
-        cost_estimate=pl.CostEstimate(
-            flops=flops, bytes_accessed=3000000, transcendentals=0
-        ),
+        cost_estimate=pl.CostEstimate(flops=0, bytes_accessed=1000, transcendentals=0),
         **more,
     )(*args)
 
@@ -327,28 +355,47 @@
     held = exchange(packed)
     (text,) = call(text_kernel, [(DEPTH + 8, 128)], (held,))
     text_received = other_core(text)
-    image, extra, own = call(
+    image, extra, near = call(
         image_kernel, [(DEPTH, ROWS), (8, ROWS), (ROWS + 8, 128)], (held, text)
     )
-    own_more = other_half(own)
     text_far, far = call(
-        far_kernel, [(DEPTH + 8, 128), (ROWS + 8, 128)], (image, text_received)
+        far_kernel, [(DEPTH + 8, 128), (ROWS + 8, 128)], (image, extra, text_received)
     )
     far_more = other_half(far)
-    sent, mixed, factors = call(
-        pair_kernel,
-        [(DEPTH, 128), (ROWS, ROWS), (8, ROWS)],
-        (log_scale, bias, image, extra, text, text_far, own, own_more, far, far_more),
+    near_more = other_half(near)
+    image_left, text_left, far_left = call(
+        left_kernel,
+        [(DEPTH, 3 * ROWS), (DEPTH, 3 * 128), (DEPTH, 3 * 128)],
+        (image, text, text_far),
+        types=[BF16] * 3,
+    )
+    *sent, mixed, factors = call(
+        far_grad_kernel,
+        [(SENT, 128)] * 3 + [(ROWS, 128), (8, ROWS)],
+        (log_scale, bias, extra, image_left, text_far, far, far_more, near),
         scalars=2,
     )
-    received = other_core(sent)
+    received = [other_core(x) for x in sent]
     image_grad, text_grad = call(
-        own_kernel,
+        near_grad_kernel,
         [(4, 2, STRIP, 128), (DEPTH, 128)],
-        (image, text, text_far, mixed, factors),
+        (
+            bias,
+            image,
+            extra,
+            image_left,
+            text_left,
+            text,
+            near,
+            near_more,
+            far_left,
+            mixed,
+            factors,
+        ),
+        scalars=1,
     )
     (grads,) = call(
-        join_kernel, [(PEERS * BACK_ROWS, 128)], (image_grad, text_grad, received)
+        join_kernel, [(PEERS * BACK_ROWS, 128)], (image_grad, text_grad, *received)
     )
     back = exchange(grads)
     image_result, text_result = call(sum_kernel, [(FEATS, ROWS)] * 2, (back,))

time: 58.6 us -> 56.4 us (0.962)
  waiting for transfers between devices: 5.03 us -> 2.79 us
    ppermute x2, waiting for transfers between devices: 4.61 us -> 2.24 us  [other_half(): return lax.ppermute(x, 'z', [(0, 3), (3, 0), (1, 2), (2, 1)])]
    ppermute x2 -> x4, starting transfers between devices: 3.05 us -> 3.47 us  [other_core(): return lax.ppermute(x, 'c', [(0, 1), (1, 0)])]
    pallas_call x8 -> x9, Pallas kernels: 5.29 us -> 5.57 us  [call(): pl.pallas_call(kernel, out_shape=[jax.ShapeDtypeStruct(s, t) for s, t in...]
  transfers between devices with their start and end apart: 4 -> 6, of which waited for: 3 -> 3; matrix products, arithmetic and copies ran while one was open for 0% -> 0% of each run, Pallas kernels for 3% -> 4%
where the time goes in v7:
time: 56.4 us; the launch traced here: 56.2 us
  blocking collectives  38.8 us (69%)
  starting transfers between devices  7.01 us (12%)
  Pallas kernels  5.57 us (10%)
  waiting for transfers between devices  2.79 us (5%)
  between operations  2.01 us (4%)
    all_to_all x2, blocking collectives, exchange(): lax.all_to_all(pieces.reshape(PEERS, rows, 1, 128), AXES, 0, 0, axis_inde...  38.8 us
    pallas_call x9, Pallas kernels, call(): pl.pallas_call(kernel, out_shape=[jax.ShapeDtypeStruct(s, t) for s, t in...  5.57 us
    ppermute x2, starting transfers between devices, other_half(): return lax.ppermute(x, 'z', [(0, 3), (3, 0), (1, 2), (2, 1)])  3.54 us
    ppermute x4, starting transfers between devices, other_core(): return lax.ppermute(x, 'c', [(0, 1), (1, 0)])  3.47 us
    ppermute x2, waiting for transfers between devices, other_half(): return lax.ppermute(x, 'z', [(0, 3), (3, 0), (1, 2), (2, 1)])  2.24 us
  transfers between devices with their start and end apart: 6, of which 3 were waited for; matrix products, arithmetic and copies ran while one was open for 0% of the time, Pallas kernels for 4%

profile of v7, /device:TPU:1, one launch (start us, length us, event | category | flops | bytes accessed | tf_op | source)
XLA Modules:
  0.0 56.2 jit_solution(7807662696234544029)
XLA Ops:
  0.6 1.2 %shard_map.77 = f32[1760,128]{1,0:T(8,128)S(1)} custom-call(f32[72,256]{1,0:T(8,128)} %bitcast.15, f32[72,256]{1,0:T(8,128)} %bitcast.16, s32[1,256]{1,0:T(1,128)} %bitcast.17, s32[1,256]{1,0:T(1,128)} %bitcast.18), custom_call_target="tpu_custom_call" | custom-call | bytes 1000 | tf_op jit(solution)/shard_map/pallas_call | solution.py:326
  1.8 20.4 %all_to_all.10 = f32[32,55,1,128]{3,2,1,0:T(1,128)S(1)} all-to-all(f32[32,55,1,128]{3,2,1,0:T(1,128)S(1)} %bitcast.12), channel_id=1, replica_groups={{0,1,2,3,4,5,6,7,32,33,34,35,36,37,38,39,64,65,66,67,68,69,70,71,96,97,..., dimensions={0} | all-to-all | bytes 1802240 | tf_op jit(solution)/shard_map/all_to_all | solution.py:44
  22.2 0.3 shard_map.78.text
  22.6 1.8 %collective-permute-start = (f32[584,128]{1,0:T(8,128)S(1)}, f32[584,128]{1,0:T(8,128)S(1)}, u32[]{:S(2)}, u32[]{:S(2)}) collective-permute-start(f32[584,128]{1,0:T(8,128)S(1)} %shard_map.78.text), channel_id=1, source_target_pairs={{0,16},{16,0},{1,17},{17,1},{2,18},{18,2},{3,19},{19,3},{4,20},{20... | collective-permute-start | bytes 897032 | tf_op jit(solution)/shard_map/ppermute | solution.py:56
  24.4 0.7 %shard_map.79 = (f32[576,256]{1,0:T(8,128)S(1)}, f32[8,256]{1,0:T(8,128)S(1)}, f32[264,128]{1,0:T(8,128)S(1)}) custom-call(f32[1760,128]{1,0:T(8,128)S(1)} %bitcast.11, f32[584,128]{1,0:T(8,128)S(1)} %shard_map.78.text), custom_call_target="tpu_custom_call" | custom-call | bytes 1000 | tf_op jit(solution)/shard_map/pallas_call | solution.py:326
  25.1 0.5 collective-permute-done.text_far
  25.6 0.5 shard_map.80
  26.1 3.4 %collective-permute-start.2 = (f32[264,128]{1,0:T(8,128)S(1)}, f32[264,128]{1,0:T(8,128)S(1)}, u32[]{:S(2)}, u32[]{:S(2)}) collective-permute-start(f32[264,128]{1,0:T(8,128)S(1)} %get-tuple-element.26.part), channel_id=1, source_target_pairs={{0,12},{12,0},{4,8},{8,4},{1,13},{13,1},{5,9},{9,5},{2,14},{14,2},... | collective-permute-start | bytes 405512 | tf_op jit(solution)/shard_map/ppermute | solution.py:60
  29.5 0.1 collective-permute-start.1
  30.9 0.2 shard_map.81
  31.1 2.1 %collective-permute-done.2.more = f32[264,128]{1,0:T(8,128)S(1)} collective-permute-done((f32[264,128]{1,0:T(8,128)S(1)}, f32[264,128]{1,0:T(8,128)S(1)}, u32[]{:S(2)}, u32[]{:S(2)}) %collective-permute-start.2) | collective-permute-done | bytes 135200 | tf_op jit(solution)/shard_map/ppermute | solution.py:60
  33.2 0.7 %shard_map.82 = (f32[192,128]{1,0:T(8,128)S(1)}, f32[192,128]{1,0:T(8,128)S(1)}, f32[192,128]{1,0:T(8,128)S(1)}, f32[256,128]{1,0:T(8,128)S(1)}, f32[8,256]{1,0:T(8,128)S(1)}) custom-call(f32[1]{0:T(128)S(6)} %copy.10.log_scale, f32[1]{0:T(128)S(6)} %copy.11.bias, f32[8,256]{1,0:T(8,128)S(1)} %get-tuple-element.20.extra, ...), custom_call_target="tpu_custom_call" | custom-call | bytes 1000 | tf_op jit(solution)/shard_map/pallas_call | solution.py:326
  33.9 1.1 %collective-permute-start.3 = (f32[192,128]{1,0:T(8,128)S(1)}, f32[192,128]{1,0:T(8,128)S(1)}, u32[]{:S(2)}, u32[]{:S(2)}) collective-permute-start(f32[192,128]{1,0:T(8,128)S(1)} %get-tuple-element.31), channel_id=1, source_target_pairs={{0,16},{16,0},{1,17},{17,1},{2,18},{18,2},{3,19},{19,3},{4,20},{20... | collective-permute-start | bytes 294920 | tf_op jit(solution)/shard_map/ppermute | solution.py:56
  35.0 0.1 collective-permute-start.4
  35.1 0.4 collective-permute-start.5
  35.5 0.2 collective-permute-done.1.more
  35.6 0.9 %shard_map.83 = (f32[4,2,144,128]{3,2,1,0:T(8,128)S(1)}, f32[576,128]{1,0:T(8,128)S(1)}) custom-call(f32[1]{0:T(128)S(6)} %copy.11.bias, f32[576,256]{1,0:T(8,128)S(1)} %get-tuple-element.19.image, f32[8,256]{1,0:T(8,128)S(1)} %get-tuple-element.20.extra, bf16[576,768]{1,0:T(8,128)(2,1)S(1)} %get-tuple-element.22.image_left, ...), custom_call_target="tpu_custom_call" | custom-call | bytes 1000 | tf_op jit(solution)/shard_map/pallas_call | solution.py:326
  36.6 0.0 collective-permute-done.3.first
  36.6 0.0 collective-permute-done.4.second
  36.6 0.0 collective-permute-done.5.third
  36.6 0.3 shard_map.84
  36.9 18.4 %all_to_all.11 = f32[32,54,1,128]{3,2,1,0:T(1,128)S(1)} all-to-all(f32[32,54,1,128]{3,2,1,0:T(1,128)S(1)} %bitcast.14), channel_id=1, replica_groups={{0,1,2,3,4,5,6,7,32,33,34,35,36,37,38,39,64,65,66,67,68,69,70,71,96,97,..., dimensions={0} | all-to-all | bytes 1769472 | tf_op jit(solution)/shard_map/all_to_all | solution.py:44
  55.3 0.9 %shard_map.85 = (f32[72,256]{1,0:T(8,128)}, f32[72,256]{1,0:T(8,128)}) custom-call(f32[1728,128]{1,0:T(8,128)S(1)} %bitcast.13), custom_call_target="tpu_custom_call" | custom-call | bytes 1000 | tf_op jit(solution)/shard_map/pallas_call | solution.py:326
Async XLA Ops:
  22.6 3.1 %collective-permute-start = (f32[584,128]{1,0:T(8,128)S(1)}, f32[584,128]{1,0:T(8,128)S(1)}, u32[]{:S(2)}, u32[]{:S(2)}) collective-permute-start(f32[584,128]{1,0:T(8,128)S(1)} %shard_map.78.text), channel_id=1, source_target_pairs={{0,16},{16,0},{1,17},{17,1},{2,18},{18,2},{3,19},{19,3},{4,20},{20... | collective-permute-start | bytes 897032 | tf_op jit(solution)/shard_map/ppermute | solution.py:56
  26.1 7.1 %collective-permute-start.2 = (f32[264,128]{1,0:T(8,128)S(1)}, f32[264,128]{1,0:T(8,128)S(1)}, u32[]{:S(2)}, u32[]{:S(2)}) collective-permute-start(f32[264,128]{1,0:T(8,128)S(1)} %get-tuple-element.26.part), channel_id=1, source_target_pairs={{0,12},{12,0},{4,8},{8,4},{1,13},{13,1},{5,9},{9,5},{2,14},{14,2},... | collective-permute-start | bytes 405512 | tf_op jit(solution)/shard_map/ppermute | solution.py:60
  29.5 6.1 %collective-permute-start.1 = (f32[264,128]{1,0:T(8,128)S(1)}, f32[264,128]{1,0:T(8,128)S(1)}, u32[]{:S(2)}, u32[]{:S(2)}) collective-permute-start(f32[264,128]{1,0:T(8,128)S(1)} %get-tuple-element.24.near.part), channel_id=1, source_target_pairs={{0,12},{12,0},{4,8},{8,4},{1,13},{13,1},{5,9},{9,5},{2,14},{14,2},... | collective-permute-start | bytes 405512 | tf_op jit(solution)/shard_map/ppermute | solution.py:60
  33.9 2.7 %collective-permute-start.3 = (f32[192,128]{1,0:T(8,128)S(1)}, f32[192,128]{1,0:T(8,128)S(1)}, u32[]{:S(2)}, u32[]{:S(2)}) collective-permute-start(f32[192,128]{1,0:T(8,128)S(1)} %get-tuple-element.31), channel_id=1, source_target_pairs={{0,16},{16,0},{1,17},{17,1},{2,18},{18,2},{3,19},{19,3},{4,20},{20... | collective-permute-start | bytes 294920 | tf_op jit(solution)/shard_map/ppermute | solution.py:56
  35.0 1.6 %collective-permute-start.4 = (f32[192,128]{1,0:T(8,128)S(1)}, f32[192,128]{1,0:T(8,128)S(1)}, u32[]{:S(2)}, u32[]{:S(2)}) collective-permute-start(f32[192,128]{1,0:T(8,128)S(1)} %get-tuple-element.32), channel_id=1, source_target_pairs={{0,16},{16,0},{1,17},{17,1},{2,18},{18,2},{3,19},{19,3},{4,20},{20... | collective-permute-start | bytes 294920 | tf_op jit(solution)/shard_map/ppermute | solution.py:56
  35.1 1.5 %collective-permute-start.5 = (f32[192,128]{1,0:T(8,128)S(1)}, f32[192,128]{1,0:T(8,128)S(1)}, u32[]{:S(2)}, u32[]{:S(2)}) collective-permute-start(f32[192,128]{1,0:T(8,128)S(1)} %get-tuple-element.33), channel_id=1, source_target_pairs={{0,16},{16,0},{1,17},{17,1},{2,18},{18,2},{3,19},{19,3},{4,20},{20... | collective-permute-start | bytes 294920 | tf_op jit(solution)/shard_map/ppermute | solution.py:56

commit v8 on v7

--- a/solution.py
+++ b/solution.py
@@ -66,13 +66,23 @@
     return jnp.concatenate([high, high, low] if left else [high, low, high], axis=axis)
 
 
-def product(first, second, axis):
-    return joined_product(joined(first, axis, True), second, axis)
-
-
 def joined_product(left, second, axis):
     dims = (((axis,), (0,)), ((), ()))
     return lax.dot_general(left, joined(second, 0, False), dims, preferred_element_type=F32)
+
+
+def halves(x):
+    high = x.astype(BF16)
+    return high, (x - high.astype(F32)).astype(BF16)
+
+
+def turned_product(high, low, second):
+    c, d = halves(second)
+
+    def dot(p, q):
+        return jnp.dot(p, q, preferred_element_type=F32)
+
+    return dot(high, c) + (dot(high, d) + dot(low, c))
 
 
 def squares(x):
@@ -168,7 +178,7 @@
     out[DEPTH:] = jnp.concatenate([squares(text), owner, jnp.zeros((6, 128), F32)], axis=0)
 
 
-def image_kernel(pieces, text, image_out, extra, part):
+def image_kernel(pieces, text, image_out, high_out, low_out, extra, part):
     core = lax.axis_index("c")
     blocks = [pieces[block_of(x, core, IN_ROWS)] for x in range(4)]
     strips = [[strip(b, IN_ROWS, e * TRIO) for b in blocks] for e in range(2)]
@@ -184,15 +194,18 @@
     image_out[...] = image
     owner = jnp.concatenate([b[54:55, :WIDE] for b in blocks], axis=1)
     extra[...] = jnp.concatenate([owner, squares(image), jnp.zeros((6, ROWS), F32)], axis=0)
-    part[:ROWS] = product(image, text[:DEPTH], 0)
+    high, low = halves(image.T)
+    high_out[...] = high
+    low_out[...] = low
+    part[:ROWS] = turned_product(high, low, text[:DEPTH])
     part[ROWS:] = text[DEPTH:]
 
 
-def far_kernel(image, extra, text_far, text_out, part):
+def far_kernel(image_high, image_low, extra, text_far, text_out, part):
     text = other_order(text_far[:DEPTH])
     text_out[:DEPTH] = text
     text_out[DEPTH:] = text_far[DEPTH:]
-    part[:ROWS] = product(image[...], text, 0)
+    part[:ROWS] = turned_product(image_high[...], image_low[...], text)
     part[ROWS:] = jnp.concatenate(
         [
             text_far[DEPTH : DEPTH + 1],
@@ -355,11 +368,16 @@
     held = exchange(packed)
     (text,) = call(text_kernel, [(DEPTH + 8, 128)], (held,))
     text_received = other_core(text)
-    image, extra, near = call(
-        image_kernel, [(DEPTH, ROWS), (8, ROWS), (ROWS + 8, 128)], (held, text)
+    image, image_high, image_low, extra, near = call(
+        image_kernel,
+        [(DEPTH, ROWS), (ROWS, DEPTH), (ROWS, DEPTH), (8, ROWS), (ROWS + 8, 128)],
+        (held, text),
+        types=[F32, BF16, BF16, F32, F32],
     )
     text_far, far = call(
-        far_kernel, [(DEPTH + 8, 128), (ROWS + 8, 128)], (image, extra, text_received)
+        far_kernel,
+        [(DEPTH + 8, 128), (ROWS + 8, 128)],
+        (image_high, image_low, extra, text_received),
     )
     far_more = other_half(far)
     near_more = other_half(near)

time: 56.4 us -> 56.4 us (level)
  no operation moved by 1% of the time
where the time goes in v8:
time: 56.4 us; the launch traced here: 56.2 us
  blocking collectives  38.8 us (69%)
  starting transfers between devices  7.01 us (12%)
  Pallas kernels  5.59 us (10%)
  waiting for transfers between devices  2.73 us (5%)
  between operations  2.01 us (4%)
    all_to_all x2, blocking collectives, exchange(): lax.all_to_all(pieces.reshape(PEERS, rows, 1, 128), AXES, 0, 0, axis_inde...  38.8 us
    pallas_call x9, Pallas kernels, call(): pl.pallas_call(kernel, out_shape=[jax.ShapeDtypeStruct(s, t) for s, t in...  5.59 us
    ppermute x2, starting transfers between devices, other_half(): return lax.ppermute(x, 'z', [(0, 3), (3, 0), (1, 2), (2, 1)])  3.54 us
    ppermute x4, starting transfers between devices, other_core(): return lax.ppermute(x, 'c', [(0, 1), (1, 0)])  3.47 us
    ppermute x2, waiting for transfers between devices, other_half(): return lax.ppermute(x, 'z', [(0, 3), (3, 0), (1, 2), (2, 1)])  2.24 us
  transfers between devices with their start and end apart: 6, of which 3 were waited for; matrix products, arithmetic and copies ran while one was open for 0% of the time, Pallas kernels for 4%

profile of v8, /device:TPU:1, one launch (start us, length us, event | category | flops | bytes accessed | tf_op | source)
XLA Modules:
  0.0 56.2 jit_solution(2178311706619154879)
XLA Ops:
  0.6 1.2 %shard_map.77 = f32[1760,128]{1,0:T(8,128)S(1)} custom-call(f32[72,256]{1,0:T(8,128)} %bitcast.15, f32[72,256]{1,0:T(8,128)} %bitcast.16, s32[1,256]{1,0:T(1,128)} %bitcast.17, s32[1,256]{1,0:T(1,128)} %bitcast.18), custom_call_target="tpu_custom_call" | custom-call | bytes 1000 | tf_op jit(solution)/shard_map/pallas_call | solution.py:339
  1.8 20.4 %all_to_all.10 = f32[32,55,1,128]{3,2,1,0:T(1,128)S(1)} all-to-all(f32[32,55,1,128]{3,2,1,0:T(1,128)S(1)} %bitcast.12), channel_id=1, replica_groups={{0,1,2,3,4,5,6,7,32,33,34,35,36,37,38,39,64,65,66,67,68,69,70,71,96,97,..., dimensions={0} | all-to-all | bytes 1802240 | tf_op jit(solution)/shard_map/all_to_all | solution.py:44
  22.2 0.3 shard_map.78.text
  22.6 1.8 %collective-permute-start = (f32[584,128]{1,0:T(8,128)S(1)}, f32[584,128]{1,0:T(8,128)S(1)}, u32[]{:S(2)}, u32[]{:S(2)}) collective-permute-start(f32[584,128]{1,0:T(8,128)S(1)} %shard_map.78.text), channel_id=1, source_target_pairs={{0,16},{16,0},{1,17},{17,1},{2,18},{18,2},{3,19},{19,3},{4,20},{20... | collective-permute-start | bytes 897032 | tf_op jit(solution)/shard_map/ppermute | solution.py:56
  24.4 0.7 %shard_map.79 = (f32[576,256]{1,0:T(8,128)S(1)}, bf16[256,576]{1,0:T(8,128)(2,1)S(1)}, bf16[256,576]{1,0:T(8,128)(2,1)S(1)}, f32[8,256]{1,0:T(8,128)S(1)}, f32[264,128]{1,0:T(8,128)S(1)}) custom-call(f32[1760,128]{1,0:T(8,128)S(1)} %bitcast.11, f32[584,128]{1,0:T(8,128)S(1)} %shard_map.78.text), custom_call_target="tpu_custom_call" | custom-call | bytes 1000 | tf_op jit(solution)/shard_map/pallas_call | solution.py:339
  25.1 0.5 collective-permute-done.text_far
  25.6 0.4 shard_map.80
  26.0 3.4 %collective-permute-start.2 = (f32[264,128]{1,0:T(8,128)S(1)}, f32[264,128]{1,0:T(8,128)S(1)}, u32[]{:S(2)}, u32[]{:S(2)}) collective-permute-start(f32[264,128]{1,0:T(8,128)S(1)} %get-tuple-element.30.part), channel_id=1, source_target_pairs={{0,12},{12,0},{4,8},{8,4},{1,13},{13,1},{5,9},{9,5},{2,14},{14,2},... | collective-permute-start | bytes 405512 | tf_op jit(solution)/shard_map/ppermute | solution.py:60
  29.5 0.1 collective-permute-start.1
  30.9 0.2 shard_map.81
  31.1 2.1 %collective-permute-done.2.more = f32[264,128]{1,0:T(8,128)S(1)} collective-permute-done((f32[264,128]{1,0:T(8,128)S(1)}, f32[264,128]{1,0:T(8,128)S(1)}, u32[]{:S(2)}, u32[]{:S(2)}) %collective-permute-start.2) | collective-permute-done | bytes 135200 | tf_op jit(solution)/shard_map/ppermute | solution.py:60
  33.1 0.7 %shard_map.82 = (f32[192,128]{1,0:T(8,128)S(1)}, f32[192,128]{1,0:T(8,128)S(1)}, f32[192,128]{1,0:T(8,128)S(1)}, f32[256,128]{1,0:T(8,128)S(1)}, f32[8,256]{1,0:T(8,128)S(1)}) custom-call(f32[1]{0:T(128)S(6)} %copy.10.log_scale, f32[1]{0:T(128)S(6)} %copy.11.bias, f32[8,256]{1,0:T(8,128)S(1)} %get-tuple-element.22.extra, ...), custom_call_target="tpu_custom_call" | custom-call | bytes 1000 | tf_op jit(solution)/shard_map/pallas_call | solution.py:339
  33.8 1.1 %collective-permute-start.3 = (f32[192,128]{1,0:T(8,128)S(1)}, f32[192,128]{1,0:T(8,128)S(1)}, u32[]{:S(2)}, u32[]{:S(2)}) collective-permute-start(f32[192,128]{1,0:T(8,128)S(1)} %get-tuple-element.35), channel_id=1, source_target_pairs={{0,16},{16,0},{1,17},{17,1},{2,18},{18,2},{3,19},{19,3},{4,20},{20... | collective-permute-start | bytes 294920 | tf_op jit(solution)/shard_map/ppermute | solution.py:56
  34.9 0.1 collective-permute-start.4
  35.0 0.4 collective-permute-start.5
  35.5 0.2 collective-permute-done.1.more
  35.6 0.9 %shard_map.83 = (f32[4,2,144,128]{3,2,1,0:T(8,128)S(1)}, f32[576,128]{1,0:T(8,128)S(1)}) custom-call(f32[1]{0:T(128)S(6)} %copy.11.bias, f32[576,256]{1,0:T(8,128)S(1)} %get-tuple-element.21.image, f32[8,256]{1,0:T(8,128)S(1)} %get-tuple-element.22.extra, bf16[576,768]{1,0:T(8,128)(2,1)S(1)} %get-tuple-element.26.image_left, ...), custom_call_target="tpu_custom_call" | custom-call | bytes 1000 | tf_op jit(solution)/shard_map/pallas_call | solution.py:339
  36.5 0.0 collective-permute-done.3.first
  36.5 0.0 collective-permute-done.4.second
  36.6 0.0 collective-permute-done.5.third
  36.6 0.3 shard_map.84
  36.9 18.4 %all_to_all.11 = f32[32,54,1,128]{3,2,1,0:T(1,128)S(1)} all-to-all(f32[32,54,1,128]{3,2,1,0:T(1,128)S(1)} %bitcast.14), channel_id=1, replica_groups={{0,1,2,3,4,5,6,7,32,33,34,35,36,37,38,39,64,65,66,67,68,69,70,71,96,97,..., dimensions={0} | all-to-all | bytes 1769472 | tf_op jit(solution)/shard_map/all_to_all | solution.py:44
  55.3 0.9 %shard_map.85 = (f32[72,256]{1,0:T(8,128)}, f32[72,256]{1,0:T(8,128)}) custom-call(f32[1728,128]{1,0:T(8,128)S(1)} %bitcast.13), custom_call_target="tpu_custom_call" | custom-call | bytes 1000 | tf_op jit(solution)/shard_map/pallas_call | solution.py:339
Async XLA Ops:
  22.6 3.1 %collective-permute-start = (f32[584,128]{1,0:T(8,128)S(1)}, f32[584,128]{1,0:T(8,128)S(1)}, u32[]{:S(2)}, u32[]{:S(2)}) collective-permute-start(f32[584,128]{1,0:T(8,128)S(1)} %shard_map.78.text), channel_id=1, source_target_pairs={{0,16},{16,0},{1,17},{17,1},{2,18},{18,2},{3,19},{19,3},{4,20},{20... | collective-permute-start | bytes 897032 | tf_op jit(solution)/shard_map/ppermute | solution.py:56
  26.0 7.1 %collective-permute-start.2 = (f32[264,128]{1,0:T(8,128)S(1)}, f32[264,128]{1,0:T(8,128)S(1)}, u32[]{:S(2)}, u32[]{:S(2)}) collective-permute-start(f32[264,128]{1,0:T(8,128)S(1)} %get-tuple-element.30.part), channel_id=1, source_target_pairs={{0,12},{12,0},{4,8},{8,4},{1,13},{13,1},{5,9},{9,5},{2,14},{14,2},... | collective-permute-start | bytes 405512 | tf_op jit(solution)/shard_map/ppermute | solution.py:60
  29.5 6.1 %collective-permute-start.1 = (f32[264,128]{1,0:T(8,128)S(1)}, f32[264,128]{1,0:T(8,128)S(1)}, u32[]{:S(2)}, u32[]{:S(2)}) collective-permute-start(f32[264,128]{1,0:T(8,128)S(1)} %get-tuple-element.28.near.part), channel_id=1, source_target_pairs={{0,12},{12,0},{4,8},{8,4},{1,13},{13,1},{5,9},{9,5},{2,14},{14,2},... | collective-permute-start | bytes 405512 | tf_op jit(solution)/shard_map/ppermute | solution.py:60
  33.8 2.7 %collective-permute-start.3 = (f32[192,128]{1,0:T(8,128)S(1)}, f32[192,128]{1,0:T(8,128)S(1)}, u32[]{:S(2)}, u32[]{:S(2)}) collective-permute-start(f32[192,128]{1,0:T(8,128)S(1)} %get-tuple-element.35), channel_id=1, source_target_pairs={{0,16},{16,0},{1,17},{17,1},{2,18},{18,2},{3,19},{19,3},{4,20},{20... | collective-permute-start | bytes 294920 | tf_op jit(solution)/shard_map/ppermute | solution.py:56
  34.9 1.6 %collective-permute-start.4 = (f32[192,128]{1,0:T(8,128)S(1)}, f32[192,128]{1,0:T(8,128)S(1)}, u32[]{:S(2)}, u32[]{:S(2)}) collective-permute-start(f32[192,128]{1,0:T(8,128)S(1)} %get-tuple-element.36), channel_id=1, source_target_pairs={{0,16},{16,0},{1,17},{17,1},{2,18},{18,2},{3,19},{19,3},{4,20},{20... | collective-permute-start | bytes 294920 | tf_op jit(solution)/shard_map/ppermute | solution.py:56
  35.0 1.5 %collective-permute-start.5 = (f32[192,128]{1,0:T(8,128)S(1)}, f32[192,128]{1,0:T(8,128)S(1)}, u32[]{:S(2)}, u32[]{:S(2)}) collective-permute-start(f32[192,128]{1,0:T(8,128)S(1)} %get-tuple-element.37), channel_id=1, source_target_pairs={{0,16},{16,0},{1,17},{17,1},{2,18},{18,2},{3,19},{19,3},{4,20},{20... | collective-permute-start | bytes 294920 | tf_op jit(solution)/shard_map/ppermute | solution.py:56

commit v9 on v7

--- a/solution.py
+++ b/solution.py
@@ -168,7 +168,7 @@
     out[DEPTH:] = jnp.concatenate([squares(text), owner, jnp.zeros((6, 128), F32)], axis=0)
 
 
-def image_kernel(pieces, text, image_out, extra, part):
+def image_kernel(pieces, image_out, extra):
     core = lax.axis_index("c")
     blocks = [pieces[block_of(x, core, IN_ROWS)] for x in range(4)]
     strips = [[strip(b, IN_ROWS, e * TRIO) for b in blocks] for e in range(2)]
@@ -184,8 +184,6 @@
     image_out[...] = image
     owner = jnp.concatenate([b[54:55, :WIDE] for b in blocks], axis=1)
     extra[...] = jnp.concatenate([owner, squares(image), jnp.zeros((6, ROWS), F32)], axis=0)
-    part[:ROWS] = product(image, text[:DEPTH], 0)
-    part[ROWS:] = text[DEPTH:]
 
 
 def far_kernel(image, extra, text_far, text_out, part):
@@ -204,6 +202,11 @@
     )
 
 
+def near_kernel(image, text, part):
+    part[:ROWS] = product(image[...], text[:DEPTH], 0)
+    part[ROWS:] = text[DEPTH:]
+
+
 def left_kernel(image, text, text_far, image_left, text_left, far_left):
     image_left[...] = joined(image[...], 1, True)
     text_left[...] = joined(text[:DEPTH], 1, True)
@@ -225,7 +228,7 @@
 
 
 def far_grad_kernel(
-    log_scale, bias, extra, image_left, text_far, part, more, near, sent0, sent1, sent2, mixed, factors
+    log_scale, bias, extra, image_left, text_far, part, more, sent0, sent1, sent2, mixed, factors
 ):
     scale = jnp.exp(jnp.full((1, 1), log_scale[0], F32))
     sums = part[ROWS + 1 : ROWS + 3] + more[ROWS + 1 : ROWS + 3]
@@ -355,9 +358,8 @@
     held = exchange(packed)
     (text,) = call(text_kernel, [(DEPTH + 8, 128)], (held,))
     text_received = other_core(text)
-    image, extra, near = call(
-        image_kernel, [(DEPTH, ROWS), (8, ROWS), (ROWS + 8, 128)], (held, text)
-    )
+    image, extra = call(image_kernel, [(DEPTH, ROWS), (8, ROWS)], (held,))
+    (near,) = call(near_kernel, [(ROWS + 8, 128)], (image, text))
     text_far, far = call(
         far_kernel, [(DEPTH + 8, 128), (ROWS + 8, 128)], (image, extra, text_received)
     )
@@ -372,7 +374,7 @@
     *sent, mixed, factors = call(
         far_grad_kernel,
         [(SENT, 128)] * 3 + [(ROWS, 128), (8, ROWS)],
-        (log_scale, bias, extra, image_left, text_far, far, far_more, near),
+        (log_scale, bias, extra, image_left, text_far, far, far_more),
         scalars=2,
     )
     received = [other_core(x) for x in sent]

time: 56.4 us -> 56.4 us (level)
  blocking collectives: 38.8 us -> 38.2 us
    all_to_all x2, blocking collectives: 38.8 us -> 38.2 us  [exchange(): lax.all_to_all(pieces.reshape(PEERS, rows, 1, 128), AXES, 0, 0, axis_inde...]
    pallas_call x9 -> x10, Pallas kernels: 5.57 us -> 5.59 us  [call(): pl.pallas_call(kernel, out_shape=[jax.ShapeDtypeStruct(s, t) for s, t in...]
where the time goes in v9:
time: 56.4 us; the launch traced here: 55.7 us
  blocking collectives  38.2 us (68%)
  starting transfers between devices  6.91 us (12%)
  Pallas kernels  5.59 us (10%)
  waiting for transfers between devices  2.96 us (5%)
  between operations  2.01 us (4%)
    all_to_all x2, blocking collectives, exchange(): lax.all_to_all(pieces.reshape(PEERS, rows, 1, 128), AXES, 0, 0, axis_inde...  38.2 us
    pallas_call x10, Pallas kernels, call(): pl.pallas_call(kernel, out_shape=[jax.ShapeDtypeStruct(s, t) for s, t in...  5.59 us
    ppermute x2, starting transfers between devices, other_half(): return lax.ppermute(x, 'z', [(0, 3), (3, 0), (1, 2), (2, 1)])  3.54 us
    ppermute x4, starting transfers between devices, other_core(): return lax.ppermute(x, 'c', [(0, 1), (1, 0)])  3.37 us
    ppermute x2, waiting for transfers between devices, other_half(): return lax.ppermute(x, 'z', [(0, 3), (3, 0), (1, 2), (2, 1)])  1.97 us
  transfers between devices with their start and end apart: 6, of which 3 were waited for; matrix products, arithmetic and copies ran while one was open for 0% of the time, Pallas kernels for 4%

profile of v9, /device:TPU:1, one launch (start us, length us, event | category | flops | bytes accessed | tf_op | source)
XLA Modules:
  0.0 55.7 jit_solution(7989572806221644889)
XLA Ops:
  0.6 1.2 %shard_map.77 = f32[1760,128]{1,0:T(8,128)S(1)} custom-call(f32[72,256]{1,0:T(8,128)} %bitcast.15, f32[72,256]{1,0:T(8,128)} %bitcast.16, s32[1,256]{1,0:T(1,128)} %bitcast.17, s32[1,256]{1,0:T(1,128)} %bitcast.18), custom_call_target="tpu_custom_call" | custom-call | bytes 1000 | tf_op jit(solution)/shard_map/pallas_call | solution.py:329
  1.8 20.4 %all_to_all.10 = f32[32,55,1,128]{3,2,1,0:T(1,128)S(1)} all-to-all(f32[32,55,1,128]{3,2,1,0:T(1,128)S(1)} %bitcast.12), channel_id=1, replica_groups={{0,1,2,3,4,5,6,7,32,33,34,35,36,37,38,39,64,65,66,67,68,69,70,71,96,97,..., dimensions={0} | all-to-all | bytes 1802240 | tf_op jit(solution)/shard_map/all_to_all | solution.py:44
  22.2 0.3 shard_map.79.text
  22.6 1.8 %collective-permute-start = (f32[584,128]{1,0:T(8,128)S(1)}, f32[584,128]{1,0:T(8,128)S(1)}, u32[]{:S(2)}, u32[]{:S(2)}) collective-permute-start(f32[584,128]{1,0:T(8,128)S(1)} %shard_map.79.text), channel_id=1, source_target_pairs={{0,16},{16,0},{1,17},{17,1},{2,18},{18,2},{3,19},{19,3},{4,20},{20... | collective-permute-start | bytes 897032 | tf_op jit(solution)/shard_map/ppermute | solution.py:56
  24.4 0.2 shard_map.78
  24.6 1.0 %collective-permute-done.text_far = f32[584,128]{1,0:T(8,128)S(1)} collective-permute-done((f32[584,128]{1,0:T(8,128)S(1)}, f32[584,128]{1,0:T(8,128)S(1)}, u32[]{:S(2)}, u32[]{:S(2)}) %collective-permute-start) | collective-permute-done | bytes 299040 | tf_op jit(solution)/shard_map/ppermute | solution.py:56
  25.6 0.4 shard_map.80
  26.1 3.4 %collective-permute-start.2 = (f32[264,128]{1,0:T(8,128)S(1)}, f32[264,128]{1,0:T(8,128)S(1)}, u32[]{:S(2)}, u32[]{:S(2)}) collective-permute-start(f32[264,128]{1,0:T(8,128)S(1)} %get-tuple-element.24.part), channel_id=1, source_target_pairs={{0,12},{12,0},{4,8},{8,4},{1,13},{13,1},{5,9},{9,5},{2,14},{14,2},... | collective-permute-start | bytes 405512 | tf_op jit(solution)/shard_map/ppermute | solution.py:60
  29.5 0.4 shard_map.82.part
  29.9 0.1 collective-permute-start.1
  31.3 0.2 shard_map.81
  31.5 1.6 %collective-permute-done.2.more = f32[264,128]{1,0:T(8,128)S(1)} collective-permute-done((f32[264,128]{1,0:T(8,128)S(1)}, f32[264,128]{1,0:T(8,128)S(1)}, u32[]{:S(2)}, u32[]{:S(2)}) %collective-permute-start.2) | collective-permute-done | bytes 135200 | tf_op jit(solution)/shard_map/ppermute | solution.py:60
  33.2 0.7 %shard_map.83 = (f32[192,128]{1,0:T(8,128)S(1)}, f32[192,128]{1,0:T(8,128)S(1)}, f32[192,128]{1,0:T(8,128)S(1)}, f32[256,128]{1,0:T(8,128)S(1)}, f32[8,256]{1,0:T(8,128)S(1)}) custom-call(f32[1]{0:T(128)S(6)} %copy.10.log_scale, f32[1]{0:T(128)S(6)} %copy.11.bias, f32[8,256]{1,0:T(8,128)S(1)} %get-tuple-element.19.extra, ...), custom_call_target="tpu_custom_call" | custom-call | bytes 1000 | tf_op jit(solution)/shard_map/pallas_call | solution.py:329
  33.8 1.0 %collective-permute-start.3 = (f32[192,128]{1,0:T(8,128)S(1)}, f32[192,128]{1,0:T(8,128)S(1)}, u32[]{:S(2)}, u32[]{:S(2)}) collective-permute-start(f32[192,128]{1,0:T(8,128)S(1)} %get-tuple-element.29), channel_id=1, source_target_pairs={{0,16},{16,0},{1,17},{17,1},{2,18},{18,2},{3,19},{19,3},{4,20},{20... | collective-permute-start | bytes 294920 | tf_op jit(solution)/shard_map/ppermute | solution.py:56
  34.9 0.1 collective-permute-start.4
  35.0 0.4 collective-permute-start.5
  35.4 0.3 collective-permute-done.1.more
  35.7 0.9 %shard_map.84 = (f32[4,2,144,128]{3,2,1,0:T(8,128)S(1)}, f32[576,128]{1,0:T(8,128)S(1)}) custom-call(f32[1]{0:T(128)S(6)} %copy.11.bias, f32[576,256]{1,0:T(8,128)S(1)} %get-tuple-element.18.image, f32[8,256]{1,0:T(8,128)S(1)} %get-tuple-element.19.extra, bf16[576,768]{1,0:T(8,128)(2,1)S(1)} %get-tuple-element.21.image_left, ...), custom_call_target="tpu_custom_call" | custom-call | bytes 1000 | tf_op jit(solution)/shard_map/pallas_call | solution.py:329
  36.7 0.0 collective-permute-done.3.first
  36.7 0.0 collective-permute-done.4.second
  36.7 0.0 collective-permute-done.5.third
  36.7 0.3 shard_map.85
  37.0 17.8 %all_to_all.11 = f32[32,54,1,128]{3,2,1,0:T(1,128)S(1)} all-to-all(f32[32,54,1,128]{3,2,1,0:T(1,128)S(1)} %bitcast.14), channel_id=1, replica_groups={{0,1,2,3,4,5,6,7,32,33,34,35,36,37,38,39,64,65,66,67,68,69,70,71,96,97,..., dimensions={0} | all-to-all | bytes 1769472 | tf_op jit(solution)/shard_map/all_to_all | solution.py:44
  54.8 0.9 %shard_map.86 = (f32[72,256]{1,0:T(8,128)}, f32[72,256]{1,0:T(8,128)}) custom-call(f32[1728,128]{1,0:T(8,128)S(1)} %bitcast.13), custom_call_target="tpu_custom_call" | custom-call | bytes 1000 | tf_op jit(solution)/shard_map/pallas_call | solution.py:329
Async XLA Ops:
  22.6 3.1 %collective-permute-start = (f32[584,128]{1,0:T(8,128)S(1)}, f32[584,128]{1,0:T(8,128)S(1)}, u32[]{:S(2)}, u32[]{:S(2)}) collective-permute-start(f32[584,128]{1,0:T(8,128)S(1)} %shard_map.79.text), channel_id=1, source_target_pairs={{0,16},{16,0},{1,17},{17,1},{2,18},{18,2},{3,19},{19,3},{4,20},{20... | collective-permute-start | bytes 897032 | tf_op jit(solution)/shard_map/ppermute | solution.py:56
  26.1 7.1 %collective-permute-start.2 = (f32[264,128]{1,0:T(8,128)S(1)}, f32[264,128]{1,0:T(8,128)S(1)}, u32[]{:S(2)}, u32[]{:S(2)}) collective-permute-start(f32[264,128]{1,0:T(8,128)S(1)} %get-tuple-element.24.part), channel_id=1, source_target_pairs={{0,12},{12,0},{4,8},{8,4},{1,13},{13,1},{5,9},{9,5},{2,14},{14,2},... | collective-permute-start | bytes 405512 | tf_op jit(solution)/shard_map/ppermute | solution.py:60
  29.9 5.8 %collective-permute-start.1 = (f32[264,128]{1,0:T(8,128)S(1)}, f32[264,128]{1,0:T(8,128)S(1)}, u32[]{:S(2)}, u32[]{:S(2)}) collective-permute-start(f32[264,128]{1,0:T(8,128)S(1)} %shard_map.82.part), channel_id=1, source_target_pairs={{0,12},{12,0},{4,8},{8,4},{1,13},{13,1},{5,9},{9,5},{2,14},{14,2},... | collective-permute-start | bytes 405512 | tf_op jit(solution)/shard_map/ppermute | solution.py:60
  33.8 2.8 %collective-permute-start.3 = (f32[192,128]{1,0:T(8,128)S(1)}, f32[192,128]{1,0:T(8,128)S(1)}, u32[]{:S(2)}, u32[]{:S(2)}) collective-permute-start(f32[192,128]{1,0:T(8,128)S(1)} %get-tuple-element.29), channel_id=1, source_target_pairs={{0,16},{16,0},{1,17},{17,1},{2,18},{18,2},{3,19},{19,3},{4,20},{20... | collective-permute-start | bytes 294920 | tf_op jit(solution)/shard_map/ppermute | solution.py:56
  34.9 1.8 %collective-permute-start.4 = (f32[192,128]{1,0:T(8,128)S(1)}, f32[192,128]{1,0:T(8,128)S(1)}, u32[]{:S(2)}, u32[]{:S(2)}) collective-permute-start(f32[192,128]{1,0:T(8,128)S(1)} %get-tuple-element.30), channel_id=1, source_target_pairs={{0,16},{16,0},{1,17},{17,1},{2,18},{18,2},{3,19},{19,3},{4,20},{20... | collective-permute-start | bytes 294920 | tf_op jit(solution)/shard_map/ppermute | solution.py:56
  35.0 1.7 %collective-permute-start.5 = (f32[192,128]{1,0:T(8,128)S(1)}, f32[192,128]{1,0:T(8,128)S(1)}, u32[]{:S(2)}, u32[]{:S(2)}) collective-permute-start(f32[192,128]{1,0:T(8,128)S(1)} %get-tuple-element.31), channel_id=1, source_target_pairs={{0,16},{16,0},{1,17},{17,1},{2,18},{18,2},{3,19},{19,3},{4,20},{20... | collective-permute-start | bytes 294920 | tf_op jit(solution)/shard_map/ppermute | solution.py:56

commit v10 on v7

--- a/solution.py
+++ b/solution.py
@@ -11,6 +11,7 @@
 BF16 = jnp.bfloat16
 
 FEATS = 72
+CUT = 24
 ROWS = 256
 PEERS = 32
 WIDE = 64
@@ -104,16 +105,13 @@
 
 def pack_kernel(image, text, image_owner, text_owner, out, held, owners, sems):
     core = lax.axis_index("c")
+    moves = [(image_owner, owners.at[0]), (text_owner, owners.at[1])]
+    for k, whole in ((0, image), (1, text)):
+        for first in range(0, FEATS, CUT):
+            part = pl.ds(first, CUT)
+            moves.append((whole.at[part], held.at[k, part]))
     copies = [
-        pltpu.make_async_copy(src, dst, sems.at[i])
-        for i, (src, dst) in enumerate(
-            (
-                (image, held.at[0]),
-                (text, held.at[1]),
-                (image_owner, owners.at[0]),
-                (text_owner, owners.at[1]),
-            )
-        )
+        pltpu.make_async_copy(src, dst, sems.at[i]) for i, (src, dst) in enumerate(moves)
     ]
     for copy in copies:
         copy.start()
@@ -349,7 +347,7 @@
         scratch_shapes=[
             pltpu.VMEM((2, FEATS, ROWS), F32),
             pltpu.VMEM((2, 1, ROWS), jnp.int32),
-            pltpu.SemaphoreType.DMA((4,)),
+            pltpu.SemaphoreType.DMA((2 + 2 * FEATS // CUT,)),
         ],
     )
     held = exchange(packed)

time: 56.4 us -> 56.4 us (level)
  no operation moved by 1% of the time
where the time goes in v10:
time: 56.4 us; the launch traced here: 56.2 us
  blocking collectives  38.8 us (69%)
  starting transfers between devices  7 us (12%)
  Pallas kernels  5.55 us (10%)
  waiting for transfers between devices  2.8 us (5%)
  between operations  2.01 us (4%)
    all_to_all x2, blocking collectives, exchange(): lax.all_to_all(pieces.reshape(PEERS, rows, 1, 128), AXES, 0, 0, axis_inde...  38.8 us
    pallas_call x9, Pallas kernels, call(): pl.pallas_call(kernel, out_shape=[jax.ShapeDtypeStruct(s, t) for s, t in...  5.55 us
    ppermute x2, starting transfers between devices, other_half(): return lax.ppermute(x, 'z', [(0, 3), (3, 0), (1, 2), (2, 1)])  3.54 us
    ppermute x4, starting transfers between devices, other_core(): return lax.ppermute(x, 'c', [(0, 1), (1, 0)])  3.46 us
    ppermute x2, waiting for transfers between devices, other_half(): return lax.ppermute(x, 'z', [(0, 3), (3, 0), (1, 2), (2, 1)])  2.24 us
  transfers between devices with their start and end apart: 6, of which 3 were waited for; matrix products, arithmetic and copies ran while one was open for 0% of the time, Pallas kernels for 4%

profile of v10, /device:TPU:1, one launch (start us, length us, event | category | flops | bytes accessed | tf_op | source)
XLA Modules:
  0.0 56.2 jit_solution(7048707619636753425)
XLA Ops:
  0.6 1.1 %shard_map.77 = f32[1760,128]{1,0:T(8,128)S(1)} custom-call(f32[72,256]{1,0:T(8,128)} %bitcast.15, f32[72,256]{1,0:T(8,128)} %bitcast.16, s32[1,256]{1,0:T(1,128)} %bitcast.17, s32[1,256]{1,0:T(1,128)} %bitcast.18), custom_call_target="tpu_custom_call" | custom-call | bytes 1000 | tf_op jit(solution)/shard_map/pallas_call | solution.py:324
  1.8 20.4 %all_to_all.10 = f32[32,55,1,128]{3,2,1,0:T(1,128)S(1)} all-to-all(f32[32,55,1,128]{3,2,1,0:T(1,128)S(1)} %bitcast.12), channel_id=1, replica_groups={{0,1,2,3,4,5,6,7,32,33,34,35,36,37,38,39,64,65,66,67,68,69,70,71,96,97,..., dimensions={0} | all-to-all | bytes 1802240 | tf_op jit(solution)/shard_map/all_to_all | solution.py:45
  22.2 0.3 shard_map.78.text
  22.5 1.8 %collective-permute-start = (f32[584,128]{1,0:T(8,128)S(1)}, f32[584,128]{1,0:T(8,128)S(1)}, u32[]{:S(2)}, u32[]{:S(2)}) collective-permute-start(f32[584,128]{1,0:T(8,128)S(1)} %shard_map.78.text), channel_id=1, source_target_pairs={{0,16},{16,0},{1,17},{17,1},{2,18},{18,2},{3,19},{19,3},{4,20},{20... | collective-permute-start | bytes 897032 | tf_op jit(solution)/shard_map/ppermute | solution.py:57
  24.4 0.7 %shard_map.79 = (f32[576,256]{1,0:T(8,128)S(1)}, f32[8,256]{1,0:T(8,128)S(1)}, f32[264,128]{1,0:T(8,128)S(1)}) custom-call(f32[1760,128]{1,0:T(8,128)S(1)} %bitcast.11, f32[584,128]{1,0:T(8,128)S(1)} %shard_map.78.text), custom_call_target="tpu_custom_call" | custom-call | bytes 1000 | tf_op jit(solution)/shard_map/pallas_call | solution.py:324
  25.0 0.5 collective-permute-done.text_far
  25.6 0.5 shard_map.80
  26.0 3.4 %collective-permute-start.2 = (f32[264,128]{1,0:T(8,128)S(1)}, f32[264,128]{1,0:T(8,128)S(1)}, u32[]{:S(2)}, u32[]{:S(2)}) collective-permute-start(f32[264,128]{1,0:T(8,128)S(1)} %get-tuple-element.26.part), channel_id=1, source_target_pairs={{0,12},{12,0},{4,8},{8,4},{1,13},{13,1},{5,9},{9,5},{2,14},{14,2},... | collective-permute-start | bytes 405512 | tf_op jit(solution)/shard_map/ppermute | solution.py:61
  29.5 0.1 collective-permute-start.1
  30.9 0.2 shard_map.81
  31.1 2.1 %collective-permute-done.2.more = f32[264,128]{1,0:T(8,128)S(1)} collective-permute-done((f32[264,128]{1,0:T(8,128)S(1)}, f32[264,128]{1,0:T(8,128)S(1)}, u32[]{:S(2)}, u32[]{:S(2)}) %collective-permute-start.2) | collective-permute-done | bytes 135200 | tf_op jit(solution)/shard_map/ppermute | solution.py:61
  33.1 0.7 %shard_map.82 = (f32[192,128]{1,0:T(8,128)S(1)}, f32[192,128]{1,0:T(8,128)S(1)}, f32[192,128]{1,0:T(8,128)S(1)}, f32[256,128]{1,0:T(8,128)S(1)}, f32[8,256]{1,0:T(8,128)S(1)}) custom-call(f32[1]{0:T(128)S(6)} %copy.10.log_scale, f32[1]{0:T(128)S(6)} %copy.11.bias, f32[8,256]{1,0:T(8,128)S(1)} %get-tuple-element.20.extra, ...), custom_call_target="tpu_custom_call" | custom-call | bytes 1000 | tf_op jit(solution)/shard_map/pallas_call | solution.py:324
  33.8 1.1 %collective-permute-start.3 = (f32[192,128]{1,0:T(8,128)S(1)}, f32[192,128]{1,0:T(8,128)S(1)}, u32[]{:S(2)}, u32[]{:S(2)}) collective-permute-start(f32[192,128]{1,0:T(8,128)S(1)} %get-tuple-element.31), channel_id=1, source_target_pairs={{0,16},{16,0},{1,17},{17,1},{2,18},{18,2},{3,19},{19,3},{4,20},{20... | collective-permute-start | bytes 294920 | tf_op jit(solution)/shard_map/ppermute | solution.py:57
  34.9 0.1 collective-permute-start.4
  35.0 0.4 collective-permute-start.5
  35.5 0.2 collective-permute-done.1.more
  35.6 0.9 %shard_map.83 = (f32[4,2,144,128]{3,2,1,0:T(8,128)S(1)}, f32[576,128]{1,0:T(8,128)S(1)}) custom-call(f32[1]{0:T(128)S(6)} %copy.11.bias, f32[576,256]{1,0:T(8,128)S(1)} %get-tuple-element.19.image, f32[8,256]{1,0:T(8,128)S(1)} %get-tuple-element.20.extra, bf16[576,768]{1,0:T(8,128)(2,1)S(1)} %get-tuple-element.22.image_left, ...), custom_call_target="tpu_custom_call" | custom-call | bytes 1000 | tf_op jit(solution)/shard_map/pallas_call | solution.py:324
  36.5 0.0 collective-permute-done.3.first
  36.6 0.0 collective-permute-done.4.second
  36.6 0.0 collective-permute-done.5.third
  36.6 0.3 shard_map.84
  36.9 18.4 %all_to_all.11 = f32[32,54,1,128]{3,2,1,0:T(1,128)S(1)} all-to-all(f32[32,54,1,128]{3,2,1,0:T(1,128)S(1)} %bitcast.14), channel_id=1, replica_groups={{0,1,2,3,4,5,6,7,32,33,34,35,36,37,38,39,64,65,66,67,68,69,70,71,96,97,..., dimensions={0} | all-to-all | bytes 1769472 | tf_op jit(solution)/shard_map/all_to_all | solution.py:45
  55.3 0.9 %shard_map.85 = (f32[72,256]{1,0:T(8,128)}, f32[72,256]{1,0:T(8,128)}) custom-call(f32[1728,128]{1,0:T(8,128)S(1)} %bitcast.13), custom_call_target="tpu_custom_call" | custom-call | bytes 1000 | tf_op jit(solution)/shard_map/pallas_call | solution.py:324
Async XLA Ops:
  22.5 3.1 %collective-permute-start = (f32[584,128]{1,0:T(8,128)S(1)}, f32[584,128]{1,0:T(8,128)S(1)}, u32[]{:S(2)}, u32[]{:S(2)}) collective-permute-start(f32[584,128]{1,0:T(8,128)S(1)} %shard_map.78.text), channel_id=1, source_target_pairs={{0,16},{16,0},{1,17},{17,1},{2,18},{18,2},{3,19},{19,3},{4,20},{20... | collective-permute-start | bytes 897032 | tf_op jit(solution)/shard_map/ppermute | solution.py:57
  26.0 7.1 %collective-permute-start.2 = (f32[264,128]{1,0:T(8,128)S(1)}, f32[264,128]{1,0:T(8,128)S(1)}, u32[]{:S(2)}, u32[]{:S(2)}) collective-permute-start(f32[264,128]{1,0:T(8,128)S(1)} %get-tuple-element.26.part), channel_id=1, source_target_pairs={{0,12},{12,0},{4,8},{8,4},{1,13},{13,1},{5,9},{9,5},{2,14},{14,2},... | collective-permute-start | bytes 405512 | tf_op jit(solution)/shard_map/ppermute | solution.py:61
  29.5 6.1 %collective-permute-start.1 = (f32[264,128]{1,0:T(8,128)S(1)}, f32[264,128]{1,0:T(8,128)S(1)}, u32[]{:S(2)}, u32[]{:S(2)}) collective-permute-start(f32[264,128]{1,0:T(8,128)S(1)} %get-tuple-element.24.near.part), channel_id=1, source_target_pairs={{0,12},{12,0},{4,8},{8,4},{1,13},{13,1},{5,9},{9,5},{2,14},{14,2},... | collective-permute-start | bytes 405512 | tf_op jit(solution)/shard_map/ppermute | solution.py:61
  33.8 2.7 %collective-permute-start.3 = (f32[192,128]{1,0:T(8,128)S(1)}, f32[192,128]{1,0:T(8,128)S(1)}, u32[]{:S(2)}, u32[]{:S(2)}) collective-permute-start(f32[192,128]{1,0:T(8,128)S(1)} %get-tuple-element.31), channel_id=1, source_target_pairs={{0,16},{16,0},{1,17},{17,1},{2,18},{18,2},{3,19},{19,3},{4,20},{20... | collective-permute-start | bytes 294920 | tf_op jit(solution)/shard_map/ppermute | solution.py:57
  34.9 1.6 %collective-permute-start.4 = (f32[192,128]{1,0:T(8,128)S(1)}, f32[192,128]{1,0:T(8,128)S(1)}, u32[]{:S(2)}, u32[]{:S(2)}) collective-permute-start(f32[192,128]{1,0:T(8,128)S(1)} %get-tuple-element.32), channel_id=1, source_target_pairs={{0,16},{16,0},{1,17},{17,1},{2,18},{18,2},{3,19},{19,3},{4,20},{20... | collective-permute-start | bytes 294920 | tf_op jit(solution)/shard_map/ppermute | solution.py:57
  35.0 1.5 %collective-permute-start.5 = (f32[192,128]{1,0:T(8,128)S(1)}, f32[192,128]{1,0:T(8,128)S(1)}, u32[]{:S(2)}, u32[]{:S(2)}) collective-permute-start(f32[192,128]{1,0:T(8,128)S(1)} %get-tuple-element.33), channel_id=1, source_target_pairs={{0,16},{16,0},{1,17},{17,1},{2,18},{18,2},{3,19},{19,3},{4,20},{20... | collective-permute-start | bytes 294920 | tf_op jit(solution)/shard_map/ppermute | solution.py:57

commit v11 on v10

--- a/solution.py
+++ b/solution.py
@@ -166,7 +166,7 @@
     out[DEPTH:] = jnp.concatenate([squares(text), owner, jnp.zeros((6, 128), F32)], axis=0)
 
 
-def image_kernel(pieces, text, image_out, extra, part):
+def image_kernel(pieces, image_out, extra):
     core = lax.axis_index("c")
     blocks = [pieces[block_of(x, core, IN_ROWS)] for x in range(4)]
     strips = [[strip(b, IN_ROWS, e * TRIO) for b in blocks] for e in range(2)]
@@ -182,8 +182,6 @@
     image_out[...] = image
     owner = jnp.concatenate([b[54:55, :WIDE] for b in blocks], axis=1)
     extra[...] = jnp.concatenate([owner, squares(image), jnp.zeros((6, ROWS), F32)], axis=0)
-    part[:ROWS] = product(image, text[:DEPTH], 0)
-    part[ROWS:] = text[DEPTH:]
 
 
 def far_kernel(image, extra, text_far, text_out, part):
@@ -202,6 +200,11 @@
     )
 
 
+def near_kernel(image, text, part):
+    part[:ROWS] = product(image[...], text[:DEPTH], 0)
+    part[ROWS:] = text[DEPTH:]
+
+
 def left_kernel(image, text, text_far, image_left, text_left, far_left):
     image_left[...] = joined(image[...], 1, True)
     text_left[...] = joined(text[:DEPTH], 1, True)
@@ -223,7 +226,7 @@
 
 
 def far_grad_kernel(
-    log_scale, bias, extra, image_left, text_far, part, more, near, sent0, sent1, sent2, mixed, factors
+    log_scale, bias, extra, image_left, text_far, part, more, sent0, sent1, sent2, mixed, factors
 ):
     scale = jnp.exp(jnp.full((1, 1), log_scale[0], F32))
     sums = part[ROWS + 1 : ROWS + 3] + more[ROWS + 1 : ROWS + 3]
@@ -353,9 +356,8 @@
     held = exchange(packed)
     (text,) = call(text_kernel, [(DEPTH + 8, 128)], (held,))
     text_received = other_core(text)
-    image, extra, near = call(
-        image_kernel, [(DEPTH, ROWS), (8, ROWS), (ROWS + 8, 128)], (held, text)
-    )
+    image, extra = call(image_kernel, [(DEPTH, ROWS), (8, ROWS)], (held,))
+    (near,) = call(near_kernel, [(ROWS + 8, 128)], (image, text))
     text_far, far = call(
         far_kernel, [(DEPTH + 8, 128), (ROWS + 8, 128)], (image, extra, text_received)
     )
@@ -370,7 +372,7 @@
     *sent, mixed, factors = call(
         far_grad_kernel,
         [(SENT, 128)] * 3 + [(ROWS, 128), (8, ROWS)],
-        (log_scale, bias, extra, image_left, text_far, far, far_more, near),
+        (log_scale, bias, extra, image_left, text_far, far, far_more),
         scalars=2,
     )
     received = [other_core(x) for x in sent]

time: 56.4 us -> 56.4 us (level)
  blocking collectives: 38.8 us -> 38.2 us
    all_to_all x2, blocking collectives: 38.8 us -> 38.2 us  [exchange(): lax.all_to_all(pieces.reshape(PEERS, rows, 1, 128), AXES, 0, 0, axis_inde...]
    pallas_call x9 -> x10, Pallas kernels: 5.55 us -> 5.55 us  [call(): pl.pallas_call(kernel, out_shape=[jax.ShapeDtypeStruct(s, t) for s, t in...]
where the time goes in v11:
time: 56.4 us; the launch traced here: 55.7 us
  blocking collectives  38.2 us (68%)
  starting transfers between devices  6.91 us (12%)
  Pallas kernels  5.55 us (10%)
  waiting for transfers between devices  2.96 us (5%)
  between operations  2.01 us (4%)
    all_to_all x2, blocking collectives, exchange(): lax.all_to_all(pieces.reshape(PEERS, rows, 1, 128), AXES, 0, 0, axis_inde...  38.2 us
    pallas_call x10, Pallas kernels, call(): pl.pallas_call(kernel, out_shape=[jax.ShapeDtypeStruct(s, t) for s, t in...  5.55 us
    ppermute x2, starting transfers between devices, other_half(): return lax.ppermute(x, 'z', [(0, 3), (3, 0), (1, 2), (2, 1)])  3.54 us
    ppermute x4, starting transfers between devices, other_core(): return lax.ppermute(x, 'c', [(0, 1), (1, 0)])  3.37 us
    ppermute x2, waiting for transfers between devices, other_half(): return lax.ppermute(x, 'z', [(0, 3), (3, 0), (1, 2), (2, 1)])  1.97 us
  transfers between devices with their start and end apart: 6, of which 3 were waited for; matrix products, arithmetic and copies ran while one was open for 0% of the time, Pallas kernels for 4%

profile of v11, /device:TPU:1, one launch (start us, length us, event | category | flops | bytes accessed | tf_op | source)
XLA Modules:
  0.0 55.7 jit_solution(2601375856087645542)
XLA Ops:
  0.6 1.1 %shard_map.77 = f32[1760,128]{1,0:T(8,128)S(1)} custom-call(f32[72,256]{1,0:T(8,128)} %bitcast.15, f32[72,256]{1,0:T(8,128)} %bitcast.16, s32[1,256]{1,0:T(1,128)} %bitcast.17, s32[1,256]{1,0:T(1,128)} %bitcast.18), custom_call_target="tpu_custom_call" | custom-call | bytes 1000 | tf_op jit(solution)/shard_map/pallas_call | solution.py:327
  1.8 20.4 %all_to_all.10 = f32[32,55,1,128]{3,2,1,0:T(1,128)S(1)} all-to-all(f32[32,55,1,128]{3,2,1,0:T(1,128)S(1)} %bitcast.12), channel_id=1, replica_groups={{0,1,2,3,4,5,6,7,32,33,34,35,36,37,38,39,64,65,66,67,68,69,70,71,96,97,..., dimensions={0} | all-to-all | bytes 1802240 | tf_op jit(solution)/shard_map/all_to_all | solution.py:45
  22.2 0.3 shard_map.79.text
  22.5 1.8 %collective-permute-start = (f32[584,128]{1,0:T(8,128)S(1)}, f32[584,128]{1,0:T(8,128)S(1)}, u32[]{:S(2)}, u32[]{:S(2)}) collective-permute-start(f32[584,128]{1,0:T(8,128)S(1)} %shard_map.79.text), channel_id=1, source_target_pairs={{0,16},{16,0},{1,17},{17,1},{2,18},{18,2},{3,19},{19,3},{4,20},{20... | collective-permute-start | bytes 897032 | tf_op jit(solution)/shard_map/ppermute | solution.py:57
  24.4 0.2 shard_map.78
  24.6 1.0 %collective-permute-done.text_far = f32[584,128]{1,0:T(8,128)S(1)} collective-permute-done((f32[584,128]{1,0:T(8,128)S(1)}, f32[584,128]{1,0:T(8,128)S(1)}, u32[]{:S(2)}, u32[]{:S(2)}) %collective-permute-start) | collective-permute-done | bytes 299040 | tf_op jit(solution)/shard_map/ppermute | solution.py:57
  25.6 0.4 shard_map.80
  26.0 3.4 %collective-permute-start.2 = (f32[264,128]{1,0:T(8,128)S(1)}, f32[264,128]{1,0:T(8,128)S(1)}, u32[]{:S(2)}, u32[]{:S(2)}) collective-permute-start(f32[264,128]{1,0:T(8,128)S(1)} %get-tuple-element.24.part), channel_id=1, source_target_pairs={{0,12},{12,0},{4,8},{8,4},{1,13},{13,1},{5,9},{9,5},{2,14},{14,2},... | collective-permute-start | bytes 405512 | tf_op jit(solution)/shard_map/ppermute | solution.py:61
  29.5 0.4 shard_map.82.part
  29.9 0.1 collective-permute-start.1
  31.3 0.2 shard_map.81
  31.5 1.6 %collective-permute-done.2.more = f32[264,128]{1,0:T(8,128)S(1)} collective-permute-done((f32[264,128]{1,0:T(8,128)S(1)}, f32[264,128]{1,0:T(8,128)S(1)}, u32[]{:S(2)}, u32[]{:S(2)}) %collective-permute-start.2) | collective-permute-done | bytes 135200 | tf_op jit(solution)/shard_map/ppermute | solution.py:61
  33.1 0.7 %shard_map.83 = (f32[192,128]{1,0:T(8,128)S(1)}, f32[192,128]{1,0:T(8,128)S(1)}, f32[192,128]{1,0:T(8,128)S(1)}, f32[256,128]{1,0:T(8,128)S(1)}, f32[8,256]{1,0:T(8,128)S(1)}) custom-call(f32[1]{0:T(128)S(6)} %copy.10.log_scale, f32[1]{0:T(128)S(6)} %copy.11.bias, f32[8,256]{1,0:T(8,128)S(1)} %get-tuple-element.19.extra, ...), custom_call_target="tpu_custom_call" | custom-call | bytes 1000 | tf_op jit(solution)/shard_map/pallas_call | solution.py:327
  33.8 1.0 %collective-permute-start.3 = (f32[192,128]{1,0:T(8,128)S(1)}, f32[192,128]{1,0:T(8,128)S(1)}, u32[]{:S(2)}, u32[]{:S(2)}) collective-permute-start(f32[192,128]{1,0:T(8,128)S(1)} %get-tuple-element.29), channel_id=1, source_target_pairs={{0,16},{16,0},{1,17},{17,1},{2,18},{18,2},{3,19},{19,3},{4,20},{20... | collective-permute-start | bytes 294920 | tf_op jit(solution)/shard_map/ppermute | solution.py:57
  34.8 0.1 collective-permute-start.4
  34.9 0.4 collective-permute-start.5
  35.3 0.3 collective-permute-done.1.more
  35.7 0.9 %shard_map.84 = (f32[4,2,144,128]{3,2,1,0:T(8,128)S(1)}, f32[576,128]{1,0:T(8,128)S(1)}) custom-call(f32[1]{0:T(128)S(6)} %copy.11.bias, f32[576,256]{1,0:T(8,128)S(1)} %get-tuple-element.18.image, f32[8,256]{1,0:T(8,128)S(1)} %get-tuple-element.19.extra, bf16[576,768]{1,0:T(8,128)(2,1)S(1)} %get-tuple-element.21.image_left, ...), custom_call_target="tpu_custom_call" | custom-call | bytes 1000 | tf_op jit(solution)/shard_map/pallas_call | solution.py:327
  36.6 0.0 collective-permute-done.3.first
  36.6 0.0 collective-permute-done.4.second
  36.6 0.0 collective-permute-done.5.third
  36.7 0.3 shard_map.85
  37.0 17.8 %all_to_all.11 = f32[32,54,1,128]{3,2,1,0:T(1,128)S(1)} all-to-all(f32[32,54,1,128]{3,2,1,0:T(1,128)S(1)} %bitcast.14), channel_id=1, replica_groups={{0,1,2,3,4,5,6,7,32,33,34,35,36,37,38,39,64,65,66,67,68,69,70,71,96,97,..., dimensions={0} | all-to-all | bytes 1769472 | tf_op jit(solution)/shard_map/all_to_all | solution.py:45
  54.8 0.9 %shard_map.86 = (f32[72,256]{1,0:T(8,128)}, f32[72,256]{1,0:T(8,128)}) custom-call(f32[1728,128]{1,0:T(8,128)S(1)} %bitcast.13), custom_call_target="tpu_custom_call" | custom-call | bytes 1000 | tf_op jit(solution)/shard_map/pallas_call | solution.py:327
Async XLA Ops:
  22.5 3.1 %collective-permute-start = (f32[584,128]{1,0:T(8,128)S(1)}, f32[584,128]{1,0:T(8,128)S(1)}, u32[]{:S(2)}, u32[]{:S(2)}) collective-permute-start(f32[584,128]{1,0:T(8,128)S(1)} %shard_map.79.text), channel_id=1, source_target_pairs={{0,16},{16,0},{1,17},{17,1},{2,18},{18,2},{3,19},{19,3},{4,20},{20... | collective-permute-start | bytes 897032 | tf_op jit(solution)/shard_map/ppermute | solution.py:57
  26.0 7.1 %collective-permute-start.2 = (f32[264,128]{1,0:T(8,128)S(1)}, f32[264,128]{1,0:T(8,128)S(1)}, u32[]{:S(2)}, u32[]{:S(2)}) collective-permute-start(f32[264,128]{1,0:T(8,128)S(1)} %get-tuple-element.24.part), channel_id=1, source_target_pairs={{0,12},{12,0},{4,8},{8,4},{1,13},{13,1},{5,9},{9,5},{2,14},{14,2},... | collective-permute-start | bytes 405512 | tf_op jit(solution)/shard_map/ppermute | solution.py:61
  29.9 5.8 %collective-permute-start.1 = (f32[264,128]{1,0:T(8,128)S(1)}, f32[264,128]{1,0:T(8,128)S(1)}, u32[]{:S(2)}, u32[]{:S(2)}) collective-permute-start(f32[264,128]{1,0:T(8,128)S(1)} %shard_map.82.part), channel_id=1, source_target_pairs={{0,12},{12,0},{4,8},{8,4},{1,13},{13,1},{5,9},{9,5},{2,14},{14,2},... | collective-permute-start | bytes 405512 | tf_op jit(solution)/shard_map/ppermute | solution.py:61
  33.8 2.8 %collective-permute-start.3 = (f32[192,128]{1,0:T(8,128)S(1)}, f32[192,128]{1,0:T(8,128)S(1)}, u32[]{:S(2)}, u32[]{:S(2)}) collective-permute-start(f32[192,128]{1,0:T(8,128)S(1)} %get-tuple-element.29), channel_id=1, source_target_pairs={{0,16},{16,0},{1,17},{17,1},{2,18},{18,2},{3,19},{19,3},{4,20},{20... | collective-permute-start | bytes 294920 | tf_op jit(solution)/shard_map/ppermute | solution.py:57
  34.8 1.8 %collective-permute-start.4 = (f32[192,128]{1,0:T(8,128)S(1)}, f32[192,128]{1,0:T(8,128)S(1)}, u32[]{:S(2)}, u32[]{:S(2)}) collective-permute-start(f32[192,128]{1,0:T(8,128)S(1)} %get-tuple-element.30), channel_id=1, source_target_pairs={{0,16},{16,0},{1,17},{17,1},{2,18},{18,2},{3,19},{19,3},{4,20},{20... | collective-permute-start | bytes 294920 | tf_op jit(solution)/shard_map/ppermute | solution.py:57
  34.9 1.7 %collective-permute-start.5 = (f32[192,128]{1,0:T(8,128)S(1)}, f32[192,128]{1,0:T(8,128)S(1)}, u32[]{:S(2)}, u32[]{:S(2)}) collective-permute-start(f32[192,128]{1,0:T(8,128)S(1)} %get-tuple-element.31), channel_id=1, source_target_pairs={{0,16},{16,0},{1,17},{17,1},{2,18},{18,2},{3,19},{19,3},{4,20},{20... | collective-permute-start | bytes 294920 | tf_op jit(solution)/shard_map/ppermute | solution.py:57
